TPU v7x, 32 devices: a whole 2x2x4 slice. The times are simulated.
32 devices in a mesh: fsdp: 4 (over y, x), blk: 8 (over z, core).
Axes of the slice: x: 2, y: 2, z: 4, core: 2. Of those that a mesh axis runs over, the one named last changes fastest.
Arguments:
- tokens: bfloat16 [12288, 1152], P(('fsdp', 'blk')), may hold values from -6 to 6
- timesteps: int32 [4, 8], P('fsdp'), may hold values from 0 to 999
- segment_ids: int32 [4, 3072], P('fsdp'), may hold values from 0 to 7, as said below
- head_mask: int32 [4, 8, 16], P('fsdp'), may hold values 0 or 1
- chan_mask: int32 [4, 8, 4608], P('fsdp'), may hold values 0 or 1
- token_mask: int32 [12288], P(('fsdp', 'blk')), may hold values 0 or 1
- w_temb: bfloat16 [256, 1152], P('fsdp'), may hold values from -0.375 to 0.375
- w_ada: bfloat16 [1152, 6912], P('fsdp'), may hold values from -0.1875 to 0.1875
- w_qkv: bfloat16 [1152, 3456], P('fsdp'), may hold values from -0.25 to 0.25
- w_out: bfloat16 [1152, 1152], P('fsdp'), may hold values from -1 to 1
- w_fc1: bfloat16 [1152, 4608], P('fsdp'), may hold values from -0.1875 to 0.1875
- w_fc2: bfloat16 [4608, 1152], P('fsdp'), may hold values from -0.1875 to 0.1875
- cotangent: bfloat16 [12288, 1152], P(('fsdp', 'blk')), may hold values from -6 to 6
Outputs:
- result: bfloat16 [12288, 1152], P(('fsdp', 'blk'))
- grad_tokens: bfloat16 [12288, 1152], P(('fsdp', 'blk'))
- grad_temb: float32 [256, 1152], P('fsdp')
- grad_ada: float32 [1152, 6912], P('fsdp')
- grad_qkv: float32 [1152, 3456], P('fsdp')
- grad_out: float32 [1152, 1152], P('fsdp')
- grad_fc1: float32 [1152, 4608], P('fsdp')
- grad_fc2: float32 [4608, 1152], P('fsdp')
Inputs may be any that keep to these rules, and one draw needn't show every extreme that they name: `segment_ids`: in each stream slot 0 holds 1024 tokens, every other slot below 7 holds 1024, 256 or no tokens, and slot 7 holds the remaining padding tokens, at least 128 of them; each slot's tokens are spread over the devices of blk as evenly as possible, their counts on two devices differing by at most one.
All inputs are finite; a program needn't handle non-finite values. No bound on the sum of `head_mask` or of `chan_mask` or of `token_mask` on one device may be relied on, other than what follows from the above.
Results may differ from a plain program's by a relative error of at most 0.022.
Values may be sent and summed in bfloat16 or wider, within the bound.
A program may use at most 256 MiB of HBM per device.

v0:
```python
import math

import jax
import jax.numpy as jnp
from jax import lax
from jax.sharding import PartitionSpec as P

HIGH = lax.Precision.HIGHEST
NEG = -1e30


def from_behind(array, axis, by):
    devices = lax.axis_size(axis)
    return lax.ppermute(array, axis, [(i, (i + by) % devices) for i in range(devices)])


def frequencies(steps, entries):
    half = entries // 2
    ladder = jnp.exp(-math.log(10000.0) * lax.iota(jnp.float32, half) / half)
    angles = steps.astype(jnp.float32)[:, None] * ladder[None, :]
    return jnp.concatenate([jnp.cos(angles), jnp.sin(angles)], axis=1)


def silu_fn(values):
    return values / (1.0 + jnp.exp(-values))


def gelu_tanh(values):
    return (
        0.5
        * values
        * (1.0 + jnp.tanh(0.7978845608028654 * (values + 0.044715 * values * values * values)))
    )


def norm_mod(values, shift_by, scale_by):
    center = values - jnp.mean(values, axis=-1, keepdims=True)
    spread = jnp.mean(center * center, axis=-1, keepdims=True)
    return center * lax.rsqrt(spread + 1e-06) * (1.0 + scale_by) + shift_by


def dot_back(left, right):
    return lax.dot_general(
        left, right, (((1,), (1,)), ((), ())), preferred_element_type=jnp.float32
    )


def grad_term(left, right, factor):
    return (
        lax.dot_general(
            left,
            right,
            (((0,), (0,)), ((), ())),
            preferred_element_type=jnp.float32,
            precision=HIGH,
        )
        * factor
    )


def reduce_weight(left, right, factor):
    return lax.psum_scatter(
        grad_term(left, right, factor).astype(jnp.bfloat16), "fsdp", scatter_dimension=0, tiled=True
    ).astype(jnp.float32)


def on_device(
    tokens,
    timesteps,
    segment_ids,
    head_mask,
    chan_mask,
    token_mask,
    w_temb,
    w_ada,
    w_qkv,
    w_out,
    w_fc1,
    w_fc2,
    cotangent,
):
    tok_rows, model_width = tokens.shape
    head_count = head_mask.shape[2]
    head_size = model_width // head_count
    item_count = head_mask.shape[1]
    span_index = lax.axis_index("blk")
    cycle_size = lax.axis_size("blk")
    score_scale = 1.0 / math.sqrt(head_size)
    segment_row = segment_ids[0]
    gathered = (
        lax.all_gather(w_temb, "fsdp", axis=0, tiled=True),
        lax.all_gather(w_ada, "fsdp", axis=0, tiled=True),
        lax.all_gather(w_qkv, "fsdp", axis=0, tiled=True),
        lax.all_gather(w_out, "fsdp", axis=0, tiled=True),
        lax.all_gather(w_fc1, "fsdp", axis=0, tiled=True),
        lax.all_gather(w_fc2, "fsdp", axis=0, tiled=True),
    )
    full_temb, full_ada, full_qkv, full_out, full_fc1, full_fc2 = gathered
    own_items = lax.dynamic_slice_in_dim(segment_row, span_index * tok_rows, tok_rows)
    picker = (own_items[:, None] == lax.iota(jnp.int32, item_count)[None, :]).astype(jnp.float32)
    spectrum = frequencies(timesteps[0], full_temb.shape[0]).astype(jnp.bfloat16)
    condition = jnp.dot(spectrum, full_temb, preferred_element_type=jnp.float32)
    lifted, silu_pull = jax.vjp(silu_fn, condition)
    lifted_low = lifted.astype(jnp.bfloat16)
    modulation = jnp.dot(lifted_low, full_ada, preferred_element_type=jnp.float32)
    per_token = jnp.dot(picker, modulation, precision=HIGH)
    shift_one, scale_one, gate_one, shift_two, scale_two, gate_two = jnp.split(per_token, 6, axis=1)
    inputs = tokens.astype(jnp.float32)
    normed, norm_one_pull = jax.vjp(norm_mod, inputs, shift_one, scale_one)
    normed_low = normed.astype(jnp.bfloat16)
    packed = jnp.dot(normed_low, full_qkv, preferred_element_type=jnp.float32).astype(jnp.bfloat16)
    queries, keys, values = jnp.split(packed, 3, axis=1)
    query_heads = queries.reshape(tok_rows, head_count, head_size)
    start_state = (
        jnp.full((head_count, tok_rows), NEG, jnp.float32),
        jnp.zeros((head_count, tok_rows), jnp.float32),
        jnp.zeros((head_count, tok_rows, head_size), jnp.float32),
    )
    carry = start_state
    key_piece = lax.all_gather(keys, "blk", axis=0, tiled=True)
    value_piece = lax.all_gather(values, "blk", axis=0, tiled=True)
    count = key_piece.shape[0] // tok_rows
    key_blocks = key_piece.reshape(count, tok_rows, head_count, head_size)
    value_blocks = value_piece.reshape(count, tok_rows, head_count, head_size)
    starts = tok_rows * lax.iota(jnp.int32, count)

    def one_block(state, block):
        key_heads, value_heads, block_start = block
        running_max, running_sum, running_acc = state
        key_items = lax.dynamic_slice_in_dim(segment_row, block_start, tok_rows)
        same = own_items[:, None] == key_items[None, :]
        scores = (
            jnp.einsum("qhd,khd->hqk", query_heads, key_heads, preferred_element_type=jnp.float32)
            * score_scale
        )
        block_max = jnp.max(jnp.where(same[None], scores, NEG), axis=2)
        new_max = jnp.maximum(running_max, block_max)
        probs = jnp.where(same[None], jnp.exp(scores - new_max[:, :, None]), 0.0)
        decay = jnp.exp(running_max - new_max)
        new_sum = running_sum * decay + jnp.sum(probs, axis=2)
        new_acc = running_acc * decay[:, :, None] + jnp.einsum(
            "hqk,khd->hqd",
            probs.astype(jnp.bfloat16),
            value_heads,
            preferred_element_type=jnp.float32,
        )
        return ((new_max, new_sum, new_acc), None)

    carry, _ = lax.scan(one_block, carry, (key_blocks, value_blocks, starts))
    fold_max, fold_sum, fold_acc = carry
    log_total = fold_max + jnp.log(fold_sum)
    attended_rows = jnp.transpose(fold_acc / fold_sum[:, :, None], (1, 0, 2))
    head_keep = jnp.dot(picker, head_mask[0].astype(jnp.float32), precision=HIGH)
    masked_low = (
        (attended_rows * head_keep[:, :, None]).reshape(tok_rows, model_width).astype(jnp.bfloat16)
    )
    attn_branch = jnp.dot(masked_low, full_out, preferred_element_type=jnp.float32)
    middle = inputs + gate_one * attn_branch
    normed_two, norm_two_pull = jax.vjp(norm_mod, middle, shift_two, scale_two)
    normed_two_low = normed_two.astype(jnp.bfloat16)
    hidden_pre = jnp.dot(normed_two_low, full_fc1, preferred_element_type=jnp.float32)
    activated, gelu_pull = jax.vjp(gelu_tanh, hidden_pre)
    channel_keep = (
        jnp.dot(picker, chan_mask[0].astype(jnp.float32), precision=HIGH)
        * token_mask.astype(jnp.float32)[:, None]
    )
    hidden_low = (activated * channel_keep).astype(jnp.bfloat16)
    mlp_branch = jnp.dot(hidden_low, full_fc2, preferred_element_type=jnp.float32)
    result = middle + gate_two * mlp_branch
    upstream = cotangent.astype(jnp.float32)
    d_gate_two = upstream * mlp_branch
    d_mlp = (upstream * gate_two).astype(jnp.bfloat16)
    d_hidden = dot_back(d_mlp, full_fc2)
    (d_pre,) = gelu_pull(d_hidden * channel_keep)
    d_pre_low = d_pre.astype(jnp.bfloat16)
    d_normed_two = dot_back(d_pre_low, full_fc1)
    d_middle_norm, d_shift_two, d_scale_two = norm_two_pull(d_normed_two)
    d_middle = upstream + d_middle_norm
    d_gate_one = d_middle * attn_branch
    d_attn = (d_middle * gate_one).astype(jnp.bfloat16)
    d_masked = dot_back(d_attn, full_out).astype(jnp.bfloat16)
    d_out_heads = d_masked.reshape(tok_rows, head_count, head_size) * head_keep[:, :, None].astype(
        jnp.bfloat16
    )
    delta = jnp.transpose(jnp.sum(d_out_heads.astype(jnp.float32) * attended_rows, axis=2))

    def block_terms(key_heads, value_heads, block_start):
        key_items = lax.dynamic_slice_in_dim(segment_row, block_start, key_heads.shape[0])
        same = own_items[:, None] == key_items[None, :]
        scores = (
            jnp.einsum("qhd,khd->hqk", query_heads, key_heads, preferred_element_type=jnp.float32)
            * score_scale
        )
        probs = jnp.where(same[None], jnp.exp(scores - log_total[:, :, None]), 0.0)
        d_probs = jnp.einsum(
            "qhd,khd->hqk", d_out_heads, value_heads, preferred_element_type=jnp.float32
        )
        d_scores = (probs * (d_probs - delta[:, :, None])).astype(jnp.bfloat16)
        d_query = (
            jnp.einsum("hqk,khd->qhd", d_scores, key_heads, preferred_element_type=jnp.float32)
            * score_scale
        )
        d_key = (
            jnp.einsum("hqk,qhd->khd", d_scores, query_heads, preferred_element_type=jnp.float32)
            * score_scale
        )
        d_value = jnp.einsum(
            "hqk,qhd->khd",
            probs.astype(jnp.bfloat16),
            d_out_heads,
            preferred_element_type=jnp.float32,
        )
        return (d_query, d_key, d_value)

    query_zero = jnp.zeros((tok_rows, head_count, head_size), jnp.float32)

    def cycle_turn(cycle_step, state):
        held_keys, held_values, acc_keys, acc_values, query_total = state
        source = (span_index - cycle_step) % cycle_size
        d_query_part, d_key_part, d_value_part = block_terms(
            held_keys.reshape(tok_rows, head_count, head_size),
            held_values.reshape(tok_rows, head_count, head_size),
            source * tok_rows,
        )
        acc_keys = acc_keys + d_key_part.reshape(tok_rows, model_width)
        acc_values = acc_values + d_value_part.reshape(tok_rows, model_width)
        held_keys, held_values = from_behind((held_keys, held_values), "blk", 1)
        acc_keys, acc_values = (
            from_behind(acc_keys.astype(jnp.bfloat16), "blk", 1).astype(acc_keys.dtype),
            from_behind(acc_values.astype(jnp.bfloat16), "blk", 1).astype(acc_values.dtype),
        )
        return (held_keys, held_values, acc_keys, acc_values, query_total + d_query_part)

    grad_zero = jnp.zeros((tok_rows, model_width), jnp.float32)
    cycle_state = lax.fori_loop(
        0, cycle_size, cycle_turn, (keys, values, grad_zero, grad_zero, query_zero)
    )
    d_key, d_value, d_query = (cycle_state[2], cycle_state[3], cycle_state[4])
    d_packed = jnp.concatenate(
        [d_query.reshape(tok_rows, model_width), d_key, d_value], axis=1
    ).astype(jnp.bfloat16)
    d_normed = dot_back(d_packed, full_qkv)
    d_input_norm, d_shift_one, d_scale_one = norm_one_pull(d_normed)
    grad_tokens = (d_middle + d_input_norm).astype(jnp.bfloat16)
    d_per_token = jnp.concatenate(
        [d_shift_one, d_scale_one, d_gate_one, d_shift_two, d_scale_two, d_gate_two], axis=1
    )
    d_mod_local = lax.dot_general(picker, d_per_token, (((0,), (0,)), ((), ())), precision=HIGH)
    d_modulation = lax.psum(d_mod_local.astype(jnp.bfloat16), "blk")
    d_lifted = dot_back(d_modulation, full_ada)
    (d_condition,) = silu_pull(d_lifted)
    leader = (span_index == 0).astype(jnp.float32)
    grad_temb = reduce_weight(spectrum.astype(jnp.float32), d_condition, leader)
    grad_ada = reduce_weight(lifted_low, d_modulation, leader)
    grad_qkv = reduce_weight(normed_low, d_packed, 1.0)
    grad_out = reduce_weight(masked_low, d_attn, 1.0)
    grad_fc1 = reduce_weight(normed_two_low, d_pre_low, 1.0)
    grad_fc2 = reduce_weight(hidden_low, d_mlp, 1.0)
    grad_temb, grad_ada, grad_qkv, grad_out, grad_fc1, grad_fc2 = (
        lax.psum(grad_temb.astype(jnp.bfloat16), "blk").astype(jnp.float32),
        lax.psum(grad_ada.astype(jnp.bfloat16), "blk").astype(jnp.float32),
        lax.psum(grad_qkv.astype(jnp.bfloat16), "blk").astype(jnp.float32),
        lax.psum(grad_out.astype(jnp.bfloat16), "blk").astype(jnp.float32),
        lax.psum(grad_fc1.astype(jnp.bfloat16), "blk").astype(jnp.float32),
        lax.psum(grad_fc2.astype(jnp.bfloat16), "blk").astype(jnp.float32),
    )
    return (
        result.astype(jnp.bfloat16),
        grad_tokens,
        grad_temb,
        grad_ada,
        grad_qkv,
        grad_out,
        grad_fc1,
        grad_fc2,
    )


def solution(mesh):
    placed = (
        P(("fsdp", "blk"), None),
        P("fsdp", None),
        P("fsdp", None),
        P("fsdp", None, None),
        P("fsdp", None, None),
        P(("fsdp", "blk")),
        P("fsdp", None),
        P("fsdp", None),
        P("fsdp", None),
        P("fsdp", None),
        P("fsdp", None),
        P("fsdp", None),
        P(("fsdp", "blk"), None),
    )
    return jax.shard_map(
        on_device,
        mesh=mesh,
        in_specs=placed,
        out_specs=(
            P(("fsdp", "blk"), None),
            P(("fsdp", "blk"), None),
            P("fsdp", None),
            P("fsdp", None),
            P("fsdp", None),
            P("fsdp", None),
            P("fsdp", None),
            P("fsdp", None),
        ),
        check_vma=False,
    )
```

profile of v0, /device:TPU:1, one launch (start us, length us, event | category | flops | bytes accessed | tf_op | source)
XLA Modules:
  0.0 2047.3 jit_solution(795229194309371699)
XLA Ops:
  20.0 142.4 %all-gather.8.cloned.1.call-done = bf16[1152,6912]{1,0:T(8,128)(2,1)} async-done(((bf16[288,6912]{1,0:T(8,128)(2,1)}), bf16[1152,6912]{1,0:T(8,128)(2,1)}) %all-gather.8.cloned.1.call-update) | async-done | bytes 15925264 | tf_op jit(solution)/shard_map/all_gather | solution.py:92
  179.0 69.2 %all-gather.10.cloned.1.call-done = bf16[1152,3456]{1,0:T(8,128)(2,1)} async-done(((bf16[288,3456]{1,0:T(8,128)(2,1)}), bf16[1152,3456]{1,0:T(8,128)(2,1)}) %all-gather.10.cloned.1.call-update) | async-done | bytes 7962640 | tf_op jit(solution)/shard_map/all_gather | solution.py:93
  265.8 63.0 %all-gather.12.cloned.1.call-done = bf16[3072,1152]{1,0:T(8,128)(2,1)} async-done(((bf16[384,1152]{1,0:T(8,128)(2,1)}), bf16[3072,1152]{1,0:T(8,128)(2,1)}) %all-gather.12.cloned.1.call-update) | async-done | bytes 7077904 | tf_op jit(solution)/shard_map/all_gather | solution.py:120
  328.9 25.3 %reshape.210 = bf16[8,384,16,72]{3,2,1,0:T(8,128)(2,1)} reshape(bf16[3072,1152]{1,0:T(8,128)(2,1)} %all-gather.12.cloned.1.call-done) | data formatting | bytes 14155776 | tf_op jit(solution)/shard_map/reshape | solution.py:123
  354.2 15.4 copy.33
  369.5 31.3 %all-gather.14.cloned.1.call-done = bf16[3072,1152]{1,0:T(8,128)(2,1)} async-done(((bf16[384,1152]{1,0:T(8,128)(2,1)}), bf16[3072,1152]{1,0:T(8,128)(2,1)}) %all-gather.14.cloned.1.call-update) | async-done | bytes 7077904 | tf_op jit(solution)/shard_map/all_gather | solution.py:121
  400.8 25.3 %reshape.211 = bf16[8,384,16,72]{3,2,1,0:T(8,128)(2,1)} reshape(bf16[3072,1152]{1,0:T(8,128)(2,1)} %all-gather.14.cloned.1.call-done) | data formatting | bytes 14155776 | tf_op jit(solution)/shard_map/reshape | solution.py:124
  426.1 15.4 copy.34
  441.5 176.5 %while.39 = (s32[]{:T(128)}, f32[16,384]{1,0:T(8,128)S(1)}, f32[16,384]{1,0:T(8,128)S(1)}, f32[16,384,72]{1,2,0:T(8,128)}, s32[384]{0:T(512)S(1)}, /*index=5*/s3...) while((s32[]{:T(128)}, f32[16,384]{1,0:T(8,128)S(1)}, ...), condition=%wide.region_5.6_spmd.clone, body=%wide.region_2.5_spmd.clone.sunk | while | flops 706934784 | bytes 73243864 | solution.py:149
  656.5 16.4 fusion.32
  673.0 10.6 multiply_reduce_fusion
  683.7 11.4 fusion.93
  707.5 445.2 %while.40 = (s32[]{:T(128)}, bf16[384,1152]{0,1:T(8,128)(2,1)}, bf16[384,1152]{0,1:T(8,128)(2,1)}, f32[384,1152]{0,1:T(8,128)S(1)}, f32[384,1152]{0,1:T(8,128)},...) while((s32[]{:T(128)}, bf16[384,1152]{0,1:T(8,128)(2,1)}, ...), condition=%wide.region_12.13_spmd.clone, body=%wide.region_11.12_spmd.clone.sunk | while | flops 1727741952 | bytes 131955384 | solution.py:235
  753.3 9.6 collective-permute-done.1
  809.0 9.6 collective-permute-done.1
  864.6 9.6 collective-permute-done.1
  920.3 9.6 collective-permute-done.1
  975.9 9.6 collective-permute-done.1
  1031.6 9.6 collective-permute-done.1
  1087.2 9.6 collective-permute-done.1
  1142.9 9.6 collective-permute-done.1
  1175.5 64.1 %all-reduce.4.cloned.1.call-done = bf16[8,6912]{1,0:T(8,128)(2,1)} async-done(((bf16[8,6912]{1,0:T(8,128)(2,1)}), bf16[8,6912]{1,0:T(8,128)(2,1)}) %all-reduce.4.cloned.1.call-update) | async-done | bytes 110608 | tf_op jit(solution)/shard_map/psum | solution.py:249
  1239.5 9.8 fusion.99
  1254.1 9.4 convolution_convert_fusion.2
  1264.7 10.0 convolution_convert_fusion.1
  1275.1 10.7 convolution_convert_fusion
  1294.8 25.9 %reduce-scatter.13.cloned.1.call-done = bf16[288,1152]{1,0:T(8,128)(2,1)} async-done(((bf16[1152,1152]{1,0:T(8,128)(2,1)}), bf16[288,1152]{1,0:T(8,128)(2,1)}) %reduce-scatter.13.cloned.1.call-update) | async-done | bytes 663568 | tf_op jit(solution)/shard_map/reduce_scatter | solution.py:62
  1320.7 87.0 %reduce-scatter.11.cloned.1.call-done = bf16[288,3456]{1,0:T(8,128)(2,1)} async-done(((bf16[1152,3456]{1,0:T(8,128)(2,1)}), bf16[288,3456]{1,0:T(8,128)(2,1)}) %reduce-scatter.11.cloned.1.call-update) | async-done | bytes 1990672 | tf_op jit(solution)/shard_map/reduce_scatter | solution.py:62
  1407.7 107.9 %reduce-scatter.15.cloned.1.call-done = bf16[288,4608]{1,0:T(8,128)(2,1)} async-done(((bf16[1152,4608]{1,0:T(8,128)(2,1)}), bf16[288,4608]{1,0:T(8,128)(2,1)}) %reduce-scatter.15.cloned.1.call-update) | async-done | bytes 2654224 | tf_op jit(solution)/shard_map/reduce_scatter | solution.py:62
  1515.6 108.0 %reduce-scatter.17.cloned.1.call-done = bf16[1152,1152]{1,0:T(8,128)(2,1)} async-done(((bf16[4608,1152]{1,0:T(8,128)(2,1)}), bf16[1152,1152]{1,0:T(8,128)(2,1)}) %reduce-scatter.17.cloned.1.call-update) | async-done | bytes 2654224 | tf_op jit(solution)/shard_map/reduce_scatter | solution.py:62
  1623.6 150.6 %reduce-scatter.9.cloned.1.call-done = bf16[288,6912]{1,0:T(8,128)(2,1)} async-done(((bf16[1152,6912]{1,0:T(8,128)(2,1)}), bf16[288,6912]{1,0:T(8,128)(2,1)}) %reduce-scatter.9.cloned.1.call-update) | async-done | bytes 3981328 | tf_op jit(solution)/shard_map/reduce_scatter | solution.py:62
  1774.2 250.2 %all-reduce.6.cloned.1.call-done = (bf16[64,1152]{1,0:T(8,128)(2,1)}, bf16[288,6912]{1,0:T(8,128)(2,1)}, bf16[288,3456]{1,0:T(8,128)(2,1)}, bf16[288,1152]{1,0:T...) async-done(((bf16[64,1152]{1,0:T(8,128)(2,1)}, bf16[288,6912]{1,0:T(8,128)(2,1)}, bf16[288,3456]{1,0:T(8,128)(2,1)}, bf16[288,1152]{1,0:T(8,128)(2,1)}, ...) | async-done | bytes 12091408 | tf_op jit(solution)/shard_map/psum | solution.py:260
  (577 shorter events, 678.5 us)
Async XLA Ops:
  7.2 155.1 %all-gather.8.cloned.1.call-start = ((), (), s32[]{:S(2)}) async-start(), calls=%async_computation.6 | async-start | bytes 19906560 | tf_op jit(solution)/shard_map/all_gather | solution.py:92
  7.9 240.4 %all-gather.10.cloned.1.call-start = ((), (), s32[]{:S(2)}) async-start(), calls=%async_computation.7 | async-start | bytes 9953280 | tf_op jit(solution)/shard_map/all_gather | solution.py:93
  8.7 320.2 %all-gather.12.cloned.1.call-start = ((), (), s32[]{:S(2)}) async-start(), calls=%async_computation.8 | async-start | bytes 7962624 | tf_op jit(solution)/shard_map/all_gather | solution.py:120
  257.1 143.7 %all-gather.14.cloned.1.call-start = ((), (), s32[]{:S(2)}) async-start(), calls=%async_computation.9 | async-start | bytes 7962624 | tf_op jit(solution)/shard_map/all_gather | solution.py:121
  257.6 362.7 %all-gather.16.cloned.1.call-start = ((), (), s32[]{:S(2)}) async-start(), calls=%async_computation.10 | async-start | bytes 3317760 | tf_op jit(solution)/shard_map/all_gather | solution.py:94
  258.2 371.5 %all-gather.18.cloned.1.call-start = ((), (), s32[]{:S(2)}) async-start(), calls=%async_computation.11 | async-start | bytes 13271040 | tf_op jit(solution)/shard_map/all_gather | solution.py:95
  258.8 397.7 %all-gather.20.cloned.1.call-start = ((), (), s32[]{:S(2)}) async-start(), calls=%async_computation.12 | async-start | bytes 13271040 | tf_op jit(solution)/shard_map/all_gather | solution.py:96
  259.6 980.0 %all-reduce.4.cloned.1.call-start = ((), (), s32[]{:S(2)}) async-start(), calls=%async_computation.13 | async-start | bytes 221184 | tf_op jit(solution)/shard_map/psum | solution.py:249
  727.3 26.0 %collective-permute-start = (bf16[384,1152]{0,1:T(8,128)(2,1)S(1)}, bf16[384,1152]{0,1:T(8,128)(2,1)}, u32[]{:S(2)}, u32[]{:S(2)}) collective-permute-start(bf16[384,1152]{0,1:T(8,128)(2,1)S(1)} %copy.62), channel_id=1, source_target_pairs={{0,1},{1,2},{2,3},{3,4},{4,5},{5,6},{6,7},{7,0},{8,9},{9,10},{10,1... | collective-permute-start | bytes 2654216 | tf_op jit(solution)/shard_map/while/body/eval_jaxpr/ppermute | solution.py:14
  728.9 34.0 %collective-permute-start.1 = (bf16[384,1152]{0,1:T(8,128)(2,1)}, bf16[384,1152]{0,1:T(8,128)(2,1)}, u32[]{:S(2)}, u32[]{:S(2)}) collective-permute-start(bf16[384,1152]{0,1:T(8,128)(2,1)} %copy.63), channel_id=1, source_target_pairs={{0,1},{1,2},{2,3},{3,4},{4,5},{5,6},{6,7},{7,0},{8,9},{9,10},{10,1... | collective-permute-start | bytes 2654216 | tf_op jit(solution)/shard_map/while/body/eval_jaxpr/ppermute | solution.py:14
  783.0 16.6 collective-permute-start.3
  783.0 26.0 %collective-permute-start = (bf16[384,1152]{0,1:T(8,128)(2,1)S(1)}, bf16[384,1152]{0,1:T(8,128)(2,1)}, u32[]{:S(2)}, u32[]{:S(2)}) collective-permute-start(bf16[384,1152]{0,1:T(8,128)(2,1)S(1)} %copy.62), channel_id=1, source_target_pairs={{0,1},{1,2},{2,3},{3,4},{4,5},{5,6},{6,7},{7,0},{8,9},{9,10},{10,1... | collective-permute-start | bytes 2654216 | tf_op jit(solution)/shard_map/while/body/eval_jaxpr/ppermute | solution.py:14
  784.6 34.0 %collective-permute-start.1 = (bf16[384,1152]{0,1:T(8,128)(2,1)}, bf16[384,1152]{0,1:T(8,128)(2,1)}, u32[]{:S(2)}, u32[]{:S(2)}) collective-permute-start(bf16[384,1152]{0,1:T(8,128)(2,1)} %copy.63), channel_id=1, source_target_pairs={{0,1},{1,2},{2,3},{3,4},{4,5},{5,6},{6,7},{7,0},{8,9},{9,10},{10,1... | collective-permute-start | bytes 2654216 | tf_op jit(solution)/shard_map/while/body/eval_jaxpr/ppermute | solution.py:14
  838.6 26.0 %collective-permute-start = (bf16[384,1152]{0,1:T(8,128)(2,1)S(1)}, bf16[384,1152]{0,1:T(8,128)(2,1)}, u32[]{:S(2)}, u32[]{:S(2)}) collective-permute-start(bf16[384,1152]{0,1:T(8,128)(2,1)S(1)} %copy.62), channel_id=1, source_target_pairs={{0,1},{1,2},{2,3},{3,4},{4,5},{5,6},{6,7},{7,0},{8,9},{9,10},{10,1... | collective-permute-start | bytes 2654216 | tf_op jit(solution)/shard_map/while/body/eval_jaxpr/ppermute | solution.py:14
  840.2 34.0 %collective-permute-start.1 = (bf16[384,1152]{0,1:T(8,128)(2,1)}, bf16[384,1152]{0,1:T(8,128)(2,1)}, u32[]{:S(2)}, u32[]{:S(2)}) collective-permute-start(bf16[384,1152]{0,1:T(8,128)(2,1)} %copy.63), channel_id=1, source_target_pairs={{0,1},{1,2},{2,3},{3,4},{4,5},{5,6},{6,7},{7,0},{8,9},{9,10},{10,1... | collective-permute-start | bytes 2654216 | tf_op jit(solution)/shard_map/while/body/eval_jaxpr/ppermute | solution.py:14
  894.3 26.0 %collective-permute-start = (bf16[384,1152]{0,1:T(8,128)(2,1)S(1)}, bf16[384,1152]{0,1:T(8,128)(2,1)}, u32[]{:S(2)}, u32[]{:S(2)}) collective-permute-start(bf16[384,1152]{0,1:T(8,128)(2,1)S(1)} %copy.62), channel_id=1, source_target_pairs={{0,1},{1,2},{2,3},{3,4},{4,5},{5,6},{6,7},{7,0},{8,9},{9,10},{10,1... | collective-permute-start | bytes 2654216 | tf_op jit(solution)/shard_map/while/body/eval_jaxpr/ppermute | solution.py:14
  895.9 33.9 %collective-permute-start.1 = (bf16[384,1152]{0,1:T(8,128)(2,1)}, bf16[384,1152]{0,1:T(8,128)(2,1)}, u32[]{:S(2)}, u32[]{:S(2)}) collective-permute-start(bf16[384,1152]{0,1:T(8,128)(2,1)} %copy.63), channel_id=1, source_target_pairs={{0,1},{1,2},{2,3},{3,4},{4,5},{5,6},{6,7},{7,0},{8,9},{9,10},{10,1... | collective-permute-start | bytes 2654216 | tf_op jit(solution)/shard_map/while/body/eval_jaxpr/ppermute | solution.py:14
  949.9 26.0 %collective-permute-start = (bf16[384,1152]{0,1:T(8,128)(2,1)S(1)}, bf16[384,1152]{0,1:T(8,128)(2,1)}, u32[]{:S(2)}, u32[]{:S(2)}) collective-permute-start(bf16[384,1152]{0,1:T(8,128)(2,1)S(1)} %copy.62), channel_id=1, source_target_pairs={{0,1},{1,2},{2,3},{3,4},{4,5},{5,6},{6,7},{7,0},{8,9},{9,10},{10,1... | collective-permute-start | bytes 2654216 | tf_op jit(solution)/shard_map/while/body/eval_jaxpr/ppermute | solution.py:14
  951.6 33.9 %collective-permute-start.1 = (bf16[384,1152]{0,1:T(8,128)(2,1)}, bf16[384,1152]{0,1:T(8,128)(2,1)}, u32[]{:S(2)}, u32[]{:S(2)}) collective-permute-start(bf16[384,1152]{0,1:T(8,128)(2,1)} %copy.63), channel_id=1, source_target_pairs={{0,1},{1,2},{2,3},{3,4},{4,5},{5,6},{6,7},{7,0},{8,9},{9,10},{10,1... | collective-permute-start | bytes 2654216 | tf_op jit(solution)/shard_map/while/body/eval_jaxpr/ppermute | solution.py:14
  1005.6 26.0 %collective-permute-start = (bf16[384,1152]{0,1:T(8,128)(2,1)S(1)}, bf16[384,1152]{0,1:T(8,128)(2,1)}, u32[]{:S(2)}, u32[]{:S(2)}) collective-permute-start(bf16[384,1152]{0,1:T(8,128)(2,1)S(1)} %copy.62), channel_id=1, source_target_pairs={{0,1},{1,2},{2,3},{3,4},{4,5},{5,6},{6,7},{7,0},{8,9},{9,10},{10,1... | collective-permute-start | bytes 2654216 | tf_op jit(solution)/shard_map/while/body/eval_jaxpr/ppermute | solution.py:14
  1007.2 33.9 %collective-permute-start.1 = (bf16[384,1152]{0,1:T(8,128)(2,1)}, bf16[384,1152]{0,1:T(8,128)(2,1)}, u32[]{:S(2)}, u32[]{:S(2)}) collective-permute-start(bf16[384,1152]{0,1:T(8,128)(2,1)} %copy.63), channel_id=1, source_target_pairs={{0,1},{1,2},{2,3},{3,4},{4,5},{5,6},{6,7},{7,0},{8,9},{9,10},{10,1... | collective-permute-start | bytes 2654216 | tf_op jit(solution)/shard_map/while/body/eval_jaxpr/ppermute | solution.py:14
  1061.3 26.0 %collective-permute-start = (bf16[384,1152]{0,1:T(8,128)(2,1)S(1)}, bf16[384,1152]{0,1:T(8,128)(2,1)}, u32[]{:S(2)}, u32[]{:S(2)}) collective-permute-start(bf16[384,1152]{0,1:T(8,128)(2,1)S(1)} %copy.62), channel_id=1, source_target_pairs={{0,1},{1,2},{2,3},{3,4},{4,5},{5,6},{6,7},{7,0},{8,9},{9,10},{10,1... | collective-permute-start | bytes 2654216 | tf_op jit(solution)/shard_map/while/body/eval_jaxpr/ppermute | solution.py:14
  1062.9 34.0 %collective-permute-start.1 = (bf16[384,1152]{0,1:T(8,128)(2,1)}, bf16[384,1152]{0,1:T(8,128)(2,1)}, u32[]{:S(2)}, u32[]{:S(2)}) collective-permute-start(bf16[384,1152]{0,1:T(8,128)(2,1)} %copy.63), channel_id=1, source_target_pairs={{0,1},{1,2},{2,3},{3,4},{4,5},{5,6},{6,7},{7,0},{8,9},{9,10},{10,1... | collective-permute-start | bytes 2654216 | tf_op jit(solution)/shard_map/while/body/eval_jaxpr/ppermute | solution.py:14
  1116.9 26.0 %collective-permute-start = (bf16[384,1152]{0,1:T(8,128)(2,1)S(1)}, bf16[384,1152]{0,1:T(8,128)(2,1)}, u32[]{:S(2)}, u32[]{:S(2)}) collective-permute-start(bf16[384,1152]{0,1:T(8,128)(2,1)S(1)} %copy.62), channel_id=1, source_target_pairs={{0,1},{1,2},{2,3},{3,4},{4,5},{5,6},{6,7},{7,0},{8,9},{9,10},{10,1... | collective-permute-start | bytes 2654216 | tf_op jit(solution)/shard_map/while/body/eval_jaxpr/ppermute | solution.py:14
  1118.5 34.0 %collective-permute-start.1 = (bf16[384,1152]{0,1:T(8,128)(2,1)}, bf16[384,1152]{0,1:T(8,128)(2,1)}, u32[]{:S(2)}, u32[]{:S(2)}) collective-permute-start(bf16[384,1152]{0,1:T(8,128)(2,1)} %copy.63), channel_id=1, source_target_pairs={{0,1},{1,2},{2,3},{3,4},{4,5},{5,6},{6,7},{7,0},{8,9},{9,10},{10,1... | collective-permute-start | bytes 2654216 | tf_op jit(solution)/shard_map/while/body/eval_jaxpr/ppermute | solution.py:14
  1175.2 119.6 %reduce-scatter.7.cloned.1.call-start = ((), (), s32[]{:S(2)}) async-start(), calls=%async_computation.14 | async-start | bytes 737280 | tf_op jit(solution)/shard_map/reduce_scatter | solution.py:62
  1250.9 69.8 %reduce-scatter.13.cloned.1.call-start = ((), (), s32[]{:S(2)}) async-start(), calls=%async_computation.17 | async-start | bytes 3317760 | tf_op jit(solution)/shard_map/reduce_scatter | solution.py:62
  1254.1 153.6 %reduce-scatter.11.cloned.1.call-start = ((), (), s32[]{:S(2)}) async-start(), calls=%async_computation.16 | async-start | bytes 9953280 | tf_op jit(solution)/shard_map/reduce_scatter | solution.py:62
  1263.6 252.0 %reduce-scatter.15.cloned.1.call-start = ((), (), s32[]{:S(2)}) async-start(), calls=%async_computation.18 | async-start | bytes 13271040 | tf_op jit(solution)/shard_map/reduce_scatter | solution.py:62
  1274.8 348.9 %reduce-scatter.17.cloned.1.call-start = ((), (), s32[]{:S(2)}) async-start(), calls=%async_computation.19 | async-start | bytes 13271040 | tf_op jit(solution)/shard_map/reduce_scatter | solution.py:62
  1285.8 488.4 %reduce-scatter.9.cloned.1.call-start = ((), (), s32[]{:S(2)}) async-start(), calls=%async_computation.15 | async-start | bytes 19906560 | tf_op jit(solution)/shard_map/reduce_scatter | solution.py:62
  1294.7 729.8 %all-reduce.6.cloned.1.call-start = ((), (), s32[]{:S(2)}) async-start(), calls=%async_computation.20 | async-start | bytes 24182784 | tf_op jit(solution)/shard_map/psum | solution.py:260
  (139 other events, 1864.9 us)
Sparse Core Ops, SparseCore 0:
  9.9 152.4 all-gather.7
  164.2 84.0 all-gather.9
  257.2 71.6 all-gather.11
  330.9 69.8 all-gather.13
  402.5 38.0 all-gather.15
  442.3 106.1 all-gather.17
  550.3 106.1 all-gather.19
  1175.3 64.2 all-reduce.3
  1251.0 26.1 reduce-scatter.6
  1280.7 39.9 reduce-scatter.12
  1324.4 83.2 reduce-scatter.10
  1410.9 104.6 reduce-scatter.14
  1519.0 104.6 reduce-scatter.16
  1626.9 147.2 reduce-scatter.8
  1776.9 247.5 all-reduce.5
where the time goes:
time: 2060 us; the launch traced here: 2050 us
  waiting for transfers between devices  1310 us (64%)
  matrix products  356 us (17%)
  local copies, waits for them, and re-layouts  175 us (8%)
  other arithmetic  134 us (7%)
  starting transfers between devices  33.5 us (2%)
    reduce_scatter x6, waiting for transfers between devices, reduce_weight(): lax.psum_scatter(grad_term(left, right, factor).astype(jnp.bfloat16), 'fs...  479 us
    psum x1, waiting for transfers between devices, on_device(): lax.psum(grad_temb.astype(jnp.bfloat16), 'blk').astype(jnp.float32)  250 us
    ppermute x32, waiting for transfers between devices, from_behind(): lax.ppermute(array, axis, [(i, (i + by) % devices) for i in range(devices)])  195 us
    all_gather x1, waiting for transfers between devices, on_device(): lax.all_gather(w_ada, 'fsdp', axis=0, tiled=True)  142 us
    all_gather x1, waiting for transfers between devices, on_device(): lax.all_gather(w_qkv, 'fsdp', axis=0, tiled=True)  69.2 us
    psum x1, waiting for transfers between devices, on_device(): d_modulation = lax.psum(d_mod_local.astype(jnp.bfloat16), 'blk')  64.1 us
    all_gather x1, waiting for transfers between devices, on_device(): key_piece = lax.all_gather(keys, 'blk', axis=0, tiled=True)  63 us
    dot_general x8, matrix products, one_block(): jnp.einsum('qhd,khd->hqk', query_heads, key_heads, preferred_element_type...  55.8 us
  transfers between devices with their start and end apart: 47, of which 38 were waited for; matrix products, arithmetic and copies ran while one was open for 20% of the time, Pallas kernels for 0%

commit v1 on v0

v1 whole, which is shorter than its diff:
```python
import functools
import math

import jax
import jax.numpy as jnp
from jax import lax
from jax.experimental import pallas as pl
from jax.experimental.pallas import tpu as pltpu
from jax.sharding import PartitionSpec as P

HIGH = lax.Precision.HIGHEST
BF16 = jnp.bfloat16
F32 = jnp.float32
I32 = jnp.int32
LANES = 128
BLOCK = 256
NEG = -1e30
LOG2E = 1.4426950408889634

VMEM = pl.BlockSpec(memory_space=pltpu.VMEM)
SMEM = pl.BlockSpec(memory_space=pltpu.SMEM)
ANY = pl.BlockSpec(memory_space=pl.ANY)


def shape(dims, kind=BF16):
    return jax.ShapeDtypeStruct(tuple(dims), kind)


def run(name, body, ins, outs, scratch=(), flops=0, vmem=48, **more):
    moved = sum(a.size * a.dtype.itemsize for _, a in ins)
    moved += sum(math.prod(o.shape) * jnp.dtype(o.dtype).itemsize for _, o in outs)
    return pl.pallas_call(
        body,
        out_shape=[o for _, o in outs],
        in_specs=[s for s, _ in ins],
        out_specs=[s for s, _ in outs],
        scratch_shapes=list(scratch),
        compiler_params=pltpu.CompilerParams(vmem_limit_bytes=vmem << 20),
        cost_estimate=pl.CostEstimate(flops=flops, bytes_accessed=moved, transcendentals=0),
        name=name,
        **more,
    )(*[a for _, a in ins])


def swap(array, axis, by):
    size = lax.axis_size(axis)
    return lax.ppermute(array, axis, [(i, i ^ by) for i in range(size)])


def after(array, *others):
    return lax.optimization_barrier((array,) + others)[0]


def nn(left, right):
    return lax.dot_general(left, right, (((1,), (0,)), ((), ())), preferred_element_type=F32)


def nt(left, right):
    return lax.dot_general(left, right, (((1,), (1,)), ((), ())), preferred_element_type=F32)


def tn(left, right):
    return lax.dot_general(left, right, (((0,), (0,)), ((), ())), preferred_element_type=F32)


def each(count, step):
    def one(index, carry):
        step(index)
        return carry

    lax.fori_loop(0, count, one, 0)


def normal(values):
    center = values - jnp.mean(values, axis=-1, keepdims=True)
    scale = lax.rsqrt(jnp.mean(center * center, axis=-1, keepdims=True) + 1e-06)
    return center * scale, scale


def normal_back(grad, normed, scale):
    along = jnp.mean(grad * normed, axis=-1, keepdims=True)
    return scale * (grad - jnp.mean(grad, axis=-1, keepdims=True) - normed * along)


def sort_body(width, items_ref, keep_ref, x_ref, c_ref, xs_ref, cs_ref, hot_ref, info_ref, perm_ref):
    count = items_ref.shape[1]
    slots = hot_ref.shape[0]
    items = items_ref[...]
    slot = lax.broadcasted_iota(I32, (slots, count), 0)
    hot = (items == slot).astype(F32)
    start = jnp.sum((items < slot).astype(F32), axis=1, keepdims=True)
    end = start + jnp.sum(hot, axis=1, keepdims=True)
    row = lax.broadcasted_iota(I32, (count, count), 0)
    col = lax.broadcasted_iota(I32, (count, count), 1)
    rank = nn(hot.astype(BF16), (row <= col).astype(BF16))
    place = jnp.sum(hot * (start + rank), axis=0, keepdims=True) - 1.0
    perm = (row.astype(F32) == place).astype(BF16)
    perm_ref[...] = perm
    xs_ref[...] = nn(perm, x_ref[...]).astype(BF16)
    cs_ref[...] = nn(perm, c_ref[...]).astype(BF16)
    keep = jnp.broadcast_to(keep_ref[...].astype(F32), (slots, count)).astype(BF16)
    kept = nt(keep, perm)
    at = lax.broadcasted_iota(I32, (slots, count), 1).astype(F32)
    hot_ref[...] = kept * ((at >= start) & (at < end)).astype(F32)
    head = (lax.broadcasted_iota(I32, (slots, LANES), 1) * width).astype(F32)
    own = ((head >= start) & (head < end)).astype(F32)
    which = lax.broadcasted_iota(I32, (slots, LANES), 0).astype(F32)
    info_ref[0:1, :] = jnp.sum(own * which, axis=0, keepdims=True).astype(I32)
    info_ref[1:2, :] = (jnp.sum(own * start, axis=0, keepdims=True) / width).astype(I32)
    info_ref[2:3, :] = (jnp.sum(own * end, axis=0, keepdims=True) / width).astype(I32)
    info_ref[3:8, :] = jnp.zeros((5, LANES), I32)


def pick_heads_body(own, size, ids_ref, w_ref, o_ref):
    width = w_ref.shape[1] // 3
    first = ids_ref[1] * (own * size)
    row = lax.broadcasted_iota(I32, (width, LANES), 0)
    col = lax.broadcasted_iota(I32, (width, LANES), 1)
    for head in range(own):
        mark = (row == first + head * size + col) & (col < size)
        pick = mark.astype(F32).astype(BF16)
        for part in range(3):
            at = (part * own + head) * LANES
            o_ref[:, at : at + LANES] = nn(
                w_ref[:, part * width : (part + 1) * width], pick
            ).astype(BF16)


def pick_half_body(parts, ids_ref, w_ref, o_ref):
    half = w_ref.shape[1] // parts // 2
    for core in range(2):

        @pl.when(ids_ref[2] == core)
        def _():
            for part in range(parts):
                at = (2 * part + core) * half
                o_ref[:, part * half : (part + 1) * half] = w_ref[:, at : at + half]


def fetch(pairs, sems):
    copies = []
    for index, (source, target) in enumerate(pairs):
        copy = pltpu.make_async_copy(source, target, sems.at[index])
        copy.start()
        copies.append(copy)
    return copies


def first_body(chips, plan, ids_ref, info_ref, mod_ref, *refs):
    n_x = 2 + 4 * (chips - 1)
    x_refs, refs = refs[:n_x], refs[n_x:]
    w_refs, (h_ref, o_ref, x_all, w_all, sems) = refs[: len(plan)], refs[len(plan) :]
    width = x_refs[0].shape[1]
    f, b, c = ids_ref[0], ids_ref[1], ids_ref[2]
    z = b // 2
    u = pl.program_id(0)

    @pl.when(u == 0)
    def _():
        rows = plan[-1][2]
        todo = [(None, x_refs[0], x_all.at[b]), (None, x_refs[1], x_all.at[b + 1 - 2 * c])]
        for s in range(1, chips):
            left, right = (z - s) * 2, (z + s) * 2
            at = 2 + 4 * (s - 1)
            todo.append((z >= s, x_refs[at], x_all.at[jnp.maximum(left, 0) + c]))
            todo.append((z >= s, x_refs[at + 1], x_all.at[jnp.maximum(left, 0) + 1 - c]))
            capped = jnp.minimum(right, 2 * chips - 2)
            todo.append((z + s < chips, x_refs[at + 2], x_all.at[capped + c]))
            todo.append((z + s < chips, x_refs[at + 3], x_all.at[capped + 1 - c]))
        for ref, (k, start, _) in zip(w_refs, plan):
            at = pl.multiple_of(lax.bitwise_xor(f, k) * rows + start, 16)
            todo.append((None, ref, w_all.at[pl.ds(at, ref.shape[0])]))
        for phase in range(2):
            for index, (when, source, target) in enumerate(todo):
                copy = pltpu.make_async_copy(source, target, sems.at[index])
                act = copy.wait if phase else copy.start
                if when is None:
                    act()
                else:
                    pl.when(when)(act)

    slot = info_ref[0, u]
    shift = mod_ref[pl.ds(slot, 1), 0:width]
    scale = mod_ref[pl.ds(slot, 1), width : 2 * width]
    rows = BLOCK // (2 * chips)
    part = x_all[:, pl.ds(pl.multiple_of(u * rows, rows), rows), :]
    values = part.reshape(BLOCK, width).astype(F32)
    normed, _ = normal(values)
    low = (normed * (1.0 + scale) + shift).astype(BF16)
    h_ref[0] = low
    o_ref[0] = nn(low, w_all[...]).astype(BF16)


def exchange_lanes(tiles, width):
    tiles = list(tiles)
    count = len(tiles)
    group = lax.broadcasted_iota(I32, tiles[0].shape, 1) // width
    half = count // 2
    while half:
        low = (group // half) % 2 == 0
        fresh = list(tiles)
        for i in range(count):
            if (i // half) % 2 == 0:
                a, d = tiles[i], tiles[i + half]
                fresh[i] = jnp.where(low, a, pltpu.roll(d, half * width, 1))
                fresh[i + half] = jnp.where(low, pltpu.roll(a, LANES - half * width, 1), d)
        tiles = fresh
        half //= 2
    return tiles


def attend_body(own, size, blocks, ids_ref, info_ref, mask_ref, qkv_ref, o_ref, lse_ref, *refs):
    outs, (held,) = refs[:blocks], refs[blocks:]
    units = qkv_ref.shape[0]
    width = BLOCK // blocks
    b = ids_ref[1]
    scale = LOG2E / math.sqrt(size)
    pad = -size % 16

    def one_unit(u):
        queries = [qkv_ref[u, :, h * LANES : (h + 1) * LANES] for h in range(own)]

        def one_block(j, carry):
            fresh = []
            for h in range(own):
                top, total, acc = carry[h]
                keys = qkv_ref[j, :, (own + h) * LANES : (own + h + 1) * LANES]
                at = (2 * own + h) * LANES
                values = qkv_ref[j, :, at : at + LANES]
                scores = nt(keys, queries[h]) * scale
                new_top = jnp.maximum(top, jnp.max(scores, axis=0, keepdims=True))
                probs = jnp.exp2(scores - new_top)
                decay = jnp.exp2(top - new_top)
                total = total * decay + jnp.sum(probs, axis=0, keepdims=True)
                acc = acc * decay + tn(values, probs.astype(BF16))
                fresh.append((new_top, total, acc))
            return tuple(fresh)

        start = tuple(
            (
                jnp.full((1, BLOCK), NEG, F32),
                jnp.zeros((1, BLOCK), F32),
                jnp.zeros((LANES, BLOCK), F32),
            )
            for _ in range(own)
        )
        done = lax.fori_loop(info_ref[1, u], info_ref[2, u], one_block, start)
        slot = info_ref[0, u]
        rows = []
        for h in range(own):
            top, total, acc = done[h]
            keep = mask_ref[slot, b * own + h].astype(F32)
            rows.append((acc * (keep / total))[0:size])
            lse_ref[u, h : h + 1, :] = top + jnp.log2(total)
        held[u] = jnp.concatenate(rows, axis=0) if own > 1 else rows[0]
        o_ref[u] = held[u].astype(BF16)

    each(units, one_unit)
    groups = LANES // width
    for g in range(units // groups):
        for e in range(blocks // groups):
            tiles = [
                held[groups * g + i, :, e * LANES : (e + 1) * LANES] for i in range(groups)
            ]
            for j, tile in enumerate(exchange_lanes(tiles, width)):
                device = groups * e + j
                for k in range(blocks):

                    @pl.when(lax.bitwise_xor(b, k) == device)
                    def _():
                        outs[k][:, g * LANES : (g + 1) * LANES] = tile.astype(BF16)


def attend_back_body(own, size, blocks, ids_ref, info_ref, mask_ref, qkv_ref, o_ref, lse_ref, *refs):
    pieces, (d_ref, given, up, delta, d_q, d_k, d_v) = refs[:blocks], refs[blocks:]
    units = qkv_ref.shape[0]
    width = BLOCK // blocks
    b = ids_ref[1]
    factor = 1.0 / math.sqrt(size)
    scale = LOG2E * factor
    for k in range(blocks):
        given[lax.bitwise_xor(b, k)] = pieces[k][...]
    up[...] = jnp.zeros_like(up)
    groups = LANES // width
    for g in range(units // groups):
        for e in range(blocks // groups):
            tiles = [
                given[groups * e + j, :, g * LANES : (g + 1) * LANES].astype(F32)
                for j in range(groups)
            ]
            for i, tile in enumerate(exchange_lanes(tiles, width)):
                unit = groups * g + i
                slot = info_ref[0, unit]
                for h in range(own):
                    keep = mask_ref[slot, b * own + h].astype(F32)
                    kept = tile[h * size : (h + 1) * size] * keep
                    up[unit, h, 0:size, e * LANES : (e + 1) * LANES] = kept.astype(BF16)
                    mine = o_ref[unit, h * size : (h + 1) * size, e * LANES : (e + 1) * LANES]
                    delta[unit, h : h + 1, e * LANES : (e + 1) * LANES] = jnp.sum(
                        kept * mine.astype(F32), axis=0, keepdims=True
                    )
    d_q[...] = jnp.zeros_like(d_q)

    def one_unit(j):
        d_k[...] = jnp.zeros_like(d_k)
        d_v[...] = jnp.zeros_like(d_v)
        keys = [qkv_ref[j, :, (own + h) * LANES : (own + h + 1) * LANES] for h in range(own)]
        turned = [keys[h].astype(F32).T.astype(BF16) for h in range(own)]

        def one_block(i, carry):
            for h in range(own):
                queries = qkv_ref[i, :, h * LANES : (h + 1) * LANES]
                at = (2 * own + h) * LANES
                values = qkv_ref[j, :, at : at + LANES]
                scores = nt(keys[h], queries) * scale
                probs = jnp.exp2(scores - lse_ref[i, h : h + 1, :])
                d_probs = nn(values, up[i, h])
                d_scores = (probs * (d_probs - delta[i, h : h + 1, :])).astype(BF16)
                d_k[h] += nn(d_scores, queries)
                d_v[h] += nt(probs.astype(BF16), up[i, h])
                d_q[i, h] += nn(turned[h], d_scores)
            return carry

        lax.fori_loop(info_ref[1, j], info_ref[2, j], one_block, 0)
        for h in range(own):
            at = (own + h) * LANES
            d_ref[j, :, at : at + LANES] = (d_k[h] * factor).astype(BF16)
            at = (2 * own + h) * LANES
            d_ref[j, :, at : at + LANES] = d_v[h].astype(BF16)

    each(units, one_unit)

    def turn(i):
        for h in range(own):
            d_ref[i, :, h * LANES : (h + 1) * LANES] = (d_q[i, h].T * factor).astype(BF16)

    each(units, turn)


def early_body(width, info_ref, mod_ref, c_ref, o_ref):
    size = c_ref.shape[1]

    def one(u):
        rows = pl.ds(pl.multiple_of(u * width, width), width)
        gate = mod_ref[pl.ds(info_ref[0, u], 1), 5 * size : 6 * size]
        o_ref[rows, :] = (c_ref[rows, :].astype(F32) * gate).astype(BF16)

    each(c_ref.shape[0] // width, one)


def project_body(width, blocks, ids_ref, info_ref, mod_ref, x_ref, *refs):
    om_refs, refs = refs[:blocks], refs[blocks:]
    w_refs, refs = refs[:-8], refs[-8:]
    attn_ref, x1_ref, h_ref, om_ref, w_ref, om_all, w_all, sems = refs
    f, b, c = ids_ref[0], ids_ref[1], ids_ref[2]
    size = x_ref.shape[1]
    copies = fetch(
        [(om_refs[k], om_all.at[lax.bitwise_xor(b, k)]) for k in range(blocks)]
        + [
            (ref, w_all.at[2 * lax.bitwise_xor(f, i // 2) + lax.bitwise_xor(c, i % 2)])
            for i, ref in enumerate(w_refs)
        ],
        sems,
    )
    for copy in copies:
        copy.wait()
    om = om_all[...].reshape(size, x_ref.shape[0])
    weight = w_all[...].reshape(size, size)
    om_ref[...] = om
    w_ref[...] = weight
    attn_ref[...] = tn(om, weight)

    def one(u):
        rows = pl.ds(pl.multiple_of(u * width, width), width)
        slot = info_ref[0, u]
        gate, shift, scale = [
            mod_ref[pl.ds(slot, 1), i * size : (i + 1) * size] for i in (2, 3, 4)
        ]
        middle = x_ref[rows, :].astype(F32) + gate * attn_ref[rows, :]
        x1_ref[rows, :] = middle
        normed, _ = normal(middle)
        h_ref[rows, :] = (normed * (1.0 + scale) + shift).astype(BF16)

    each(x_ref.shape[0] // width, one)


def ff_body(plan1, plan2, outs1, outs2, step, ids_ref, hot_m, hot_o, chan_ref, *refs):
    n1, n2 = len(plan1), len(plan2)
    rows_refs, refs = refs[:4], refs[4:]
    w1_refs, w2_refs, refs = refs[:n1], refs[n1 : n1 + n2], refs[n1 + n2 :]
    mlp_m, mlp_o, dh_m, dh_o = refs[:4]
    g1_refs, refs = refs[4 : 4 + len(outs1)], refs[4 + len(outs1) :]
    g2_refs, refs = refs[: len(outs2)], refs[len(outs2) :]
    w1, w2, h, dm, turned, hid_s, du_s, mlp, dh, g1, g2, sems = refs
    f = ids_ref[0]
    total = h.shape[0]
    count = total // 2
    f_size, size = w2.shape
    row1, row2 = plan1[-1][2], plan2[-1][2]
    shards = size // row1

    def placed(refs, plan, rows, target):
        for ref, (k, start, _) in zip(refs, plan):
            at = pl.multiple_of(lax.bitwise_xor(f, k) * rows + start, 16)
            yield ref, target.at[pl.ds(at, ref.shape[0])]

    copies = fetch(
        [
            (rows_refs[0], h.at[0:count]),
            (rows_refs[1], h.at[count:total]),
            (rows_refs[2], dm.at[0:count]),
            (rows_refs[3], dm.at[count:total]),
        ]
        + list(placed(w1_refs, plan1, row1, w1))
        + list(placed(w2_refs, plan2, row2, w2)),
        sems,
    )
    for copy in copies:
        copy.wait()
    for at in range(0, total, LANES):
        turned[:, at : at + LANES] = h[at : at + LANES, :].astype(F32).T.astype(BF16)
    mlp[...] = jnp.zeros_like(mlp)
    dh[...] = jnp.zeros_like(dh)
    hots = [hot_m[...].astype(BF16), hot_o[...].astype(BF16)]

    def one(index):
        cols = pl.ds(pl.multiple_of(index * step, step), step)
        up = w1[:, cols]
        down = w2[cols, :]
        chan = chan_ref[:, cols].astype(F32).astype(BF16)
        for side in range(2):
            rows = slice(side * count, (side + 1) * count)
            keep = tn(hots[side], chan)
            pre = nn(h[rows, :], up)
            inner = pre * pre
            bent = jnp.tanh(0.7978845608028654 * (pre + 0.044715 * inner * pre))
            half = 0.5 * (1.0 + bent)
            hid = (pre * half * keep).astype(BF16)
            slope = half + (0.5 * 0.7978845608028654) * pre * (1.0 - bent * bent) * (
                1.0 + (3.0 * 0.044715) * inner
            )
            back = nt(dm[rows, :], down)
            du = (slope * back * keep).astype(BF16)
            hid_s[rows, :] = hid
            du_s[rows, :] = du
            mlp[rows, :] += nn(hid, down)
            dh[rows, :] += nt(du, up)
        g1[:, cols] = nn(turned[...], du_s[...]).astype(BF16)
        g2[cols, :] = tn(hid_s[...], dm[...]).astype(BF16)

    each(f_size // step, one)
    mlp_m[...] = mlp[0:count, :]
    mlp_o[...] = mlp[count:total, :].astype(BF16)
    dh_m[...] = dh[0:count, :]
    dh_o[...] = dh[count:total, :].astype(BF16)

    def leave(refs, outs, rows, source):
        for ref, (ks, start, height) in zip(refs, outs):
            for i, k in enumerate(ks):
                at = pl.multiple_of(lax.bitwise_xor(f, k) * rows + start, 16)
                yield source.at[pl.ds(at, height)], ref.at[i]

    copies = fetch(
        list(leave(g1_refs, outs1, row1, g1)) + list(leave(g2_refs, outs2, row2, g2)), sems
    )
    for copy in copies:
        copy.wait()


def middle_body(
    width, blocks, ids_ref, info_ref, mod_ref, x1_ref, c_ref, dh_ref, got_ref, w_ref, *refs
):
    outs, (dx_ref, da_ref, sum_ref) = refs[:blocks], refs[blocks:]
    b = ids_ref[1]
    count, size = x1_ref.shape
    part = size // blocks
    sum_ref[...] = jnp.zeros_like(sum_ref)

    def one(u):
        rows = pl.ds(pl.multiple_of(u * width, width), width)
        slot = info_ref[0, u]
        gate = mod_ref[pl.ds(slot, 1), 2 * size : 3 * size]
        scale = mod_ref[pl.ds(slot, 1), 4 * size : 5 * size]
        normed, spread = normal(x1_ref[rows, :])
        grad = dh_ref[rows, :] + got_ref[rows, :].astype(F32)
        sum_ref[pl.ds(slot, 1), 0:size] += jnp.sum(grad, axis=0, keepdims=True)
        sum_ref[pl.ds(slot, 1), size : 2 * size] += jnp.sum(grad * normed, axis=0, keepdims=True)
        dx = c_ref[rows, :].astype(F32) + normal_back(grad * (1.0 + scale), normed, spread)
        dx_ref[rows, :] = dx
        da_ref[rows, :] = (dx * gate).astype(BF16)

    each(count // width, one)
    for k in range(blocks):
        outs[k][...] = nt(w_ref[lax.bitwise_xor(b, k)], da_ref[...]).astype(BF16)


def result_body(
    width, shards, ids_ref, info_ref, mod_ref, x1_ref, c_ref, mlp_ref, got_ref, attn_ref, dx_ref,
    da_ref, om_ref, perm_ref, r_ref, sum_ref, mine_ref, other_ref, held, grad,
):
    f, c = ids_ref[0], ids_ref[2]
    count, size = x1_ref.shape
    sum_ref[...] = jnp.zeros_like(sum_ref)

    def one(u):
        rows = pl.ds(pl.multiple_of(u * width, width), width)
        slot = info_ref[0, u]
        gate = mod_ref[pl.ds(slot, 1), 5 * size : 6 * size]
        mlp = mlp_ref[rows, :] + got_ref[rows, :].astype(F32)
        held[rows, :] = (x1_ref[rows, :] + gate * mlp).astype(BF16)
        sum_ref[pl.ds(slot, 1), 0:size] += jnp.sum(
            dx_ref[rows, :] * attn_ref[rows, :], axis=0, keepdims=True
        )
        sum_ref[pl.ds(slot, 1), size : 2 * size] += jnp.sum(
            c_ref[rows, :].astype(F32) * mlp, axis=0, keepdims=True
        )

    each(count // width, one)
    r_ref[...] = tn(perm_ref[...], held[...]).astype(BF16)
    grad[...] = nn(om_ref[...], da_ref[...]).astype(BF16).reshape(grad.shape)
    for k in range(shards):
        base = 2 * lax.bitwise_xor(f, k)
        mine_ref[k] = grad[base + c]
        other_ref[k] = grad[base + 1 - c]


def qkv_back_body(plan, outs, blocks, ids_ref, h_ref, d_ref, w_ref, *refs):
    n = len(outs)
    dh_ref, g_refs, (acc, low, sems) = refs[0], refs[1 : 1 + n], refs[1 + n :]
    f = ids_ref[0]
    step = pl.program_id(0)
    per, _, size = h_ref.shape
    rows = plan[-1][2]
    width = BLOCK // blocks
    for i in range(per):
        piece = nt(d_ref[i], w_ref[...]).astype(BF16)
        dh_ref[:, i] = piece.reshape(blocks, width, size)
    part = tn(h_ref[...].reshape(per * BLOCK, size), d_ref[...].reshape(per * BLOCK, -1))

    @pl.when(step == 0)
    def _():
        acc[...] = part

    @pl.when(step > 0)
    def _():
        acc[...] += part

    @pl.when(step == pl.num_programs(0) - 1)
    def _():
        low[...] = acc[...].astype(BF16)
        todo = []
        for ref, (ks, start, height) in zip(g_refs, outs):
            for i, k in enumerate(ks):
                at = pl.multiple_of(lax.bitwise_xor(f, k) * rows + start, 16)
                todo.append((low.at[pl.ds(at, height)], ref.at[i]))
        for copy in fetch(todo, sems):
            copy.wait()


def last_body(width, info_ref, mod_ref, x_ref, dx_ref, dh_ref, perm_ref, o_ref, sum_ref, held):
    count, size = x_ref.shape
    sum_ref[...] = jnp.zeros_like(sum_ref)

    def one(u):
        rows = pl.ds(pl.multiple_of(u * width, width), width)
        slot = info_ref[0, u]
        scale = mod_ref[pl.ds(slot, 1), size : 2 * size]
        normed, spread = normal(x_ref[rows, :].astype(F32))
        grad = dh_ref[rows, :].astype(F32)
        sum_ref[pl.ds(slot, 1), 0:size] += jnp.sum(grad, axis=0, keepdims=True)
        sum_ref[pl.ds(slot, 1), size : 2 * size] += jnp.sum(grad * normed, axis=0, keepdims=True)
        dx = dx_ref[rows, :] + normal_back(grad * (1.0 + scale), normed, spread)
        held[rows, :] = dx.astype(BF16)

    each(count // width, one)
    o_ref[...] = tn(perm_ref[...], held[...]).astype(BF16)


def gather_plan(shards, rows):
    if shards == 4:
        half = rows // 2
        return [(0, 0, rows), (1, 0, rows), (2, 0, rows), (3, 0, rows), (3, half, rows)]
    return [(k, 0, rows) for k in range(shards)]


def gather_rows(own, shards):
    if shards == 4:
        half = own.shape[0] // 2
        one, two = swap(own, "fsdp", 1), swap(own, "fsdp", 2)
        top, low = swap(one[:half], "fsdp", 2), swap(two[half:], "fsdp", 1)
        return [own, one, two, top, low]
    return [own] + [swap(own, "fsdp", k) for k in range(1, shards)]


def reduce_plan(shards, rows):
    if shards == 4:
        half = rows // 2
        return [
            ((0, 2), 0, half),
            ((1, 3), 0, half),
            ((0, 1), half, half),
            ((2, 3), half, half),
        ]
    return [(tuple(range(shards)), 0, rows)]


def add(left, right):
    return (left.astype(F32) + right.astype(F32)).astype(BF16)


def reduce_rows(pieces, shards):
    if shards == 4:
        keep_a, send_a, keep_b, send_b = pieces
        sum_a = add(keep_a, swap(send_a, "fsdp", 1))
        sum_b = add(keep_b, swap(send_b, "fsdp", 2))
        return (
            add(sum_a[0], swap(sum_a[1], "fsdp", 2)),
            add(sum_b[0], swap(sum_b[1], "fsdp", 1)),
        )
    (pieces,) = pieces
    total = pieces[0]
    for k in range(1, shards):
        total = add(total, swap(pieces[k], "fsdp", k))
    half = total.shape[0] // 2
    return total[:half], total[half:]


def sum_chips(pair, chips):
    one, two = pair
    if chips == 4:
        even = (lax.axis_index("blk") // 2) % 2 == 0
        send, keep = jnp.where(even, two, one), jnp.where(even, one, two)
        part = add(keep, swap(send, "blk", 2))
        part = add(part, swap(part, "blk", 4))
        other = swap(part, "blk", 2)
        return jnp.where(even, part, other), jnp.where(even, other, part)
    groups = [[2 * i + core for i in range(chips)] for core in range(2)]
    both = lax.psum(jnp.concatenate([one, two]), "blk", axis_index_groups=groups)
    return both[: one.shape[0]], both[one.shape[0] :]


def line_gather(own, chips):
    out = []
    behind = ahead = own
    for s in range(1, chips):
        first, last = 2 * (s - 1), 2 * (chips - 1)
        behind = lax.ppermute(behind, "blk", [(i, i + 2) for i in range(first, last)])
        ahead = lax.ppermute(ahead, "blk", [(i + 2, i) for i in range(last - first)])
        out += [behind, swap(behind, "blk", 1), ahead, swap(ahead, "blk", 1)]
    return out


def both_cores(array):
    other = swap(array, "blk", 1)
    first = lax.axis_index("blk") % 2 == 0
    return jnp.where(first, array, other), jnp.where(first, other, array)


def on_device(
    tokens,
    timesteps,
    segment_ids,
    head_mask,
    chan_mask,
    token_mask,
    w_temb,
    w_ada,
    w_qkv,
    w_out,
    w_fc1,
    w_fc2,
    cotangent,
):
    count, size = tokens.shape
    slots, heads = head_mask.shape[1:]
    head_size = size // heads
    shards, blocks = lax.axis_size("fsdp"), lax.axis_size("blk")
    chips = blocks // 2
    f, b = lax.axis_index("fsdp"), lax.axis_index("blk")
    c = b % 2
    width = BLOCK // blocks
    units = count // width
    own = heads // blocks
    wide = 3 * own * LANES
    hidden = w_fc1.shape[1]
    half = hidden // 2
    ids = jnp.stack([f, b, c]).astype(I32)

    items = lax.dynamic_slice_in_dim(segment_ids, b * count, count, axis=1)
    x_s, c_s, hot, info, perm = run(
        "sort_tokens",
        functools.partial(sort_body, width),
        [(VMEM, items), (VMEM, token_mask[None, :]), (VMEM, tokens), (VMEM, cotangent)],
        [
            (VMEM, shape((count, size))),
            (VMEM, shape((count, size))),
            (VMEM, shape((slots, count), F32)),
            (VMEM, shape((8, LANES), I32)),
            (VMEM, shape((count, count))),
        ],
    )

    rows = w_temb.shape[0]
    entries = rows * shards
    index = jnp.concatenate([(f ^ k) * rows + lax.iota(I32, rows) for k in range(shards)])
    ladder = jnp.exp(
        -math.log(10000.0) * (index % (entries // 2)).astype(F32) / (entries // 2)
    )
    steps = jnp.concatenate(
        [timesteps[0]] + [swap(timesteps, "fsdp", k)[0] for k in range(1, shards)]
    )
    angles = steps.astype(F32)[:, None] * ladder[None, :]
    spectrum = jnp.where(index[None, :] < entries // 2, jnp.cos(angles), jnp.sin(angles))
    spectrum = spectrum.astype(BF16)
    temb = jnp.concatenate([w_temb] + [swap(w_temb, "fsdp", k) for k in range(1, shards)])
    ada_rows = w_ada.shape[0]
    condition = lax.dynamic_slice_in_dim(nn(spectrum, temb), f * ada_rows, ada_rows, axis=1)
    lifted, silu_pull = jax.vjp(lambda v: v / (1.0 + jnp.exp(-v)), condition)
    lifted = lifted.astype(BF16)
    partial = nn(lifted, w_ada).reshape(shards, slots, -1)
    mod = partial[0]
    for k in range(1, shards):
        mod = mod + swap(partial[k], "fsdp", k)

    x_parts = [x_s, swap(x_s, "blk", 1)] + line_gather(x_s, chips)

    (w_heads,) = run(
        "pick_heads",
        functools.partial(pick_heads_body, own, head_size),
        [(SMEM, ids), (VMEM, w_qkv)],
        [(VMEM, shape((w_qkv.shape[0], wide)))],
    )
    (w_fc1_half,) = run(
        "pick_half",
        functools.partial(pick_half_body, shards),
        [(SMEM, ids), (VMEM, w_fc1)],
        [(VMEM, shape((w_fc1.shape[0], half)))],
    )
    plan_qkv = gather_plan(shards, w_heads.shape[0])
    qkv_parts = gather_rows(w_heads, shards)
    out_rows = w_out.shape[0] // 2
    w_out_half = lax.dynamic_slice_in_dim(w_out, c * out_rows, out_rows)
    w_out_other = lax.dynamic_slice_in_dim(w_out, (1 - c) * out_rows, out_rows)
    w_out_half = after(w_out_half, qkv_parts[1])
    got = [swap(w_out_half, "fsdp", k) for k in range(1, shards)]
    out_parts = [w_out_half, w_out_other]
    for piece in got:
        out_parts += [piece, swap(piece, "blk", 1)]
    plan1 = gather_plan(shards, w_fc1_half.shape[0])
    fc1_parts = gather_rows(after(w_fc1_half, got[0], got[1]), shards)
    fc2_rows = w_fc2.shape[0] // 2
    w_fc2_half = lax.dynamic_slice_in_dim(w_fc2, c * fc2_rows, fc2_rows)
    plan2 = gather_plan(shards, fc2_rows)
    fc2_parts = gather_rows(after(w_fc2_half, fc1_parts[1], fc1_parts[2]), shards)

    (dm,) = run(
        "grad_mlp",
        functools.partial(early_body, width),
        [(SMEM, info), (VMEM, mod), (VMEM, c_s)],
        [(VMEM, shape((count, size)))],
    )
    dm_other = swap(dm, "blk", 1)
    hot_other = swap(hot, "blk", 1)

    whole = pl.BlockSpec(memory_space=pltpu.VMEM)
    n_copies = len(x_parts) + len(plan_qkv)
    normed, qkv = run(
        "norm_qkv",
        functools.partial(first_body, chips, plan_qkv),
        [(SMEM, ids), (SMEM, info), (whole, mod)]
        + [(ANY, part) for part in x_parts]
        + [(ANY, part) for part in qkv_parts],
        [
            (pl.BlockSpec((1, BLOCK, size), lambda u: (u, 0, 0)), shape((units, BLOCK, size))),
            (pl.BlockSpec((1, BLOCK, wide), lambda u: (u, 0, 0)), shape((units, BLOCK, wide))),
        ],
        [
            pltpu.VMEM((blocks, count, size), BF16),
            pltpu.VMEM((size, wide), BF16),
            pltpu.SemaphoreType.DMA((n_copies,)),
        ],
        flops=2 * units * BLOCK * size * wide,
        grid=(units,),
    )

    mask = head_mask[0]
    narrow = own * head_size
    outs = run(
        "attend",
        functools.partial(attend_body, own, head_size, blocks),
        [(SMEM, ids), (SMEM, info), (SMEM, mask), (VMEM, qkv)],
        [
            (VMEM, shape((units, narrow, BLOCK))),
            (VMEM, shape((units, 8, BLOCK), F32)),
        ]
        + [(VMEM, shape((narrow, count)))] * blocks,
        [pltpu.VMEM((units, narrow, BLOCK), F32)],
        flops=2 * units * units * BLOCK * BLOCK * wide // 3,
    )
    held, lse, pieces = outs[0], outs[1], outs[2:]
    om_parts = [pieces[0]] + [swap(pieces[k], "blk", k) for k in range(1, blocks)]

    attn, x1, h2, om, w_out_all = run(
        "project",
        functools.partial(project_body, width, blocks),
        [(SMEM, ids), (SMEM, info), (VMEM, mod), (VMEM, x_s)]
        + [(ANY, part) for part in om_parts]
        + [(ANY, part) for part in out_parts],
        [
            (VMEM, shape((count, size), F32)),
            (VMEM, shape((count, size), F32)),
            (VMEM, shape((count, size))),
            (VMEM, shape((size, count))),
            (VMEM, shape((size, size))),
        ],
        [
            pltpu.VMEM((blocks, narrow, count), BF16),
            pltpu.VMEM((2 * shards, out_rows, size), BF16),
            pltpu.SemaphoreType.DMA((blocks + 2 * shards,)),
        ],
        flops=2 * count * size * size,
    )
    h2_other = swap(h2, "blk", 1)

    outs1 = reduce_plan(shards, w_fc1_half.shape[0])
    outs2 = reduce_plan(shards, fc2_rows)
    chan = chan_mask[0].reshape(slots, shards, 2, half // shards)
    chan = lax.dynamic_slice_in_dim(chan, c, 1, axis=2).reshape(slots, half)
    n_sems = max(
        4 + len(plan1) + len(plan2),
        sum(len(ks) for ks, _, _ in outs1) + sum(len(ks) for ks, _, _ in outs2),
    )
    outs = run(
        "feed_forward",
        functools.partial(ff_body, plan1, plan2, outs1, outs2, 256),
        [(SMEM, ids), (VMEM, hot), (VMEM, hot_other), (VMEM, chan)]
        + [(ANY, a) for a in (h2, h2_other, dm, dm_other)]
        + [(ANY, a) for a in fc1_parts]
        + [(ANY, a) for a in fc2_parts],
        [
            (VMEM, shape((count, size), F32)),
            (VMEM, shape((count, size))),
            (VMEM, shape((count, size), F32)),
            (VMEM, shape((count, size))),
        ]
        + [(ANY, shape((len(ks), height, half))) for ks, _, height in outs1]
        + [(ANY, shape((len(ks), height, size))) for ks, _, height in outs2],
        [
            pltpu.VMEM((size, half), BF16),
            pltpu.VMEM((half, size), BF16),
            pltpu.VMEM((2 * count, size), BF16),
            pltpu.VMEM((2 * count, size), BF16),
            pltpu.VMEM((size, 2 * count), BF16),
            pltpu.VMEM((2 * count, 256), BF16),
            pltpu.VMEM((2 * count, 256), BF16),
            pltpu.VMEM((2 * count, size), F32),
            pltpu.VMEM((2 * count, size), F32),
            pltpu.VMEM((size, half), BF16),
            pltpu.VMEM((half, size), BF16),
            pltpu.SemaphoreType.DMA((n_sems,)),
        ],
        flops=6 * 2 * 2 * count * size * half,
        vmem=60,
    )
    mlp, mlp_send, dh2, dh2_send = outs[:4]
    g1_parts, g2_parts = outs[4 : 4 + len(outs1)], outs[4 + len(outs1) :]
    dh2_got = swap(dh2_send, "blk", 1)
    mlp_got = swap(mlp_send, "blk", 1)

    outs = run(
        "middle_back",
        functools.partial(middle_body, width, blocks),
        [(SMEM, ids), (SMEM, info), (VMEM, mod), (VMEM, x1), (VMEM, c_s), (VMEM, dh2)]
        + [(VMEM, dh2_got), (VMEM, w_out_all.reshape(blocks, narrow, size))],
        [(VMEM, shape((narrow, count)))] * blocks
        + [
            (VMEM, shape((count, size), F32)),
            (VMEM, shape((count, size))),
            (VMEM, shape((slots, 2 * size), F32)),
        ],
        flops=2 * count * size * size,
    )
    pieces, (dx1, d_attn, sums_two) = outs[:blocks], outs[blocks:]
    up_parts = [pieces[0]] + [swap(pieces[k], "blk", k) for k in range(1, blocks)]

    result, sums_gate, g_out, g_out_send = run(
        "result",
        functools.partial(result_body, width, shards),
        [(SMEM, ids), (SMEM, info)]
        + [(VMEM, a) for a in (mod, x1, c_s, mlp, mlp_got, attn, dx1, d_attn, om, perm)],
        [
            (VMEM, shape((count, size))),
            (VMEM, shape((slots, 2 * size), F32)),
            (VMEM, shape((shards, out_rows, size))),
            (VMEM, shape((shards, out_rows, size))),
        ],
        [pltpu.VMEM((count, size), BF16), pltpu.VMEM((2 * shards, out_rows, size), BF16)],
        flops=2 * count * size * size,
    )
    g_out = add(g_out, swap(g_out_send, "blk", 1))

    (d_qkv,) = run(
        "attend_back",
        functools.partial(attend_back_body, own, head_size, blocks),
        [(SMEM, ids), (SMEM, info), (SMEM, mask)]
        + [(VMEM, a) for a in (qkv, held, lse)]
        + [(VMEM, a) for a in up_parts],
        [(VMEM, shape((units, BLOCK, wide)))],
        [
            pltpu.VMEM((blocks, narrow, count), BF16),
            pltpu.VMEM((units, own, LANES, BLOCK), BF16),
            pltpu.VMEM((units, 8, BLOCK), F32),
            pltpu.VMEM((units, own, LANES, BLOCK), F32),
            pltpu.VMEM((own, BLOCK, LANES), F32),
            pltpu.VMEM((own, BLOCK, LANES), F32),
        ],
        flops=5 * units * units * BLOCK * BLOCK * wide // 3,
    )
    w_heads_all = jnp.zeros((size, wide), BF16)
    for part, (k, start, rows_in) in zip(qkv_parts, plan_qkv):
        w_heads_all = lax.dynamic_update_slice_in_dim(
            w_heads_all, part, (f ^ k) * rows_in + start, axis=0
        )
    per = 4
    outs_qkv = reduce_plan(shards, w_heads.shape[0])
    outs = run(
        "qkv_back",
        functools.partial(qkv_back_body, plan_qkv, outs_qkv, blocks),
        [
            (SMEM, ids),
            (pl.BlockSpec((per, BLOCK, size), lambda i: (i, 0, 0)), normed),
            (pl.BlockSpec((per, BLOCK, wide), lambda i: (i, 0, 0)), d_qkv),
            (whole, w_heads_all),
        ],
        [
            (
                pl.BlockSpec((blocks, per, width, size), lambda i: (0, i, 0, 0)),
                shape((blocks, units, width, size)),
            )
        ]
        + [(ANY, shape((len(ks), height, wide))) for ks, _, height in outs_qkv],
        [
            pltpu.VMEM((size, wide), F32),
            pltpu.VMEM((size, wide), BF16),
            pltpu.SemaphoreType.DMA((2 * shards,)),
        ],
        flops=4 * units * BLOCK * size * wide,
        grid=(units // per,),
    )
    d_normed, gq_parts = outs[0], outs[1:]
    d_normed = lax.psum_scatter(
        d_normed.reshape(blocks * count, size), "blk", scatter_dimension=0, tiled=True
    )
    grad_tokens, sums_one = run(
        "first_back",
        functools.partial(last_body, width),
        [(SMEM, info)] + [(VMEM, a) for a in (mod, x_s, dx1, d_normed, perm)],
        [(VMEM, shape((count, size))), (VMEM, shape((slots, 2 * size), F32))],
        [pltpu.VMEM((count, size), BF16)],
    )

    def over_stream(sums):
        low = sums.astype(BF16)
        total = low.astype(F32)
        for k in (1, 2, 4, 8, 16):
            if k < blocks:
                total = total + swap(total, "blk", k)
        low = total.astype(BF16)
        return jnp.concatenate([low] + [swap(low, "fsdp", k) for k in range(1, shards)])

    gate_all, two_all, one_all = over_stream(sums_gate), over_stream(sums_two), over_stream(sums_one)
    d_mod = jnp.concatenate(
        [one_all, gate_all[:, :size], two_all, gate_all[:, size:]], axis=1
    )
    grad_ada = tn(lifted, d_mod)
    (d_condition,) = silu_pull(nt(d_mod, w_ada))
    d_all = jnp.zeros((shards * slots, size), F32)
    for k in range(shards):
        piece = d_condition if k == 0 else swap(d_condition, "fsdp", k)
        piece = piece.reshape(shards, slots, ada_rows)
        piece = jnp.concatenate([piece[r ^ k] for r in range(shards)])
        d_all = lax.dynamic_update_slice_in_dim(d_all, piece, (f ^ k) * ada_rows, axis=1)
    grad_temb = lax.dot_general(
        spectrum[:, :rows].astype(F32), d_all, (((0,), (0,)), ((), ())), precision=HIGH
    )

    g1_one, g1_two = sum_chips(reduce_rows(g1_parts, shards), chips)
    g2_one, g2_two = sum_chips(reduce_rows(g2_parts, shards), chips)
    if shards == 4:
        cut = out_rows // 2
        pieces = [
            jnp.stack([g_out[0, :cut], g_out[2, :cut]]),
            jnp.stack([g_out[1, :cut], g_out[3, :cut]]),
            g_out[0:2, cut:],
            g_out[2:4, cut:],
        ]
    else:
        pieces = [g_out]
    o_one, o_two = sum_chips(reduce_rows(pieces, shards), chips)
    first, second = both_cores(jnp.concatenate([o_one, o_two]))
    grad_out = jnp.concatenate([first, second]).astype(F32)
    first, second = both_cores(jnp.concatenate([g2_one, g2_two]))
    grad_fc2 = jnp.concatenate([first, second]).astype(F32)
    first, second = both_cores(jnp.concatenate([g1_one, g1_two]))
    part = half // shards
    grad_fc1 = jnp.concatenate(
        [side[:, i * part : (i + 1) * part] for i in range(shards) for side in (first, second)],
        axis=1,
    ).astype(F32)
    gq = lax.all_gather(jnp.concatenate(reduce_rows(gq_parts, shards)), "blk", axis=0)
    gq = gq.reshape(blocks, -1, 3, own, LANES)[..., :head_size]
    grad_qkv = jnp.transpose(gq, (1, 2, 0, 3, 4)).reshape(w_qkv.shape).astype(F32)
    return (
        result,
        grad_tokens,
        grad_temb,
        grad_ada,
        grad_qkv,
        grad_out,
        grad_fc1,
        grad_fc2,
    )


def solution(mesh):
    placed = (
        P(("fsdp", "blk"), None),
        P("fsdp", None),
        P("fsdp", None),
        P("fsdp", None, None),
        P("fsdp", None, None),
        P(("fsdp", "blk")),
        P("fsdp", None),
        P("fsdp", None),
        P("fsdp", None),
        P("fsdp", None),
        P("fsdp", None),
        P("fsdp", None),
        P(("fsdp", "blk"), None),
    )
    return jax.shard_map(
        on_device,
        mesh=mesh,
        in_specs=placed,
        out_specs=(
            P(("fsdp", "blk"), None),
            P(("fsdp", "blk"), None),
            P("fsdp", None),
            P("fsdp", None),
            P("fsdp", None),
            P("fsdp", None),
            P("fsdp", None),
            P("fsdp", None),
        ),
        check_vma=False,
    )
```

time: 2060 us -> 776 us (0.38)
  waiting for transfers between devices: 1310 us -> 300 us
  matrix products: 356 us -> 12.6 us
  Pallas kernels: 0 us -> 202 us
  starting transfers between devices: 33.5 us -> 144 us
  other arithmetic: 134 us -> 29.1 us
  local copies, waits for them, and re-layouts: 175 us -> 72.3 us
    reduce_scatter x6 -> x1, waiting for transfers between devices: 479 us -> 0.01 us  [on_device(): lax.psum_scatter(d_normed.reshape(blocks * count, size), 'blk', scatter_d...]
    dot_general x77 -> x5, matrix products: 356 us -> 12.6 us  [the longest x1 5.61 us: tn(): lax.dot_general(left, right, (((0,), (0,)), ((), ())), preferred_element_...]
    psum x2 -> x0, waiting for transfers between devices: 314 us -> none  [the longest x1 250 us: on_device(): lax.psum(grad_temb.astype(jnp.bfloat16), 'blk').astype(jnp.float32)]
    all_gather x7 -> x1, waiting for transfers between devices: 314 us -> 0.01 us  [on_device(): lax.all_gather(jnp.concatenate(reduce_rows(gq_parts, shards)), 'blk', axi...]
    pallas_call x0 -> x13, Pallas kernels: none -> 202 us  [run(): pl.pallas_call(body, out_shape=[o for _, o in outs], in_specs=[s for s, _...]
    ppermute x32 -> x109, starting transfers between devices: 32.2 us -> 144 us  [the longest x103 132 us: swap(): return lax.ppermute(array, axis, [(i, i ^ by) for i in range(size)])]
    ppermute x32 -> x109, waiting for transfers between devices: 195 us -> 300 us  [the longest x103 286 us: swap(): return lax.ppermute(array, axis, [(i, i ^ by) for i in range(size)])]
    convert_element_type x44 -> x29, other arithmetic: 72.7 us -> 18.4 us  [the longest x17 5.89 us: add(): return (left.astype(F32) + right.astype(F32)).astype(BF16)]
  transfers between devices with their start and end apart: 47 -> 111, of which waited for: 38 -> 42; matrix products, arithmetic and copies ran while one was open for 20% -> 11% of each run, Pallas kernels for 0% -> 12%
where the time goes in v1:
time: 776 us
  waiting for transfers between devices  300 us (39%)
  Pallas kernels  202 us (26%)
  starting transfers between devices  144 us (19%)
  local copies, waits for them, and re-layouts  72.3 us (9%)
  other arithmetic  29.1 us (4%)
  between operations  15.6 us (2%)
  matrix products  12.6 us (2%)
    ppermute x103, waiting for transfers between devices, swap(): return lax.ppermute(array, axis, [(i, i ^ by) for i in range(size)])  286 us
    pallas_call x13, Pallas kernels, run(): pl.pallas_call(body, out_shape=[o for _, o in outs], in_specs=[s for s, _...  202 us
    ppermute x103, starting transfers between devices, swap(): return lax.ppermute(array, axis, [(i, i ^ by) for i in range(size)])  132 us
    unnamed x184, local copies, waits for them, and re-layouts  36.1 us
  transfers between devices with their start and end apart: 111, of which 42 were waited for; matrix products, arithmetic and copies ran while one was open for 11% of the time, Pallas kernels for 12%

profile of v1, /device:TPU:1, one launch (start us, length us, event | category | flops | bytes accessed | tf_op | source)
XLA Modules:
  0.0 775.5 jit_solution(3410739619651914715)
XLA Ops:
  34.5 7.8 %collective-permute-done.6 = f32[8,6912]{1,0:T(8,128)} collective-permute-done((f32[8,6912]{1,0:T(8,128)}, f32[8,6912]{1,0:T(8,128)}, u32[]{:S(2)}, u32[]{:S(2)}) %collective-permute-start.6) | collective-permute-done | bytes 221216 | tf_op jit(solution)/shard_map/ppermute | solution.py:47
  77.6 8.3 %collective-permute-done.16.refs_8_ = bf16[384,1152]{1,0:T(8,128)(2,1)} collective-permute-done((bf16[384,1152]{1,0:T(8,128)(2,1)}, bf16[384,1152]{1,0:T(8,128)(2,1)}, u32[]{:S(2)}, u32[]{:S(2)}) %collective-permute-start.16) | collective-permute-done | bytes 884768 | tf_op jit(solution)/shard_map/ppermute | solution.py:648
  88.3 9.4 %collective-permute-done.42.refs_5_ = bf16[288,2304]{1,0:T(8,128)(2,1)} collective-permute-done((bf16[288,2304]{1,0:T(8,128)(2,1)}, bf16[288,2304]{1,0:T(8,128)(2,1)}, u32[]{:S(2)}, u32[]{:S(2)}) %collective-permute-start.42) | collective-permute-done | bytes 1327136 | tf_op jit(solution)/shard_map/ppermute | solution.py:47
  116.0 16.5 %norm_qkv.1 = (bf16[12,256,1152]{2,1,0:T(8,128)(2,1)}, bf16[12,256,768]{2,1,0:T(8,128)(2,1)}) custom-call(s32[3]{0:T(128)S(1)} %pad_add_fusion.1.ids_ref, s32[8,128]{1,0:T(8,128)S(1)} %get-tuple-element.67.info_ref, f32[8,6912]{1,0:T(8,128)S(1)} %fusion.17.mod_ref, bf16[384,1152]{1,0:T(8,128)(2,1)} %get-tuple-element.68.refs_0_.x_ref, ...), custom_call_target="tpu_custom_call" | custom-call | flops 5435817984 | bytes 26177548 | tf_op jit(solution)/shard_map/norm_qkv/pallas_call | solution.py:32
  134.0 33.0 %attend.1 = (bf16[12,144,256]{2,1,0:T(8,128)(2,1)S(1)}, f32[12,8,256]{2,1,0:T(8,128)S(1)}, bf16[144,384]{1,0:T(8,128)(2,1)S(1)}, bf16[144,384]{1,0:T(8,128)(2,1)...) custom-call(s32[3]{0:T(128)S(1)} %pad_add_fusion.1.ids_ref, ...), custom_call_target="tpu_custom_call" | custom-call | flops 4831838208 | bytes 6590988 | tf_op jit(solution)/shard_map/attend/pallas_call | solution.py:32
  177.5 6.6 collective-permute-done.29.refs_4_
  193.4 22.3 %project.1 = (f32[384,1152]{1,0:T(8,128)}, f32[384,1152]{1,0:T(8,128)}, bf16[384,1152]{1,0:T(8,128)(2,1)}, bf16[1152,384]{1,0:T(8,128)(2,1)S(1)}, bf16[1152,1152]{1,0:T(8,128)(2,1)}) custom-call(s32[3]{0:T(128)S(1)} %pad_add_fusion.1.ids_ref, s32[8,128]{1,0:T(8,128)S(1)} %get-tuple-element.67.info_ref, f32[8,6912]{1,0:T(8,128)S(1)} %fusion.17.mod_ref, ...), custom_call_target="tpu_custom_call" | custom-call | flops 1019215872 | bytes 12611596 | tf_op jit(solution)/shard_map/project/pallas_call | solution.py:32
  219.9 7.6 collective-permute-start.45
  234.8 7.4 collective-permute-done.45.refs_8_
  242.2 6.8 collective-permute-done.48.refs_12_
  249.0 7.3 collective-permute-done.49.refs_13_
  257.2 46.6 %feed_forward.1 = (f32[384,1152]{1,0:T(8,128)}, bf16[384,1152]{1,0:T(8,128)(2,1)}, f32[384,1152]{1,0:T(8,128)}, bf16[384,1152]{1,0:T(8,128)(2,1)}, bf16[2,144,23...) custom-call(s32[3]{0:T(128)} %copy-done.35, ...), custom_call_target="tpu_custom_call" | custom-call | flops 24461180928 | bytes 30179340 | tf_op jit(solution)/shard_map/feed_forward/pallas_call | solution.py:32
  308.5 9.1 %middle_back.1 = (bf16[144,384]{1,0:T(8,128)(2,1)S(1)}, bf16[144,384]{1,0:T(8,128)(2,1)S(1)}, bf16[144,384]{1,0:T(8,128)(2,1)S(1)}, bf16[144,384]{1,0:T(8,128)(2...) custom-call(s32[3]{0:T(128)S(1)} %copy-done.36, ...), custom_call_target="tpu_custom_call" | custom-call | flops 1019215872 | bytes 11800588 | tf_op jit(solution)/shard_map/middle_back/pallas_call | solution.py:32
  330.2 10.2 %collective-permute-done.56.refs_5_ = bf16[144,384]{1,0:T(8,128)(2,1)S(1)} collective-permute-done((bf16[144,384]{1,0:T(8,128)(2,1)S(1)}, bf16[144,384]{1,0:T(8,128)(2,1)S(1)}, u32[]{:S(2)}, u32[]{:S(2)}) %collective-permute-start.56) | collective-permute-done | bytes 110624 | tf_op jit(solution)/shard_map/ppermute | solution.py:47
  340.4 33.4 %attend_back.1.d_ref = bf16[12,256,768]{2,1,0:T(8,128)(2,1)} custom-call(s32[3]{0:T(128)S(1)} %copy-done.36, s32[8,128]{1,0:T(8,128)S(1)} %get-tuple-element.67.info_ref, s32[8,16]{1,0:T(8,128)S(1)} %bitcast.98, bf16[12,256,768]{2,1,0:T(8,128)(2,1)} %get-tuple-element.69.qkv_ref, bf16[12,144,256]{2,1,0:T(8,128)(2,1)S(1)} %copy-done.47, ...), custom_call_target="tpu_custom_call" | custom-call | flops 12079595520 | bytes 11309580 | tf_op jit(solution)/shard_map/attend_back/pallas_call | solution.py:32
  373.9 19.4 %qkv_back.1 = (bf16[8,12,32,1152]{3,2,1,0:T(8,128)(2,1)}, bf16[2,144,768]{2,1,0:T(8,128)(2,1)S(1)}, bf16[2,144,768]{2,1,0:T(8,128)(2,1)S(1)}, bf16[2,144,768]{2,1,0:T(8,128)(2,1)S(1)}, bf16[2,144,768]{2,1,0:T(8,128)(2,1)S(1)}) custom-call(s32[3]{0:T(128)S(1)} %copy-done.36, bf16[12,256,1152]{2,1,0:T(8,128)(2,1)} %get-tuple-element.96.h_ref, ...), custom_call_target="tpu_custom_call" | custom-call | flops 10871635968 | bytes 22413324 | tf_op jit(solution)/shard_map/qkv_back/pallas_call | solution.py:32
  403.6 8.0 %result.1 = (bf16[384,1152]{1,0:T(8,128)(2,1)}, f32[8,2304]{1,0:T(8,128)S(1)}, bf16[4,144,1152]{2,1,0:T(8,128)(2,1)S(1)}, bf16[4,144,1152]{2,1,0:T(8,128)(2,1)}) custom-call(s32[3]{0:T(128)S(1)} %copy-done.36, s32[8,128]{1,0:T(8,128)S(1)} %get-tuple-element.67.info_ref, f32[8,6912]{1,0:T(8,128)S(1)} %fusion.17.mod_ref, ...), custom_call_target="tpu_custom_call" | custom-call | flops 1019215872 | bytes 14749708 | tf_op jit(solution)/shard_map/result/pallas_call | solution.py:32
  446.9 10.5 %collective-permute-done.68 = bf16[8,2304]{1,0:T(8,128)(2,1)S(1)} collective-permute-done((bf16[8,2304]{1,0:T(8,128)(2,1)S(1)}, bf16[8,2304]{1,0:T(8,128)(2,1)S(1)}, u32[]{:S(2)}, u32[]{:S(2)}) %collective-permute-start.68) | collective-permute-done | bytes 36896 | tf_op jit(solution)/shard_map/ppermute | solution.py:47
  467.9 22.8 %collective-permute-done.95 = bf16[2,144,2304]{2,1,0:T(8,128)(2,1)S(1)} collective-permute-done((bf16[2,144,2304]{2,1,0:T(8,128)(2,1)S(1)}, bf16[2,144,2304]{2,1,0:T(8,128)(2,1)S(1)}, u32[]{:S(2)}, u32[]{:S(2)}) %collective-permute-start.95) | collective-permute-done | bytes 1327136 | tf_op jit(solution)/shard_map/ppermute | solution.py:47
  501.5 17.9 %collective-permute-done.81 = bf16[144,768]{1,0:T(8,128)(2,1)S(1)} collective-permute-done((bf16[144,768]{1,0:T(8,128)(2,1)S(1)}, bf16[144,768]{1,0:T(8,128)(2,1)S(1)}, u32[]{:S(2)}, u32[]{:S(2)}) %collective-permute-start.81) | collective-permute-done | bytes 221216 | tf_op jit(solution)/shard_map/ppermute | solution.py:47
  534.8 10.0 %collective-permute-done.85 = bf16[2,72,1152]{2,1,0:T(8,128)(2,1)S(1)} collective-permute-done((bf16[2,72,1152]{2,1,0:T(8,128)(2,1)S(1)}, bf16[2,72,1152]{2,1,0:T(8,128)(2,1)S(1)}, u32[]{:S(2)}, u32[]{:S(2)}) %collective-permute-start.85) | collective-permute-done | bytes 331808 | tf_op jit(solution)/shard_map/ppermute | solution.py:47
  552.1 7.5 collective-permute-done.86
  562.9 21.9 %collective-permute-done.89 = bf16[72,1152]{1,0:T(8,128)(2,1)S(1)} collective-permute-done((bf16[72,1152]{1,0:T(8,128)(2,1)S(1)}, bf16[72,1152]{1,0:T(8,128)(2,1)S(1)}, u32[]{:S(2)}, u32[]{:S(2)}) %collective-permute-start.89) | collective-permute-done | bytes 165920 | tf_op jit(solution)/shard_map/ppermute | solution.py:47
  587.9 12.0 %collective-permute-done.90 = bf16[72,1152]{1,0:T(8,128)(2,1)S(1)} collective-permute-done((bf16[72,1152]{1,0:T(8,128)(2,1)S(1)}, bf16[72,1152]{1,0:T(8,128)(2,1)S(1)}, u32[]{:S(2)}, u32[]{:S(2)}) %collective-permute-start.90) | collective-permute-done | bytes 165920 | tf_op jit(solution)/shard_map/ppermute | solution.py:47
  605.4 11.1 %collective-permute-done.91 = bf16[72,1152]{1,0:T(8,128)(2,1)S(1)} collective-permute-done((bf16[72,1152]{1,0:T(8,128)(2,1)S(1)}, bf16[72,1152]{1,0:T(8,128)(2,1)S(1)}, u32[]{:S(2)}, u32[]{:S(2)}) %collective-permute-start.91) | collective-permute-done | bytes 165920 | tf_op jit(solution)/shard_map/ppermute | solution.py:47
  619.6 28.2 %collective-permute-done.106 = bf16[288,1152]{1,0:T(8,128)(2,1)S(1)} collective-permute-done((bf16[288,1152]{1,0:T(8,128)(2,1)S(1)}, bf16[288,1152]{1,0:T(8,128)(2,1)S(1)}, u32[]{:S(2)}, u32[]{:S(2)}) %collective-permute-start.106) | collective-permute-done | bytes 663584 | tf_op jit(solution)/shard_map/ppermute | solution.py:47
  649.7 12.3 %collective-permute-done.98 = bf16[144,2304]{1,0:T(8,128)(2,1)S(1)} collective-permute-done((bf16[144,2304]{1,0:T(8,128)(2,1)S(1)}, bf16[144,2304]{1,0:T(8,128)(2,1)S(1)}, u32[]{:S(2)}, u32[]{:S(2)}) %collective-permute-start.98) | collective-permute-done | bytes 663584 | tf_op jit(solution)/shard_map/ppermute | solution.py:47
  663.8 13.5 %collective-permute-done.107 = bf16[288,1152]{1,0:T(8,128)(2,1)S(1)} collective-permute-done((bf16[288,1152]{1,0:T(8,128)(2,1)S(1)}, bf16[288,1152]{1,0:T(8,128)(2,1)S(1)}, u32[]{:S(2)}, u32[]{:S(2)}) %collective-permute-start.107) | collective-permute-done | bytes 663584 | tf_op jit(solution)/shard_map/ppermute | solution.py:47
  682.3 9.2 %collective-permute-done.99 = bf16[144,2304]{1,0:T(8,128)(2,1)S(1)} collective-permute-done((bf16[144,2304]{1,0:T(8,128)(2,1)S(1)}, bf16[144,2304]{1,0:T(8,128)(2,1)S(1)}, u32[]{:S(2)}, u32[]{:S(2)}) %collective-permute-start.99) | collective-permute-done | bytes 663584 | tf_op jit(solution)/shard_map/ppermute | solution.py:47
  698.8 6.7 first_back.1
  728.8 7.8 %reshape.220 = bf16[8,288,3,2,128]{4,3,2,1,0:T(2,128)(2,1)} reshape(bf16[2304,768]{1,0:T(8,128)(2,1)} %all-gather.3.cloned.1.call-done) | data formatting | bytes 7077888 | tf_op jit(solution)/shard_map/reshape | solution.py:1011
  736.7 7.2 copy.27
  (497 shorter events, 301.7 us)
Async XLA Ops:
  7.2 690.4 %reduce-scatter.2.cloned.1.call-start = ((), (), s32[]{:S(2)}) async-start(), calls=%async_computation.1 | async-start | bytes 7962624 | tf_op jit(solution)/shard_map/reduce_scatter | solution.py:951
  21.9 36.6 %collective-permute-start.10 = (bf16[384,1152]{1,0:T(8,128)(2,1)}, bf16[384,1152]{1,0:T(8,128)(2,1)}, u32[]{:S(2)}, u32[]{:S(2)}) collective-permute-start(bf16[384,1152]{1,0:T(8,128)(2,1)} %get-tuple-element.68.refs_0_.x_ref), channel_id=1, source_target_pairs={{0,2},{1,3},{2,4},{3,5},{4,6},{5,7},{8,10},{9,11},{10,12},{11,13},... | collective-permute-start | bytes 2654216 | tf_op jit(solution)/shard_map/ppermute | solution.py:647
  26.2 34.0 %collective-permute-start.12 = (bf16[384,1152]{1,0:T(8,128)(2,1)}, bf16[384,1152]{1,0:T(8,128)(2,1)}, u32[]{:S(2)}, u32[]{:S(2)}) collective-permute-start(bf16[384,1152]{1,0:T(8,128)(2,1)} %get-tuple-element.68.refs_0_.x_ref), channel_id=1, source_target_pairs={{2,0},{3,1},{4,2},{5,3},{6,4},{7,5},{10,8},{11,9},{12,10},{13,11},... | collective-permute-start | bytes 2654216 | tf_op jit(solution)/shard_map/ppermute | solution.py:648
  69.9 27.7 %collective-permute-start.42 = (bf16[288,2304]{1,0:T(8,128)(2,1)}, bf16[288,2304]{1,0:T(8,128)(2,1)}, u32[]{:S(2)}, u32[]{:S(2)}) collective-permute-start(bf16[288,2304]{1,0:T(8,128)(2,1)} %pick_half.1.refs_4_), channel_id=1, source_target_pairs={{0,8},{8,0},{16,24},{24,16},{1,9},{9,1},{17,25},{25,17},{2,10},{10... | collective-permute-start | bytes 3981320 | tf_op jit(solution)/shard_map/ppermute | solution.py:47
  71.0 30.8 %collective-permute-start.43 = (bf16[288,2304]{1,0:T(8,128)(2,1)}, bf16[288,2304]{1,0:T(8,128)(2,1)}, u32[]{:S(2)}, u32[]{:S(2)}) collective-permute-start(bf16[288,2304]{1,0:T(8,128)(2,1)} %pick_half.1.refs_4_), channel_id=1, source_target_pairs={{0,16},{8,24},{16,0},{24,8},{1,17},{9,25},{17,1},{25,9},{2,18},{10... | collective-permute-start | bytes 3981320 | tf_op jit(solution)/shard_map/ppermute | solution.py:47
  76.1 26.8 %collective-permute-start.18 = (bf16[384,1152]{1,0:T(8,128)(2,1)}, bf16[384,1152]{1,0:T(8,128)(2,1)}, u32[]{:S(2)}, u32[]{:S(2)}) collective-permute-start(bf16[384,1152]{1,0:T(8,128)(2,1)} %collective-permute-done.14.refs_6_), channel_id=1, source_target_pairs={{4,6},{5,7},{12,14},{13,15},{20,22},{21,23},{28,30},{29,31}} | collective-permute-start | bytes 2654216 | tf_op jit(solution)/shard_map/ppermute | solution.py:647
  112.2 116.5 %collective-permute-start.41 = (bf16[384,1152]{1,0:T(8,128)(2,1)S(1)}, bf16[384,1152]{1,0:T(8,128)(2,1)S(1)}, u32[]{:S(2)}, u32[]{:S(2)}) collective-permute-start(bf16[384,1152]{1,0:T(8,128)(2,1)S(1)} %grad_mlp.1.refs_2_), channel_id=1, source_target_pairs={{0,1},{1,0},{2,3},{3,2},{4,5},{5,4},{6,7},{7,6},{8,9},{9,8},{10,11... | collective-permute-start | bytes 2654216 | tf_op jit(solution)/shard_map/ppermute | solution.py:47
  113.7 104.9 %collective-permute-start.46 = (bf16[576,1152]{1,0:T(8,128)(2,1)S(1)}, bf16[576,1152]{1,0:T(8,128)(2,1)S(1)}, u32[]{:S(2)}, u32[]{:S(2)}) collective-permute-start(bf16[576,1152]{1,0:T(8,128)(2,1)S(1)} %constant_dynamic-slice_fusion.refs_9_), channel_id=1, source_target_pairs={{0,8},{8,0},{16,24},{24,16},{1,9},{9,1},{17,25},{25,17},{2,10},{10... | collective-permute-start | bytes 3981320 | tf_op jit(solution)/shard_map/ppermute | solution.py:47
  114.7 105.2 %collective-permute-start.47 = (bf16[576,1152]{1,0:T(8,128)(2,1)S(1)}, bf16[576,1152]{1,0:T(8,128)(2,1)S(1)}, u32[]{:S(2)}, u32[]{:S(2)}) collective-permute-start(bf16[576,1152]{1,0:T(8,128)(2,1)S(1)} %constant_dynamic-slice_fusion.refs_9_), channel_id=1, source_target_pairs={{0,16},{8,24},{16,0},{24,8},{1,17},{9,25},{17,1},{25,9},{2,18},{10... | collective-permute-start | bytes 3981320 | tf_op jit(solution)/shard_map/ppermute | solution.py:47
  132.5 36.0 %collective-permute-start.36 = (bf16[144,1152]{1,0:T(8,128)(2,1)S(1)}, bf16[144,1152]{1,0:T(8,128)(2,1)S(1)}, u32[]{:S(2)}, u32[]{:S(2)}) collective-permute-start(bf16[144,1152]{1,0:T(8,128)(2,1)S(1)} %copy-done.28), channel_id=1, source_target_pairs={{0,1},{1,0},{2,3},{3,2},{4,5},{5,4},{6,7},{7,6},{8,9},{9,8},{10,11... | collective-permute-start | bytes 995336 | tf_op jit(solution)/shard_map/ppermute | solution.py:47
  133.9 35.1 %collective-permute-start.38 = (bf16[144,1152]{1,0:T(8,128)(2,1)S(1)}, bf16[144,1152]{1,0:T(8,128)(2,1)S(1)}, u32[]{:S(2)}, u32[]{:S(2)}) collective-permute-start(bf16[144,1152]{1,0:T(8,128)(2,1)S(1)} %collective-permute-done.37.refs_14_), channel_id=1, source_target_pairs={{0,1},{1,0},{2,3},{3,2},{4,5},{5,4},{6,7},{7,6},{8,9},{9,8},{10,11... | collective-permute-start | bytes 995336 | tf_op jit(solution)/shard_map/ppermute | solution.py:47
  215.7 40.7 %collective-permute-start.40 = (bf16[384,1152]{1,0:T(8,128)(2,1)}, bf16[384,1152]{1,0:T(8,128)(2,1)}, u32[]{:S(2)}, u32[]{:S(2)}) collective-permute-start(bf16[384,1152]{1,0:T(8,128)(2,1)} %get-tuple-element.82.refs_0_), channel_id=1, source_target_pairs={{0,1},{1,0},{2,3},{3,2},{4,5},{5,4},{6,7},{7,6},{8,9},{9,8},{10,11... | collective-permute-start | bytes 2654216 | tf_op jit(solution)/shard_map/ppermute | solution.py:47
  229.6 26.8 %collective-permute-start.49 = (bf16[288,1152]{1,0:T(8,128)(2,1)}, bf16[288,1152]{1,0:T(8,128)(2,1)S(1)}, u32[]{:S(2)}, u32[]{:S(2)}) collective-permute-start(bf16[288,1152]{1,0:T(8,128)(2,1)} %slice.254), channel_id=1, source_target_pairs={{0,8},{8,0},{16,24},{24,16},{1,9},{9,1},{17,25},{25,17},{2,10},{10... | collective-permute-start | bytes 1990664 | tf_op jit(solution)/shard_map/ppermute | solution.py:47
  396.4 332.4 %all-gather.3.cloned.1.call-start = ((), (), s32[]{:S(2)}) async-start(), calls=%async_computation.2 | async-start | bytes 3981312 | tf_op jit(solution)/shard_map/all_gather | solution.py:1010
  424.0 41.7 %collective-permute-start.101 = (bf16[2,288,1152]{2,1,0:T(8,128)(2,1)S(1)}, bf16[2,288,1152]{2,1,0:T(8,128)(2,1)S(1)}, u32[]{:S(2)}, u32[]{:S(2)}) collective-permute-start(bf16[2,288,1152]{2,1,0:T(8,128)(2,1)S(1)} %copy-done.84), channel_id=1, source_target_pairs={{0,8},{8,0},{16,24},{24,16},{1,9},{9,1},{17,25},{25,17},{2,10},{10... | collective-permute-start | bytes 3981320 | tf_op jit(solution)/shard_map/ppermute | solution.py:47
  428.7 63.5 %collective-permute-start.103 = (bf16[2,288,1152]{2,1,0:T(8,128)(2,1)S(1)}, bf16[2,288,1152]{2,1,0:T(8,128)(2,1)S(1)}, u32[]{:S(2)}, u32[]{:S(2)}) collective-permute-start(bf16[2,288,1152]{2,1,0:T(8,128)(2,1)S(1)} %copy-done.82), channel_id=1, source_target_pairs={{0,16},{8,24},{16,0},{24,8},{1,17},{9,25},{17,1},{25,9},{2,18},{10... | collective-permute-start | bytes 3981320 | tf_op jit(solution)/shard_map/ppermute | solution.py:47
  457.4 33.2 %collective-permute-start.95 = (bf16[2,144,2304]{2,1,0:T(8,128)(2,1)S(1)}, bf16[2,144,2304]{2,1,0:T(8,128)(2,1)S(1)}, u32[]{:S(2)}, u32[]{:S(2)}) collective-permute-start(bf16[2,144,2304]{2,1,0:T(8,128)(2,1)S(1)} %copy-done.83), channel_id=1, source_target_pairs={{0,16},{8,24},{16,0},{24,8},{1,17},{9,25},{17,1},{25,9},{2,18},{10... | collective-permute-start | bytes 3981320 | tf_op jit(solution)/shard_map/ppermute | solution.py:47
  461.4 33.2 %collective-permute-start.93 = (bf16[2,144,2304]{2,1,0:T(8,128)(2,1)S(1)}, bf16[2,144,2304]{2,1,0:T(8,128)(2,1)S(1)}, u32[]{:S(2)}, u32[]{:S(2)}) collective-permute-start(bf16[2,144,2304]{2,1,0:T(8,128)(2,1)S(1)} %copy-done.81), channel_id=1, source_target_pairs={{0,8},{8,0},{16,24},{24,16},{1,9},{9,1},{17,25},{25,17},{2,10},{10... | collective-permute-start | bytes 3981320 | tf_op jit(solution)/shard_map/ppermute | solution.py:47
  462.5 62.5 %collective-permute-start.84 = (bf16[4,144,1152]{2,1,0:T(8,128)(2,1)}, bf16[4,144,1152]{2,1,0:T(8,128)(2,1)}, u32[]{:S(2)}, u32[]{:S(2)}) collective-permute-start(bf16[4,144,1152]{2,1,0:T(8,128)(2,1)} %get-tuple-element.117), channel_id=1, source_target_pairs={{0,1},{1,0},{2,3},{3,2},{4,5},{5,4},{6,7},{7,6},{8,9},{9,8},{10,11... | collective-permute-start | bytes 3981320 | tf_op jit(solution)/shard_map/ppermute | solution.py:47
  465.8 32.3 %collective-permute-start.80 = (bf16[2,144,768]{2,1,0:T(8,128)(2,1)S(1)}, bf16[2,144,768]{2,1,0:T(8,128)(2,1)S(1)}, u32[]{:S(2)}, u32[]{:S(2)}) collective-permute-start(bf16[2,144,768]{2,1,0:T(8,128)(2,1)S(1)} %copy-done.42), channel_id=1, source_target_pairs={{0,8},{8,0},{16,24},{24,16},{1,9},{9,1},{17,25},{25,17},{2,10},{10... | collective-permute-start | bytes 1327112 | tf_op jit(solution)/shard_map/ppermute | solution.py:47
  492.2 228.4 %collective-permute-start.74 = (bf16[8,2304]{1,0:T(8,128)(2,1)}, bf16[8,2304]{1,0:T(8,128)(2,1)}, u32[]{:S(2)}, u32[]{:S(2)}) collective-permute-start(bf16[8,2304]{1,0:T(8,128)(2,1)} %add_convert_fusion.15), channel_id=1, source_target_pairs={{0,8},{8,0},{16,24},{24,16},{1,9},{9,1},{17,25},{25,17},{2,10},{10... | collective-permute-start | bytes 110600 | tf_op jit(solution)/shard_map/ppermute | solution.py:47
  494.6 51.2 %collective-permute-start.102 = (bf16[288,1152]{1,0:T(8,128)(2,1)}, bf16[288,1152]{1,0:T(8,128)(2,1)S(1)}, u32[]{:S(2)}, u32[]{:S(2)}) collective-permute-start(bf16[288,1152]{1,0:T(8,128)(2,1)} %slice_bitcast_fusion.2), channel_id=1, source_target_pairs={{0,16},{8,24},{16,0},{24,8},{1,17},{9,25},{17,1},{25,9},{2,18},{10... | collective-permute-start | bytes 1990664 | tf_op jit(solution)/shard_map/ppermute | solution.py:47
  498.1 47.8 %collective-permute-start.104 = (bf16[288,1152]{1,0:T(8,128)(2,1)}, bf16[288,1152]{1,0:T(8,128)(2,1)S(1)}, u32[]{:S(2)}, u32[]{:S(2)}) collective-permute-start(bf16[288,1152]{1,0:T(8,128)(2,1)} %slice_bitcast_fusion), channel_id=1, source_target_pairs={{0,8},{8,0},{16,24},{24,16},{1,9},{9,1},{17,25},{25,17},{2,10},{10... | collective-permute-start | bytes 1990664 | tf_op jit(solution)/shard_map/ppermute | solution.py:47
  524.2 35.8 %collective-permute-start.96 = (bf16[144,2304]{1,0:T(8,128)(2,1)}, bf16[144,2304]{1,0:T(8,128)(2,1)}, u32[]{:S(2)}, u32[]{:S(2)}) collective-permute-start(bf16[144,2304]{1,0:T(8,128)(2,1)} %slice_bitcast_fusion.4), channel_id=1, source_target_pairs={{0,8},{8,0},{16,24},{24,16},{1,9},{9,1},{17,25},{25,17},{2,10},{10... | collective-permute-start | bytes 1990664 | tf_op jit(solution)/shard_map/ppermute | solution.py:47
  550.9 201.8 %collective-permute-start.75 = (bf16[8,2304]{1,0:T(8,128)(2,1)}, bf16[8,2304]{1,0:T(8,128)(2,1)}, u32[]{:S(2)}, u32[]{:S(2)}) collective-permute-start(bf16[8,2304]{1,0:T(8,128)(2,1)} %add_convert_fusion.15), channel_id=1, source_target_pairs={{0,16},{8,24},{16,0},{24,8},{1,17},{9,25},{17,1},{25,9},{2,18},{10... | collective-permute-start | bytes 110600 | tf_op jit(solution)/shard_map/ppermute | solution.py:47
  559.6 193.1 %collective-permute-start.76 = (bf16[8,2304]{1,0:T(8,128)(2,1)}, bf16[8,2304]{1,0:T(8,128)(2,1)}, u32[]{:S(2)}, u32[]{:S(2)}) collective-permute-start(bf16[8,2304]{1,0:T(8,128)(2,1)} %add_convert_fusion.15), channel_id=1, source_target_pairs={{0,24},{8,16},{16,8},{24,0},{1,25},{9,17},{17,9},{25,1},{2,26},{10... | collective-permute-start | bytes 110600 | tf_op jit(solution)/shard_map/ppermute | solution.py:47
  599.9 47.8 %collective-permute-start.106 = (bf16[288,1152]{1,0:T(8,128)(2,1)S(1)}, bf16[288,1152]{1,0:T(8,128)(2,1)S(1)}, u32[]{:S(2)}, u32[]{:S(2)}) collective-permute-start(bf16[288,1152]{1,0:T(8,128)(2,1)S(1)} %add_convert_fusion.6), channel_id=1, source_target_pairs={{0,4},{1,5},{2,6},{3,7},{4,0},{5,1},{6,2},{7,3},{8,12},{9,13},{10,... | collective-permute-start | bytes 1990664 | tf_op jit(solution)/shard_map/ppermute | solution.py:47
  616.5 45.4 %collective-permute-start.98 = (bf16[144,2304]{1,0:T(8,128)(2,1)S(1)}, bf16[144,2304]{1,0:T(8,128)(2,1)S(1)}, u32[]{:S(2)}, u32[]{:S(2)}) collective-permute-start(bf16[144,2304]{1,0:T(8,128)(2,1)S(1)} %add_convert_fusion.8), channel_id=1, source_target_pairs={{0,4},{1,5},{2,6},{3,7},{4,0},{5,1},{6,2},{7,3},{8,12},{9,13},{10,... | collective-permute-start | bytes 1990664 | tf_op jit(solution)/shard_map/ppermute | solution.py:47
  662.1 29.4 %collective-permute-start.99 = (bf16[144,2304]{1,0:T(8,128)(2,1)S(1)}, bf16[144,2304]{1,0:T(8,128)(2,1)S(1)}, u32[]{:S(2)}, u32[]{:S(2)}) collective-permute-start(bf16[144,2304]{1,0:T(8,128)(2,1)S(1)} %add_convert_fusion.7), channel_id=1, source_target_pairs={{0,2},{1,3},{2,0},{3,1},{4,6},{5,7},{6,4},{7,5},{8,10},{9,11},{10,... | collective-permute-start | bytes 1990664 | tf_op jit(solution)/shard_map/ppermute | solution.py:47
  716.9 35.9 %collective-permute-start.62 = (bf16[8,2304]{1,0:T(8,128)(2,1)}, bf16[8,2304]{1,0:T(8,128)(2,1)}, u32[]{:S(2)}, u32[]{:S(2)}) collective-permute-start(bf16[8,2304]{1,0:T(8,128)(2,1)} %add_convert_fusion.17), channel_id=1, source_target_pairs={{0,8},{8,0},{16,24},{24,16},{1,9},{9,1},{17,25},{25,17},{2,10},{10... | collective-permute-start | bytes 110600 | tf_op jit(solution)/shard_map/ppermute | solution.py:47
  717.3 35.4 %collective-permute-start.63 = (bf16[8,2304]{1,0:T(8,128)(2,1)}, bf16[8,2304]{1,0:T(8,128)(2,1)}, u32[]{:S(2)}, u32[]{:S(2)}) collective-permute-start(bf16[8,2304]{1,0:T(8,128)(2,1)} %add_convert_fusion.17), channel_id=1, source_target_pairs={{0,16},{8,24},{16,0},{24,8},{1,17},{9,25},{17,1},{25,9},{2,18},{10... | collective-permute-start | bytes 110600 | tf_op jit(solution)/shard_map/ppermute | solution.py:47
  720.6 32.2 %collective-permute-start.64 = (bf16[8,2304]{1,0:T(8,128)(2,1)}, bf16[8,2304]{1,0:T(8,128)(2,1)}, u32[]{:S(2)}, u32[]{:S(2)}) collective-permute-start(bf16[8,2304]{1,0:T(8,128)(2,1)} %add_convert_fusion.17), channel_id=1, source_target_pairs={{0,24},{8,16},{16,8},{24,0},{1,25},{9,17},{17,9},{25,1},{2,26},{10... | collective-permute-start | bytes 110600 | tf_op jit(solution)/shard_map/ppermute | solution.py:47
  (170 other events, 2454.9 us)
Sparse Core Ops, SparseCore 0:
  396.5 88.8 reduce-scatter.1
  525.2 46.6 all-gather.2

commit v2 on v1

--- a/solution.py
+++ b/solution.py
@@ -26,7 +26,7 @@
     return jax.ShapeDtypeStruct(tuple(dims), kind)
 
 
-def run(name, body, ins, outs, scratch=(), flops=0, vmem=48, **more):
+def run(name, body, ins, outs, scratch=(), flops=0, vmem=48, collective=None, **more):
     moved = sum(a.size * a.dtype.itemsize for _, a in ins)
     moved += sum(math.prod(o.shape) * jnp.dtype(o.dtype).itemsize for _, o in outs)
     return pl.pallas_call(
@@ -35,7 +35,11 @@
         in_specs=[s for s, _ in ins],
         out_specs=[s for s, _ in outs],
         scratch_shapes=list(scratch),
-        compiler_params=pltpu.CompilerParams(vmem_limit_bytes=vmem << 20),
+        compiler_params=pltpu.CompilerParams(
+            vmem_limit_bytes=vmem << 20,
+            collective_id=collective,
+            has_side_effects=collective is not None,
+        ),
         cost_estimate=pl.CostEstimate(flops=flops, bytes_accessed=moved, transcendentals=0),
         name=name,
         **more,
@@ -51,6 +55,13 @@
     return lax.optimization_barrier((array,) + others)[0]
 
 
+def frequencies(steps, entries):
+    half = entries // 2
+    ladder = jnp.exp(-math.log(10000.0) * lax.iota(jnp.int32, half) / half)
+    angles = steps.astype(F32)[:, None] * ladder[None, :]
+    return jnp.concatenate([jnp.cos(angles), jnp.sin(angles)], axis=1)
+
+
 def nn(left, right):
     return lax.dot_general(left, right, (((1,), (0,)), ((), ())), preferred_element_type=F32)
 
@@ -63,12 +74,16 @@
     return lax.dot_general(left, right, (((0,), (0,)), ((), ())), preferred_element_type=F32)
 
 
-def each(count, step):
+def each(count, step, group=1):
+    if count % group:
+        group = 1
+
     def one(index, carry):
-        step(index)
+        for i in range(group):
+            step(index * group + i)
         return carry
 
-    lax.fori_loop(0, count, one, 0)
+    lax.fori_loop(0, count // group, one, 0)
 
 
 def normal(values):
@@ -82,9 +97,140 @@
     return scale * (grad - jnp.mean(grad, axis=-1, keepdims=True) - normed * along)
 
 
-def sort_body(width, items_ref, keep_ref, x_ref, c_ref, xs_ref, cs_ref, hot_ref, info_ref, perm_ref):
-    count = items_ref.shape[1]
-    slots = hot_ref.shape[0]
+def flip(index, by):
+    bit = 1
+    while bit <= by:
+        if by & bit:
+            index = index + bit * (1 - 2 * ((index // bit) % 2))
+        bit *= 2
+    return index
+
+
+def fetch(pairs, sems, first=0):
+    copies = []
+    for index, (source, target) in enumerate(pairs, first):
+        copy = pltpu.make_async_copy(source, target, sems.at[index])
+        copy.start()
+        copies.append(copy)
+    return copies
+
+
+class Routes:
+    def __init__(self, sent, got):
+        self.sent, self.got, self.known, self.started = sent, got, {}, []
+
+    def slot(self, name):
+        return self.known.setdefault(name, len(self.known))
+
+    def copy(self, name, source, target, to):
+        slot = self.slot(name)
+        return pltpu.make_async_remote_copy(
+            src_ref=source,
+            dst_ref=target,
+            send_sem=self.sent.at[slot],
+            recv_sem=self.got.at[slot],
+            device_id=to,
+            device_id_type=pl.DeviceIdType.MESH,
+        )
+
+    def start(self, name, source, target, to, when=None):
+        def make():
+            return self.copy(name, source, target, to)
+
+        self.started.append((make, when))
+        if when is None:
+            make().start()
+        else:
+            pl.when(when)(lambda: make().start())
+
+    def arrive(self, name, target, when=None):
+        def wait():
+            b = lax.axis_index("blk")
+            self.copy(name, target, target, {"blk": b + 1 - 2 * (b % 2)}).wait_recv()
+
+        if when is None:
+            wait()
+        else:
+            pl.when(when)(wait)
+
+    def finish(self):
+        for make, when in self.started:
+            if when is None:
+                make().wait_send()
+            else:
+                pl.when(when)(lambda make=make: make().wait_send())
+
+
+def greet(shards, chips):
+    f, b = lax.axis_index("fsdp"), lax.axis_index("blk")
+    z, c = b // 2, b % 2
+    barrier = pltpu.get_barrier_semaphore()
+
+    def signal(to):
+        pl.semaphore_signal(barrier, inc=1, device_id=to, device_id_type=pl.DeviceIdType.MESH)
+
+    for k in range(1, shards):
+        signal({"fsdp": flip(f, k)})
+    signal({"blk": b + 1 - 2 * c})
+    pl.when(z > 0)(lambda: signal({"blk": b - 2}))
+    pl.when(z < chips - 1)(lambda: signal({"blk": b + 2}))
+    ends = (z == 0).astype(I32) + (z == chips - 1).astype(I32)
+    pl.semaphore_wait(barrier, shards + 2 - ends)
+
+
+def pick_half_body(parts, ids_ref, w1_ref, w2_ref, o_ref):
+    rows, hidden = w1_ref.shape
+    half = hidden // parts // 2
+    size = o_ref.shape[1]
+    down = w2_ref.shape[0] // 2
+    blocks = hidden // 2 // size
+    for core in range(2):
+
+        @pl.when(ids_ref[2] == core)
+        def _():
+            picked = jnp.concatenate(
+                [
+                    w1_ref[:, (2 * part + core) * half : (2 * part + core + 1) * half]
+                    for part in range(parts)
+                ],
+                axis=1,
+            )
+            for block in range(blocks):
+                o_ref[block * rows : (block + 1) * rows, :] = picked[
+                    :, block * size : (block + 1) * size
+                ]
+            o_ref[blocks * rows :, :] = w2_ref[core * down : (core + 1) * down, :]
+
+
+def front_body(
+    shards, chips, heads, items_ref, keep_ref, x_ref, c_ref, spec_ref, temb_ref, ada_ref, qkvw_ref,
+    outw_ref, xs_ref, cs_ref, hot_ref, info_ref, perm_ref, mod_ref, cond_ref, low_ref, dm_ref, h_ref,
+    qkv_ref, wh_ref, wo_ref, x_all, spec_all, temb_all, part_own, part_got, hots, dms, wh_all, wo_all,
+    h_all, ada_s, qkvw_s, local, sent, got,
+):
+    f, b = lax.axis_index("fsdp"), lax.axis_index("blk")
+    z, c = b // 2, b % 2
+    blocks = 2 * chips
+    pair = b + 1 - 2 * c
+    width = BLOCK // blocks
+    count, size = x_ref.shape
+    units = count // width
+    own = heads // blocks
+    head_size = size // heads
+    slots = spec_ref.shape[0]
+    routes = Routes(sent, got)
+    inside = fetch(
+        [(ada_ref, ada_s), (qkvw_ref, qkvw_s), (outw_ref, wo_all.at[f])], local, units
+    )
+    greet(shards, chips)
+
+    spec_all[f] = spec_ref[...]
+    temb_all[f] = temb_ref[...]
+    for k in range(1, shards):
+        to = {"fsdp": flip(f, k)}
+        routes.start(("spec", k), spec_ref, spec_all.at[f], to)
+        routes.start(("temb", k), temb_ref, temb_all.at[f], to)
+
     items = items_ref[...]
     slot = lax.broadcasted_iota(I32, (slots, count), 0)
     hot = (items == slot).astype(F32)
@@ -96,99 +242,195 @@
     place = jnp.sum(hot * (start + rank), axis=0, keepdims=True) - 1.0
     perm = (row.astype(F32) == place).astype(BF16)
     perm_ref[...] = perm
-    xs_ref[...] = nn(perm, x_ref[...]).astype(BF16)
+    x_s = nn(perm, x_ref[...]).astype(BF16)
+    xs_ref[...] = x_s
+    x_all[b] = x_s
+
+    def line(side, s, send):
+        away = s - 1 if send else s
+        chip = z - away if side == 0 else z + away
+        ahead = z + 1 < chips if side == 0 else z > 0
+        known = z >= away if side == 0 else z + away < chips
+        when = known & ahead if send else known
+        return chip * 2 + c, {"blk": b + 2 if side == 0 else b - 2}, when
+
+    def send_on(s):
+        for side in range(2):
+            device, to, when = line(side, s, True)
+            routes.start(("line", side, s), x_all.at[device], x_all.at[device], to, when)
+
+    send_on(1)
+    routes.start("pair", x_all.at[b], x_all.at[b], {"blk": pair})
     cs_ref[...] = nn(perm, c_ref[...]).astype(BF16)
     keep = jnp.broadcast_to(keep_ref[...].astype(F32), (slots, count)).astype(BF16)
     kept = nt(keep, perm)
     at = lax.broadcasted_iota(I32, (slots, count), 1).astype(F32)
-    hot_ref[...] = kept * ((at >= start) & (at < end)).astype(F32)
-    head = (lax.broadcasted_iota(I32, (slots, LANES), 1) * width).astype(F32)
-    own = ((head >= start) & (head < end)).astype(F32)
+    hots[0] = kept * ((at >= start) & (at < end)).astype(F32)
+    first = (lax.broadcasted_iota(I32, (slots, LANES), 1) * width).astype(F32)
+    mine = ((first >= start) & (first < end)).astype(F32)
     which = lax.broadcasted_iota(I32, (slots, LANES), 0).astype(F32)
-    info_ref[0:1, :] = jnp.sum(own * which, axis=0, keepdims=True).astype(I32)
-    info_ref[1:2, :] = (jnp.sum(own * start, axis=0, keepdims=True) / width).astype(I32)
-    info_ref[2:3, :] = (jnp.sum(own * end, axis=0, keepdims=True) / width).astype(I32)
+    info_ref[0:1, :] = jnp.sum(mine * which, axis=0, keepdims=True).astype(I32)
+    info_ref[1:2, :] = (jnp.sum(mine * start, axis=0, keepdims=True) / width).astype(I32)
+    info_ref[2:3, :] = (jnp.sum(mine * end, axis=0, keepdims=True) / width).astype(I32)
     info_ref[3:8, :] = jnp.zeros((5, LANES), I32)
 
-
-def pick_heads_body(own, size, ids_ref, w_ref, o_ref):
-    width = w_ref.shape[1] // 3
-    first = ids_ref[1] * (own * size)
-    row = lax.broadcasted_iota(I32, (width, LANES), 0)
-    col = lax.broadcasted_iota(I32, (width, LANES), 1)
+    for k in range(1, shards):
+        other = flip(f, k)
+        routes.arrive(("spec", k), spec_all.at[other])
+        routes.arrive(("temb", k), temb_all.at[other])
+    spectra = spec_all[...].reshape(shards * slots, -1).astype(BF16)
+    condition = nn(spectra, temb_all[...].reshape(-1, size))
+    rows = ada_ref.shape[0]
+    for shard in range(shards):
+
+        @pl.when(f == shard)
+        def _():
+            cond_ref[...] = condition[:, shard * rows : (shard + 1) * rows]
+
+    values = cond_ref[...]
+    lifted = (values / (1.0 + jnp.exp(-values))).astype(BF16)
+    low_ref[...] = lifted
+    inside[0].wait()
+    part_own[...] = nn(lifted, ada_s[...]).reshape(part_own.shape)
+    for k in range(1, shards):
+        other = flip(f, k)
+        routes.start(("part", k), part_own.at[other], part_got.at[f], {"fsdp": other})
+
+    rows = qkvw_ref.shape[0]
+    inside[1].wait()
+    row = lax.broadcasted_iota(I32, (size, LANES), 0)
+    col = lax.broadcasted_iota(I32, (size, LANES), 1)
+    picked = []
     for head in range(own):
-        mark = (row == first + head * size + col) & (col < size)
-        pick = mark.astype(F32).astype(BF16)
-        for part in range(3):
+        mark = (row == (b * own + head) * head_size + col) & (col < head_size)
+        picked.append(mark.astype(F32).astype(BF16))
+    for part in range(3):
+        for head in range(own):
             at = (part * own + head) * LANES
-            o_ref[:, at : at + LANES] = nn(
-                w_ref[:, part * width : (part + 1) * width], pick
+            wh_all[f, :, at : at + LANES] = nn(
+                qkvw_s[:, part * size : (part + 1) * size], picked[head]
             ).astype(BF16)
-
-
-def pick_half_body(parts, ids_ref, w_ref, o_ref):
-    half = w_ref.shape[1] // parts // 2
-    for core in range(2):
-
-        @pl.when(ids_ref[2] == core)
-        def _():
-            for part in range(parts):
-                at = (2 * part + core) * half
-                o_ref[:, part * half : (part + 1) * half] = w_ref[:, at : at + half]
-
-
-def fetch(pairs, sems):
-    copies = []
-    for index, (source, target) in enumerate(pairs):
-        copy = pltpu.make_async_copy(source, target, sems.at[index])
-        copy.start()
-        copies.append(copy)
-    return copies
-
-
-def first_body(chips, plan, ids_ref, info_ref, mod_ref, *refs):
-    n_x = 2 + 4 * (chips - 1)
-    x_refs, refs = refs[:n_x], refs[n_x:]
-    w_refs, (h_ref, o_ref, x_all, w_all, sems) = refs[: len(plan)], refs[len(plan) :]
-    width = x_refs[0].shape[1]
-    f, b, c = ids_ref[0], ids_ref[1], ids_ref[2]
-    z = b // 2
-    u = pl.program_id(0)
-
-    @pl.when(u == 0)
-    def _():
-        rows = plan[-1][2]
-        todo = [(None, x_refs[0], x_all.at[b]), (None, x_refs[1], x_all.at[b + 1 - 2 * c])]
-        for s in range(1, chips):
-            left, right = (z - s) * 2, (z + s) * 2
-            at = 2 + 4 * (s - 1)
-            todo.append((z >= s, x_refs[at], x_all.at[jnp.maximum(left, 0) + c]))
-            todo.append((z >= s, x_refs[at + 1], x_all.at[jnp.maximum(left, 0) + 1 - c]))
-            capped = jnp.minimum(right, 2 * chips - 2)
-            todo.append((z + s < chips, x_refs[at + 2], x_all.at[capped + c]))
-            todo.append((z + s < chips, x_refs[at + 3], x_all.at[capped + 1 - c]))
-        for ref, (k, start, _) in zip(w_refs, plan):
-            at = pl.multiple_of(lax.bitwise_xor(f, k) * rows + start, 16)
-            todo.append((None, ref, w_all.at[pl.ds(at, ref.shape[0])]))
-        for phase in range(2):
-            for index, (when, source, target) in enumerate(todo):
-                copy = pltpu.make_async_copy(source, target, sems.at[index])
-                act = copy.wait if phase else copy.start
-                if when is None:
-                    act()
-                else:
-                    pl.when(when)(act)
-
-    slot = info_ref[0, u]
-    shift = mod_ref[pl.ds(slot, 1), 0:width]
-    scale = mod_ref[pl.ds(slot, 1), width : 2 * width]
-    rows = BLOCK // (2 * chips)
-    part = x_all[:, pl.ds(pl.multiple_of(u * rows, rows), rows), :]
-    values = part.reshape(BLOCK, width).astype(F32)
-    normed, _ = normal(values)
-    low = (normed * (1.0 + scale) + shift).astype(BF16)
-    h_ref[0] = low
-    o_ref[0] = nn(low, w_all[...]).astype(BF16)
+    if shards == 4:
+        for k in (1, 2):
+            routes.start(("head", k), wh_all.at[f], wh_all.at[f], {"fsdp": flip(f, k)})
+    else:
+        for k in range(1, shards):
+            routes.start(("head", k), wh_all.at[f], wh_all.at[f], {"fsdp": flip(f, k)})
+
+    def take(s):
+        for side in range(2):
+            device, _, when = line(side, s, False)
+            routes.arrive(("line", side, s), x_all.at[device], when)
+            if s + 1 < chips:
+                device, to, onward = line(side, s + 1, True)
+                routes.start(
+                    ("line", side, s + 1), x_all.at[device], x_all.at[device], to, onward
+                )
+            device, _, when = line(side, s, False)
+            routes.start(
+                ("pair", side, s), x_all.at[device], x_all.at[device], {"blk": pair}, when
+            )
+
+    take(1)
+    if shards == 4:
+        half = rows // 2
+        for k, low in ((1, 0), (2, half)):
+            routes.arrive(("head", k), wh_all.at[flip(f, k)])
+            part = wh_all.at[flip(f, k), low : low + half]
+            routes.start(("head", 3, k), part, part, {"fsdp": flip(f, 3 - k)})
+
+    for k in range(1, shards):
+        routes.start(("out", k), outw_ref.at[c], wo_all.at[f, c], {"fsdp": flip(f, k)})
+
+    total = part_own[f]
+    for k in range(1, shards):
+        other = flip(f, k)
+        routes.arrive(("part", k), part_got.at[other])
+        total = total + part_got[other]
+    mod_ref[...] = lax.dot_general(
+        mine[:, : mod_ref.shape[0]], total, (((0,), (0,)), ((), ())), precision=HIGH,
+        preferred_element_type=F32,
+    )
+
+    def early(u):
+        rows = pl.ds(pl.multiple_of(u * width, width), width)
+        gate = mod_ref[pl.ds(u, 1), 5 * size : 6 * size]
+        dms[0, rows, :] = (cs_ref[rows, :].astype(F32) * gate).astype(BF16)
+
+    each(units, early)
+    routes.start("dm", dms.at[0], dms.at[1], {"blk": pair})
+    routes.start("hot", hots.at[0], hots.at[1], {"blk": pair})
+
+    if shards == 4:
+        half = rows // 2
+        routes.arrive(("head", 3, 1), wh_all.at[flip(f, 3), 0:half])
+        routes.arrive(("head", 3, 2), wh_all.at[flip(f, 3), half:rows])
+    else:
+        for k in range(1, shards):
+            routes.arrive(("head", k), wh_all.at[flip(f, k)])
+    wh_ref[...] = wh_all[...].reshape(wh_ref.shape)
+
+    def block(device):
+        at = pl.ds(pl.multiple_of(device * width, width), width)
+
+        def one(u):
+            shift = mod_ref[pl.ds(u, 1), 0:size]
+            scale = mod_ref[pl.ds(u, 1), size : 2 * size]
+            part = x_all[device, pl.ds(pl.multiple_of(u * width, width), width), :]
+            normed, _ = normal(part.astype(F32))
+            low = (normed * (1.0 + scale) + shift).astype(BF16)
+            h_all[pl.ds(pl.multiple_of(u * width, width), width), :] = low
+
+        each(units, one, 3)
+        copies = fetch(
+            [
+                (h_all.at[u * width : (u + 1) * width], h_ref.at[u, at])
+                for u in range(units)
+            ],
+            local,
+        )
+        found = nn(h_all[...], wh_ref[...]).astype(BF16)
+        qkv_ref[:, at, :] = found.reshape(units, width, found.shape[1])
+        for copy in copies:
+            copy.wait()
+
+    routes.arrive("pair", x_all.at[pair])
+    each(2, lambda core: block(z * 2 + core))
+
+    def work(s):
+        for side in range(2):
+            device, _, when = line(side, s, False)
+            routes.arrive(("pair", side, s), x_all.at[device + 1 - 2 * c], when)
+
+        def pick(q):
+            chip = z - s + 2 * s * (q // 2)
+
+            @pl.when((chip >= 0) & (chip < chips))
+            def _():
+                block(chip * 2 + q % 2)
+
+        each(4, pick)
+
+    for s in range(2, chips):
+        take(s)
+        if s == 2:
+            for k in range(1, shards):
+                other = flip(f, k)
+                routes.arrive(("out", k), wo_all.at[other, c])
+                routes.start(
+                    ("pair out", k), wo_all.at[other, c], wo_all.at[other, c], {"blk": pair}
+                )
+        work(s - 1)
+    work(chips - 1)
+    inside[2].wait()
+    for k in range(1, shards):
+        routes.arrive(("pair out", k), wo_all.at[flip(f, k), 1 - c])
+    routes.arrive("dm", dms.at[1])
+    routes.arrive("hot", hots.at[1])
+    routes.finish()
+    copies = fetch([(wo_all, wo_ref), (dms, dm_ref), (hots, hot_ref)], local)
+    for copy in copies:
+        copy.wait()
 
 
 def exchange_lanes(tiles, width):
@@ -337,45 +579,24 @@
     each(units, turn)
 
 
-def early_body(width, info_ref, mod_ref, c_ref, o_ref):
-    size = c_ref.shape[1]
-
-    def one(u):
-        rows = pl.ds(pl.multiple_of(u * width, width), width)
-        gate = mod_ref[pl.ds(info_ref[0, u], 1), 5 * size : 6 * size]
-        o_ref[rows, :] = (c_ref[rows, :].astype(F32) * gate).astype(BF16)
-
-    each(c_ref.shape[0] // width, one)
-
-
-def project_body(width, blocks, ids_ref, info_ref, mod_ref, x_ref, *refs):
+def project_body(width, blocks, ids_ref, mod_ref, x_ref, w_ref, *refs):
     om_refs, refs = refs[:blocks], refs[blocks:]
-    w_refs, refs = refs[:-8], refs[-8:]
-    attn_ref, x1_ref, h_ref, om_ref, w_ref, om_all, w_all, sems = refs
-    f, b, c = ids_ref[0], ids_ref[1], ids_ref[2]
+    attn_ref, x1_ref, h_ref, om_ref, om_all, sems = refs
+    b = ids_ref[1]
     size = x_ref.shape[1]
     copies = fetch(
-        [(om_refs[k], om_all.at[lax.bitwise_xor(b, k)]) for k in range(blocks)]
-        + [
-            (ref, w_all.at[2 * lax.bitwise_xor(f, i // 2) + lax.bitwise_xor(c, i % 2)])
-            for i, ref in enumerate(w_refs)
-        ],
-        sems,
+        [(om_refs[k], om_all.at[lax.bitwise_xor(b, k)]) for k in range(blocks)], sems
     )
     for copy in copies:
         copy.wait()
     om = om_all[...].reshape(size, x_ref.shape[0])
-    weight = w_all[...].reshape(size, size)
     om_ref[...] = om
-    w_ref[...] = weight
+    weight = w_ref[...]
     attn_ref[...] = tn(om, weight)
 
     def one(u):
         rows = pl.ds(pl.multiple_of(u * width, width), width)
-        slot = info_ref[0, u]
-        gate, shift, scale = [
-            mod_ref[pl.ds(slot, 1), i * size : (i + 1) * size] for i in (2, 3, 4)
-        ]
+        gate, shift, scale = [mod_ref[pl.ds(u, 1), i * size : (i + 1) * size] for i in (2, 3, 4)]
         middle = x_ref[rows, :].astype(F32) + gate * attn_ref[rows, :]
         x1_ref[rows, :] = middle
         normed, _ = normal(middle)
@@ -384,35 +605,31 @@
     each(x_ref.shape[0] // width, one)
 
 
-def ff_body(plan1, plan2, outs1, outs2, step, ids_ref, hot_m, hot_o, chan_ref, *refs):
-    n1, n2 = len(plan1), len(plan2)
-    rows_refs, refs = refs[:4], refs[4:]
-    w1_refs, w2_refs, refs = refs[:n1], refs[n1 : n1 + n2], refs[n1 + n2 :]
-    mlp_m, mlp_o, dh_m, dh_o = refs[:4]
-    g1_refs, refs = refs[4 : 4 + len(outs1)], refs[4 + len(outs1) :]
-    g2_refs, refs = refs[: len(outs2)], refs[len(outs2) :]
-    w1, w2, h, dm, turned, hid_s, du_s, mlp, dh, g1, g2, sems = refs
-    f = ids_ref[0]
+def ff_body(shards, step, hot_ref, chan_ref, h_m, h_o, dm_ref, w_ref, *refs):
+    mlp_m, mlp_o, dh_m, dh_o, g_ref, w1, w2, h, dm, turned, hid_s, du_s, mlp, dh, g1, g2, sems = refs
     total = h.shape[0]
     count = total // 2
     f_size, size = w2.shape
-    row1, row2 = plan1[-1][2], plan2[-1][2]
-    shards = size // row1
-
-    def placed(refs, plan, rows, target):
-        for ref, (k, start, _) in zip(refs, plan):
-            at = pl.multiple_of(lax.bitwise_xor(f, k) * rows + start, 16)
-            yield ref, target.at[pl.ds(at, ref.shape[0])]
+    blocks = f_size // size
+    row1, row2 = size // shards, f_size // shards
+
+    def placed(rows, one, two):
+        for shard in range(shards):
+            for block in range(blocks):
+                yield (
+                    rows.at[shard, block * row1 : (block + 1) * row1],
+                    one.at[shard * row1 : (shard + 1) * row1, block * size : (block + 1) * size],
+                )
+            yield rows.at[shard, blocks * row1 :], two.at[shard * row2 : (shard + 1) * row2]
 
     copies = fetch(
         [
-            (rows_refs[0], h.at[0:count]),
-            (rows_refs[1], h.at[count:total]),
-            (rows_refs[2], dm.at[0:count]),
-            (rows_refs[3], dm.at[count:total]),
+            (h_m, h.at[0:count]),
+            (h_o, h.at[count:total]),
+            (dm_ref.at[0], dm.at[0:count]),
+            (dm_ref.at[1], dm.at[count:total]),
         ]
-        + list(placed(w1_refs, plan1, row1, w1))
-        + list(placed(w2_refs, plan2, row2, w2)),
+        + list(placed(w_ref, w1, w2)),
         sems,
     )
     for copy in copies:
@@ -421,7 +638,7 @@
         turned[:, at : at + LANES] = h[at : at + LANES, :].astype(F32).T.astype(BF16)
     mlp[...] = jnp.zeros_like(mlp)
     dh[...] = jnp.zeros_like(dh)
-    hots = [hot_m[...].astype(BF16), hot_o[...].astype(BF16)]
+    hots = [hot_ref[side].astype(BF16) for side in range(2)]
 
     def one(index):
         cols = pl.ds(pl.multiple_of(index * step, step), step)
@@ -454,16 +671,7 @@
     dh_m[...] = dh[0:count, :]
     dh_o[...] = dh[count:total, :].astype(BF16)
 
-    def leave(refs, outs, rows, source):
-        for ref, (ks, start, height) in zip(refs, outs):
-            for i, k in enumerate(ks):
-                at = pl.multiple_of(lax.bitwise_xor(f, k) * rows + start, 16)
-                yield source.at[pl.ds(at, height)], ref.at[i]
-
-    copies = fetch(
-        list(leave(g1_refs, outs1, row1, g1)) + list(leave(g2_refs, outs2, row2, g2)), sems
-    )
-    for copy in copies:
+    for copy in fetch([(found, rows) for rows, found in placed(g_ref, g1, g2)], sems):
         copy.wait()
 
 
@@ -479,8 +687,8 @@
     def one(u):
         rows = pl.ds(pl.multiple_of(u * width, width), width)
         slot = info_ref[0, u]
-        gate = mod_ref[pl.ds(slot, 1), 2 * size : 3 * size]
-        scale = mod_ref[pl.ds(slot, 1), 4 * size : 5 * size]
+        gate = mod_ref[pl.ds(u, 1), 2 * size : 3 * size]
+        scale = mod_ref[pl.ds(u, 1), 4 * size : 5 * size]
         normed, spread = normal(x1_ref[rows, :])
         grad = dh_ref[rows, :] + got_ref[rows, :].astype(F32)
         sum_ref[pl.ds(slot, 1), 0:size] += jnp.sum(grad, axis=0, keepdims=True)
@@ -505,7 +713,7 @@
     def one(u):
         rows = pl.ds(pl.multiple_of(u * width, width), width)
         slot = info_ref[0, u]
-        gate = mod_ref[pl.ds(slot, 1), 5 * size : 6 * size]
+        gate = mod_ref[pl.ds(u, 1), 5 * size : 6 * size]
         mlp = mlp_ref[rows, :] + got_ref[rows, :].astype(F32)
         held[rows, :] = (x1_ref[rows, :] + gate * mlp).astype(BF16)
         sum_ref[pl.ds(slot, 1), 0:size] += jnp.sum(
@@ -524,13 +732,12 @@
         other_ref[k] = grad[base + 1 - c]
 
 
-def qkv_back_body(plan, outs, blocks, ids_ref, h_ref, d_ref, w_ref, *refs):
+def qkv_back_body(rows, outs, blocks, ids_ref, h_ref, d_ref, w_ref, *refs):
     n = len(outs)
     dh_ref, g_refs, (acc, low, sems) = refs[0], refs[1 : 1 + n], refs[1 + n :]
     f = ids_ref[0]
     step = pl.program_id(0)
     per, _, size = h_ref.shape
-    rows = plan[-1][2]
     width = BLOCK // blocks
     for i in range(per):
         piece = nt(d_ref[i], w_ref[...]).astype(BF16)
@@ -564,7 +771,7 @@
     def one(u):
         rows = pl.ds(pl.multiple_of(u * width, width), width)
         slot = info_ref[0, u]
-        scale = mod_ref[pl.ds(slot, 1), size : 2 * size]
+        scale = mod_ref[pl.ds(u, 1), size : 2 * size]
         normed, spread = normal(x_ref[rows, :].astype(F32))
         grad = dh_ref[rows, :].astype(F32)
         sum_ref[pl.ds(slot, 1), 0:size] += jnp.sum(grad, axis=0, keepdims=True)
@@ -574,22 +781,6 @@
 
     each(count // width, one)
     o_ref[...] = tn(perm_ref[...], held[...]).astype(BF16)
-
-
-def gather_plan(shards, rows):
-    if shards == 4:
-        half = rows // 2
-        return [(0, 0, rows), (1, 0, rows), (2, 0, rows), (3, 0, rows), (3, half, rows)]
-    return [(k, 0, rows) for k in range(shards)]
-
-
-def gather_rows(own, shards):
-    if shards == 4:
-        half = own.shape[0] // 2
-        one, two = swap(own, "fsdp", 1), swap(own, "fsdp", 2)
-        top, low = swap(one[:half], "fsdp", 2), swap(two[half:], "fsdp", 1)
-        return [own, one, two, top, low]
-    return [own] + [swap(own, "fsdp", k) for k in range(1, shards)]
 
 
 def reduce_plan(shards, rows):
@@ -637,17 +828,6 @@
     groups = [[2 * i + core for i in range(chips)] for core in range(2)]
     both = lax.psum(jnp.concatenate([one, two]), "blk", axis_index_groups=groups)
     return both[: one.shape[0]], both[one.shape[0] :]
-
-
-def line_gather(own, chips):
-    out = []
-    behind = ahead = own
-    for s in range(1, chips):
-        first, last = 2 * (s - 1), 2 * (chips - 1)
-        behind = lax.ppermute(behind, "blk", [(i, i + 2) for i in range(first, last)])
-        ahead = lax.ppermute(ahead, "blk", [(i + 2, i) for i in range(last - first)])
-        out += [behind, swap(behind, "blk", 1), ahead, swap(ahead, "blk", 1)]
-    return out
 
 
 def both_cores(array):
@@ -686,102 +866,69 @@
     half = hidden // 2
     ids = jnp.stack([f, b, c]).astype(I32)
 
+    fc_rows = (half // size) * w_fc1.shape[0] + w_fc2.shape[0] // 2
+    (fc_own,) = run(
+        "pick_half",
+        functools.partial(pick_half_body, shards),
+        [(SMEM, ids), (VMEM, w_fc1), (VMEM, w_fc2)],
+        [(VMEM, shape((fc_rows, size)))],
+    )
+    fc_all = lax.all_gather(fc_own, "fsdp", axis=0, tiled=True).reshape(shards, fc_rows, size)
+
     items = lax.dynamic_slice_in_dim(segment_ids, b * count, count, axis=1)
-    x_s, c_s, hot, info, perm = run(
-        "sort_tokens",
-        functools.partial(sort_body, width),
-        [(VMEM, items), (VMEM, token_mask[None, :]), (VMEM, tokens), (VMEM, cotangent)],
+    rows = w_temb.shape[0]
+    entries = rows * shards
+    spectrum = frequencies(timesteps[0], entries).astype(BF16).astype(F32)
+    out_rows = w_out.shape[0] // 2
+    ada_rows, wider = w_ada.shape
+    padded = -(-units // 8) * 8
+    n_copies = 8 * shards + 4 * chips + 8
+    outs = run(
+        "front",
+        functools.partial(front_body, shards, chips, heads),
+        [
+            (VMEM, a)
+            for a in (items, token_mask[None, :], tokens, cotangent, spectrum, w_temb)
+        ]
+        + [(ANY, a) for a in (w_ada, w_qkv, w_out.reshape(2, out_rows, size))],
         [
             (VMEM, shape((count, size))),
             (VMEM, shape((count, size))),
-            (VMEM, shape((slots, count), F32)),
+            (ANY, shape((2, slots, count), F32)),
             (VMEM, shape((8, LANES), I32)),
             (VMEM, shape((count, count))),
+            (VMEM, shape((padded, wider), F32)),
+            (VMEM, shape((shards * slots, ada_rows), F32)),
+            (VMEM, shape((shards * slots, ada_rows))),
+            (ANY, shape((2, count, size))),
+            (ANY, shape((units, BLOCK, size))),
+            (VMEM, shape((units, BLOCK, wide))),
+            (VMEM, shape((size, wide))),
+            (ANY, shape((shards, 2, out_rows, size))),
         ],
-    )
-
-    rows = w_temb.shape[0]
-    entries = rows * shards
-    index = jnp.concatenate([(f ^ k) * rows + lax.iota(I32, rows) for k in range(shards)])
-    ladder = jnp.exp(
-        -math.log(10000.0) * (index % (entries // 2)).astype(F32) / (entries // 2)
-    )
-    steps = jnp.concatenate(
-        [timesteps[0]] + [swap(timesteps, "fsdp", k)[0] for k in range(1, shards)]
-    )
-    angles = steps.astype(F32)[:, None] * ladder[None, :]
-    spectrum = jnp.where(index[None, :] < entries // 2, jnp.cos(angles), jnp.sin(angles))
-    spectrum = spectrum.astype(BF16)
-    temb = jnp.concatenate([w_temb] + [swap(w_temb, "fsdp", k) for k in range(1, shards)])
-    ada_rows = w_ada.shape[0]
-    condition = lax.dynamic_slice_in_dim(nn(spectrum, temb), f * ada_rows, ada_rows, axis=1)
-    lifted, silu_pull = jax.vjp(lambda v: v / (1.0 + jnp.exp(-v)), condition)
-    lifted = lifted.astype(BF16)
-    partial = nn(lifted, w_ada).reshape(shards, slots, -1)
-    mod = partial[0]
-    for k in range(1, shards):
-        mod = mod + swap(partial[k], "fsdp", k)
-
-    x_parts = [x_s, swap(x_s, "blk", 1)] + line_gather(x_s, chips)
-
-    (w_heads,) = run(
-        "pick_heads",
-        functools.partial(pick_heads_body, own, head_size),
-        [(SMEM, ids), (VMEM, w_qkv)],
-        [(VMEM, shape((w_qkv.shape[0], wide)))],
-    )
-    (w_fc1_half,) = run(
-        "pick_half",
-        functools.partial(pick_half_body, shards),
-        [(SMEM, ids), (VMEM, w_fc1)],
-        [(VMEM, shape((w_fc1.shape[0], half)))],
-    )
-    plan_qkv = gather_plan(shards, w_heads.shape[0])
-    qkv_parts = gather_rows(w_heads, shards)
-    out_rows = w_out.shape[0] // 2
-    w_out_half = lax.dynamic_slice_in_dim(w_out, c * out_rows, out_rows)
-    w_out_other = lax.dynamic_slice_in_dim(w_out, (1 - c) * out_rows, out_rows)
-    w_out_half = after(w_out_half, qkv_parts[1])
-    got = [swap(w_out_half, "fsdp", k) for k in range(1, shards)]
-    out_parts = [w_out_half, w_out_other]
-    for piece in got:
-        out_parts += [piece, swap(piece, "blk", 1)]
-    plan1 = gather_plan(shards, w_fc1_half.shape[0])
-    fc1_parts = gather_rows(after(w_fc1_half, got[0], got[1]), shards)
-    fc2_rows = w_fc2.shape[0] // 2
-    w_fc2_half = lax.dynamic_slice_in_dim(w_fc2, c * fc2_rows, fc2_rows)
-    plan2 = gather_plan(shards, fc2_rows)
-    fc2_parts = gather_rows(after(w_fc2_half, fc1_parts[1], fc1_parts[2]), shards)
-
-    (dm,) = run(
-        "grad_mlp",
-        functools.partial(early_body, width),
-        [(SMEM, info), (VMEM, mod), (VMEM, c_s)],
-        [(VMEM, shape((count, size)))],
-    )
-    dm_other = swap(dm, "blk", 1)
-    hot_other = swap(hot, "blk", 1)
-
-    whole = pl.BlockSpec(memory_space=pltpu.VMEM)
-    n_copies = len(x_parts) + len(plan_qkv)
-    normed, qkv = run(
-        "norm_qkv",
-        functools.partial(first_body, chips, plan_qkv),
-        [(SMEM, ids), (SMEM, info), (whole, mod)]
-        + [(ANY, part) for part in x_parts]
-        + [(ANY, part) for part in qkv_parts],
-        [
-            (pl.BlockSpec((1, BLOCK, size), lambda u: (u, 0, 0)), shape((units, BLOCK, size))),
-            (pl.BlockSpec((1, BLOCK, wide), lambda u: (u, 0, 0)), shape((units, BLOCK, wide))),
-        ],
         [
             pltpu.VMEM((blocks, count, size), BF16),
-            pltpu.VMEM((size, wide), BF16),
+            pltpu.VMEM((shards, slots, entries), F32),
+            pltpu.VMEM((shards, rows, size), BF16),
+            pltpu.VMEM((shards, slots, wider), F32),
+            pltpu.VMEM((shards, slots, wider), F32),
+            pltpu.VMEM((2, slots, count), F32),
+            pltpu.VMEM((2, count, size), BF16),
+            pltpu.VMEM((shards, w_qkv.shape[0], wide), BF16),
+            pltpu.VMEM((shards, 2, out_rows, size), BF16),
+            pltpu.VMEM((count, size), BF16),
+            pltpu.VMEM(w_ada.shape, BF16),
+            pltpu.VMEM(w_qkv.shape, BF16),
+            pltpu.SemaphoreType.DMA((units + 3,)),
+            pltpu.SemaphoreType.DMA((n_copies,)),
             pltpu.SemaphoreType.DMA((n_copies,)),
         ],
         flops=2 * units * BLOCK * size * wide,
-        grid=(units,),
-    )
+        vmem=60,
+        collective=0,
+    )
+    x_s, c_s, hots, info, perm, mod, condition, lifted, dms, normed, qkv, w_heads, w_out_all = outs
+    w_out_all = w_out_all.reshape(size, size)
 
     mask = head_mask[0]
     narrow = own * head_size
@@ -800,51 +947,39 @@
     held, lse, pieces = outs[0], outs[1], outs[2:]
     om_parts = [pieces[0]] + [swap(pieces[k], "blk", k) for k in range(1, blocks)]
 
-    attn, x1, h2, om, w_out_all = run(
+    attn, x1, h2, om = run(
         "project",
         functools.partial(project_body, width, blocks),
-        [(SMEM, ids), (SMEM, info), (VMEM, mod), (VMEM, x_s)]
-        + [(ANY, part) for part in om_parts]
-        + [(ANY, part) for part in out_parts],
+        [(SMEM, ids), (VMEM, mod), (VMEM, x_s), (VMEM, w_out_all)]
+        + [(ANY, part) for part in om_parts],
         [
             (VMEM, shape((count, size), F32)),
             (VMEM, shape((count, size), F32)),
             (VMEM, shape((count, size))),
             (VMEM, shape((size, count))),
-            (VMEM, shape((size, size))),
         ],
         [
             pltpu.VMEM((blocks, narrow, count), BF16),
-            pltpu.VMEM((2 * shards, out_rows, size), BF16),
-            pltpu.SemaphoreType.DMA((blocks + 2 * shards,)),
+            pltpu.SemaphoreType.DMA((blocks,)),
         ],
         flops=2 * count * size * size,
     )
     h2_other = swap(h2, "blk", 1)
 
-    outs1 = reduce_plan(shards, w_fc1_half.shape[0])
-    outs2 = reduce_plan(shards, fc2_rows)
     chan = chan_mask[0].reshape(slots, shards, 2, half // shards)
     chan = lax.dynamic_slice_in_dim(chan, c, 1, axis=2).reshape(slots, half)
-    n_sems = max(
-        4 + len(plan1) + len(plan2),
-        sum(len(ks) for ks, _, _ in outs1) + sum(len(ks) for ks, _, _ in outs2),
-    )
-    outs = run(
+    n_sems = 4 + shards * (half // size + 1)
+    mlp, mlp_send, dh2, dh2_send, g_fc = run(
         "feed_forward",
-        functools.partial(ff_body, plan1, plan2, outs1, outs2, 256),
-        [(SMEM, ids), (VMEM, hot), (VMEM, hot_other), (VMEM, chan)]
-        + [(ANY, a) for a in (h2, h2_other, dm, dm_other)]
-        + [(ANY, a) for a in fc1_parts]
-        + [(ANY, a) for a in fc2_parts],
+        functools.partial(ff_body, shards, 256),
+        [(VMEM, hots), (VMEM, chan)] + [(ANY, a) for a in (h2, h2_other, dms, fc_all)],
         [
             (VMEM, shape((count, size), F32)),
             (VMEM, shape((count, size))),
             (VMEM, shape((count, size), F32)),
             (VMEM, shape((count, size))),
-        ]
-        + [(ANY, shape((len(ks), height, half))) for ks, _, height in outs1]
-        + [(ANY, shape((len(ks), height, size))) for ks, _, height in outs2],
+            (ANY, shape((shards, fc_rows, size))),
+        ],
         [
             pltpu.VMEM((size, half), BF16),
             pltpu.VMEM((half, size), BF16),
@@ -862,8 +997,9 @@
         flops=6 * 2 * 2 * count * size * half,
         vmem=60,
     )
-    mlp, mlp_send, dh2, dh2_send = outs[:4]
-    g1_parts, g2_parts = outs[4 : 4 + len(outs1)], outs[4 + len(outs1) :]
+    g_fc = lax.psum_scatter(
+        g_fc.reshape(shards * fc_rows, size), "fsdp", scatter_dimension=0, tiled=True
+    )
     dh2_got = swap(dh2_send, "blk", 1)
     mlp_got = swap(mlp_send, "blk", 1)
 
@@ -916,21 +1052,17 @@
         ],
         flops=5 * units * units * BLOCK * BLOCK * wide // 3,
     )
-    w_heads_all = jnp.zeros((size, wide), BF16)
-    for part, (k, start, rows_in) in zip(qkv_parts, plan_qkv):
-        w_heads_all = lax.dynamic_update_slice_in_dim(
-            w_heads_all, part, (f ^ k) * rows_in + start, axis=0
-        )
     per = 4
-    outs_qkv = reduce_plan(shards, w_heads.shape[0])
+    rows_qkv = w_qkv.shape[0]
+    outs_qkv = reduce_plan(shards, rows_qkv)
     outs = run(
         "qkv_back",
-        functools.partial(qkv_back_body, plan_qkv, outs_qkv, blocks),
+        functools.partial(qkv_back_body, rows_qkv, outs_qkv, blocks),
         [
             (SMEM, ids),
             (pl.BlockSpec((per, BLOCK, size), lambda i: (i, 0, 0)), normed),
             (pl.BlockSpec((per, BLOCK, wide), lambda i: (i, 0, 0)), d_qkv),
-            (whole, w_heads_all),
+            (VMEM, w_heads),
         ],
         [
             (
@@ -966,26 +1098,27 @@
             if k < blocks:
                 total = total + swap(total, "blk", k)
         low = total.astype(BF16)
-        return jnp.concatenate([low] + [swap(low, "fsdp", k) for k in range(1, shards)])
+        return lax.all_gather(low, "fsdp", axis=0, tiled=True)
 
     gate_all, two_all, one_all = over_stream(sums_gate), over_stream(sums_two), over_stream(sums_one)
     d_mod = jnp.concatenate(
         [one_all, gate_all[:, :size], two_all, gate_all[:, size:]], axis=1
     )
     grad_ada = tn(lifted, d_mod)
+    _, silu_pull = jax.vjp(lambda v: v / (1.0 + jnp.exp(-v)), condition)
     (d_condition,) = silu_pull(nt(d_mod, w_ada))
-    d_all = jnp.zeros((shards * slots, size), F32)
-    for k in range(shards):
-        piece = d_condition if k == 0 else swap(d_condition, "fsdp", k)
-        piece = piece.reshape(shards, slots, ada_rows)
-        piece = jnp.concatenate([piece[r ^ k] for r in range(shards)])
-        d_all = lax.dynamic_update_slice_in_dim(d_all, piece, (f ^ k) * ada_rows, axis=1)
+    d_all = lax.all_gather(d_condition, "fsdp", axis=1, tiled=True)
+    steps = lax.all_gather(timesteps, "fsdp", axis=0, tiled=True)
+    spectra = frequencies(steps.reshape(-1), entries).astype(BF16).astype(F32)
     grad_temb = lax.dot_general(
-        spectrum[:, :rows].astype(F32), d_all, (((0,), (0,)), ((), ())), precision=HIGH
-    )
-
-    g1_one, g1_two = sum_chips(reduce_rows(g1_parts, shards), chips)
-    g2_one, g2_two = sum_chips(reduce_rows(g2_parts, shards), chips)
+        lax.dynamic_slice_in_dim(spectra, f * rows, rows, axis=1),
+        d_all,
+        (((0,), (0,)), ((), ())),
+        precision=HIGH,
+    )
+
+    cut = fc_rows - w_fc2.shape[0] // 2
+    g1, g2 = sum_chips((g_fc[:cut], g_fc[cut:]), chips)
     if shards == 4:
         cut = out_rows // 2
         pieces = [
@@ -999,9 +1132,11 @@
     o_one, o_two = sum_chips(reduce_rows(pieces, shards), chips)
     first, second = both_cores(jnp.concatenate([o_one, o_two]))
     grad_out = jnp.concatenate([first, second]).astype(F32)
-    first, second = both_cores(jnp.concatenate([g2_one, g2_two]))
+    first, second = both_cores(g2)
     grad_fc2 = jnp.concatenate([first, second]).astype(F32)
-    first, second = both_cores(jnp.concatenate([g1_one, g1_two]))
+    first, second = both_cores(
+        jnp.concatenate(jnp.split(g1, half // size, axis=0), axis=1)
+    )
     part = half // shards
     grad_fc1 = jnp.concatenate(
         [side[:, i * part : (i + 1) * part] for i in range(shards) for side in (first, second)],

time: 776 us -> 654 us (0.84); the launches traced: 776 us -> 642 us
  waiting for transfers between devices: 300 us -> 164 us
  starting transfers between devices: 144 us -> 70.5 us
  Pallas kernels: 202 us -> 269 us
  blocking collectives: 0 us -> 39 us
  local copies, waits for them, and re-layouts: 72.3 us -> 46.5 us
    ppermute x103 -> x44, waiting for transfers between devices: 286 us -> 164 us  [swap(): return lax.ppermute(array, axis, [(i, i ^ by) for i in range(size)])]
    pallas_call x13 -> x10, Pallas kernels: 202 us -> 269 us  [run(): pl.pallas_call(body, out_shape=[o for _, o in outs], in_specs=[s for s, _...]
    ppermute x103 -> x44, starting transfers between devices: 132 us -> 69.9 us  [swap(): return lax.ppermute(array, axis, [(i, i ^ by) for i in range(size)])]
    all_gather x0 -> x5, blocking collectives: none -> 39 us  [the longest x3 20.2 us: over_stream(): return lax.all_gather(low, 'fsdp', axis=0, tiled=True)]
    ppermute x6 -> x0, waiting for transfers between devices: 13.9 us -> none  [the longest x3 13.9 us: line_gather(): lax.ppermute(ahead, 'blk', [(i + 2, i) for i in range(last - first)])]
    ppermute x6 -> x0, starting transfers between devices: 11.3 us -> none  [the longest x3 7.49 us: line_gather(): lax.ppermute(behind, 'blk', [(i, i + 2) for i in range(first, last)])]
    unnamed x184 -> x93, local copies, waits for them, and re-layouts: 36.1 us -> 28.7 us
  transfers between devices with their start and end apart: 111 -> 48, of which waited for: 42 -> 18; matrix products, arithmetic and copies ran while one was open for 11% -> 10% of each run, Pallas kernels for 12% -> 34%
where the time goes in v2:
time: 654 us; the launch traced here: 642 us
  Pallas kernels  269 us (41%)
  waiting for transfers between devices  164 us (25%)
  starting transfers between devices  70.5 us (11%)
  local copies, waits for them, and re-layouts  46.5 us (7%)
  blocking collectives  39 us (6%)
  other arithmetic  30.5 us (5%)
  between operations  14.6 us (2%)
  matrix products  7.62 us (1%)
    pallas_call x10, Pallas kernels, run(): pl.pallas_call(body, out_shape=[o for _, o in outs], in_specs=[s for s, _...  269 us
    ppermute x44, waiting for transfers between devices, swap(): return lax.ppermute(array, axis, [(i, i ^ by) for i in range(size)])  164 us
    ppermute x44, starting transfers between devices, swap(): return lax.ppermute(array, axis, [(i, i ^ by) for i in range(size)])  69.9 us
    unnamed x93, local copies, waits for them, and re-layouts  28.7 us
    all_gather x3, blocking collectives, over_stream(): return lax.all_gather(low, 'fsdp', axis=0, tiled=True)  20.2 us
  transfers between devices with their start and end apart: 48, of which 18 were waited for; matrix products, arithmetic and copies ran while one was open for 10% of the time, Pallas kernels for 34%

profile of v2, /device:TPU:1, one launch (start us, length us, event | category | flops | bytes accessed | tf_op | source)
XLA Modules:
  0.0 641.8 jit_solution(9530758851994990452)
XLA Ops:
  15.2 102.0 %front.1 = (bf16[384,1152]{1,0:T(8,128)(2,1)}, bf16[384,1152]{1,0:T(8,128)(2,1)}, f32[2,8,384]{2,1,0:T(8,128)}, s32[8,128]{1,0:T(8,128)}, bf16[384,384]{1,0:T(8,...) custom-call(s32[1,384]{1,0:T(1,128)} %constant_dynamic-slice_fusion., ...), custom_call_target="tpu_custom_call" | custom-call | flops 5435817984 | bytes 29144064 | tf_op jit(solution)/shard_map/front/pallas_call | solution.py:32
  117.9 33.3 %attend.1 = (bf16[12,144,256]{2,1,0:T(8,128)(2,1)S(1)}, f32[12,8,256]{2,1,0:T(8,128)S(1)}, bf16[144,384]{1,0:T(8,128)(2,1)S(1)}, bf16[144,384]{1,0:T(8,128)(2,1)...) custom-call(s32[3]{0:T(128)S(1)} %pad_add_fusion.ids_ref, ...), custom_call_target="tpu_custom_call" | custom-call | flops 4831838208 | bytes 6590988 | tf_op jit(solution)/shard_map/attend/pallas_call | solution.py:32
  166.3 8.6 %collective-permute-done.4.refs_5_ = bf16[144,384]{1,0:T(8,128)(2,1)S(1)} collective-permute-done((bf16[144,384]{1,0:T(8,128)(2,1)S(1)}, bf16[144,384]{1,0:T(8,128)(2,1)S(1)}, u32[]{:S(2)}, u32[]{:S(2)}) %collective-permute-start.4) | collective-permute-done | bytes 110624 | tf_op jit(solution)/shard_map/ppermute | solution.py:51
  174.9 8.1 %project.1 = (f32[384,1152]{1,0:T(8,128)S(1)}, f32[384,1152]{1,0:T(8,128)}, bf16[384,1152]{1,0:T(8,128)(2,1)S(1)}, bf16[1152,384]{1,0:T(8,128)(2,1)S(1)}) custom-call(s32[3]{0:T(128)S(1)} %pad_add_fusion.ids_ref, f32[16,6912]{1,0:T(8,128)S(1)} %copy-done.4, bf16[384,1152]{1,0:T(8,128)(2,1)S(1)} %copy-done.5, bf16[1152,1152]{1,0:T(8,128)(2,1)} %bitcast.67, ...), custom_call_target="tpu_custom_call" | custom-call | flops 1019215872 | bytes 10174476 | tf_op jit(solution)/shard_map/project/pallas_call | solution.py:32
  186.8 46.7 %feed_forward.1 = (f32[384,1152]{1,0:T(8,128)}, bf16[384,1152]{1,0:T(8,128)(2,1)}, f32[384,1152]{1,0:T(8,128)}, bf16[384,1152]{1,0:T(8,128)(2,1)}, bf16[4,1152,1152]{2,1,0:T(8,128)(2,1)}) custom-call(f32[2,8,384]{2,1,0:T(8,128)} %get-tuple-element.77.hot_ref, s32[8,2304]{1,0:T(8,128)} %reshape.69.chan_ref, bf16[384,1152]{1,0:T(8,128)(2,1)} %copy-done.21, ...), custom_call_target="tpu_custom_call" | custom-call | flops 24461180928 | bytes 30179328 | tf_op jit(solution)/shard_map/feed_forward/pallas_call | solution.py:32
  236.7 8.9 %middle_back.1 = (bf16[144,384]{1,0:T(8,128)(2,1)S(1)}, bf16[144,384]{1,0:T(8,128)(2,1)S(1)}, bf16[144,384]{1,0:T(8,128)(2,1)S(1)}, bf16[144,384]{1,0:T(8,128)(2...) custom-call(s32[3]{0:T(128)S(1)} %pad_add_fusion.ids_ref, ...), custom_call_target="tpu_custom_call" | custom-call | flops 1019215872 | bytes 12021772 | tf_op jit(solution)/shard_map/middle_back/pallas_call | solution.py:32
  246.8 5.0 collective-permute-start.11
  261.8 8.1 %collective-permute-done.14.refs_5_ = bf16[144,384]{1,0:T(8,128)(2,1)S(1)} collective-permute-done((bf16[144,384]{1,0:T(8,128)(2,1)S(1)}, bf16[144,384]{1,0:T(8,128)(2,1)S(1)}, u32[]{:S(2)}, u32[]{:S(2)}) %collective-permute-start.14) | collective-permute-done | bytes 110624 | tf_op jit(solution)/shard_map/ppermute | solution.py:51
  269.9 33.6 %attend_back.1.d_ref = bf16[12,256,768]{2,1,0:T(8,128)(2,1)} custom-call(s32[3]{0:T(128)S(1)} %pad_add_fusion.ids_ref, s32[8,128]{1,0:T(8,128)S(1)} %copy-done.20, s32[8,16]{1,0:T(8,128)S(1)} %bitcast.63, bf16[12,256,768]{2,1,0:T(8,128)(2,1)} %get-tuple-element.66.qkv_ref, bf16[12,144,256]{2,1,0:T(8,128)(2,1)S(1)} %copy-done.27, ...), custom_call_target="tpu_custom_call" | custom-call | flops 12079595520 | bytes 11309580 | tf_op jit(solution)/shard_map/attend_back/pallas_call | solution.py:32
  303.5 19.4 %qkv_back.1 = (bf16[8,12,32,1152]{3,2,1,0:T(8,128)(2,1)}, bf16[2,144,768]{2,1,0:T(8,128)(2,1)S(1)}, bf16[2,144,768]{2,1,0:T(8,128)(2,1)S(1)}, bf16[2,144,768]{2,1,0:T(8,128)(2,1)S(1)}, bf16[2,144,768]{2,1,0:T(8,128)(2,1)S(1)}) custom-call(s32[3]{0:T(128)S(1)} %pad_add_fusion.ids_ref, bf16[12,256,1152]{2,1,0:T(8,128)(2,1)} %get-tuple-element.90.h_ref, ...), custom_call_target="tpu_custom_call" | custom-call | flops 10871635968 | bytes 22413324 | tf_op jit(solution)/shard_map/qkv_back/pallas_call | solution.py:32
  326.3 12.0 %all-gather.1 = s32[4,1,8]{2,1,0:T(1,128)S(1)} all-gather(s32[1,1,8]{2,1,0:T(1,128)S(1)} %bitcast.70), channel_id=1, replica_groups=mesh['fsdp'=4,'blk'=8] {'fsdp'}, dimensions={0}, use_global_device_ids=true | all-gather | bytes 160 | tf_op jit(solution)/shard_map/all_gather | solution.py:1111
  341.3 7.9 %result.1 = (bf16[384,1152]{1,0:T(8,128)(2,1)}, f32[8,2304]{1,0:T(8,128)S(1)}, bf16[4,144,1152]{2,1,0:T(8,128)(2,1)S(1)}, bf16[4,144,1152]{2,1,0:T(8,128)(2,1)}) custom-call(s32[3]{0:T(128)S(1)} %pad_add_fusion.ids_ref, s32[8,128]{1,0:T(8,128)S(1)} %copy-done.20, f32[16,6912]{1,0:T(8,128)S(1)} %copy-done.4, f32[384,1152]{1,0:T(8,128)} %get-tuple-element.75.x1_ref, ...), custom_call_target="tpu_custom_call" | custom-call | flops 1019215872 | bytes 14970892 | tf_op jit(solution)/shard_map/result/pallas_call | solution.py:32
  350.3 5.1 collective-permute-start.24
  369.4 6.8 %collective-permute-done.22 = f32[8,2304]{1,0:T(8,128)S(1)} collective-permute-done((f32[8,2304]{1,0:T(8,128)S(1)}, f32[8,2304]{1,0:T(8,128)S(1)}, u32[]{:S(2)}, u32[]{:S(2)}) %collective-permute-start.22) | collective-permute-done | bytes 73760 | tf_op jit(solution)/shard_map/ppermute | solution.py:51
  376.2 6.5 %all_gather.27 = bf16[32,2304]{1,0:T(8,128)(2,1)S(1)} all-gather(bf16[8,2304]{1,0:T(8,128)(2,1)S(1)} %add_convert_fusion.10), channel_id=1, replica_groups=mesh['fsdp'=4,'blk'=8] {'fsdp'}, dimensions={0}, use_global_device_ids=true | all-gather | bytes 184320 | tf_op jit(solution)/shard_map/all_gather | solution.py:1101
  390.2 4.7 collective-permute-done.33
  405.2 4.8 collective-permute-done.35
  411.2 6.9 %all_gather.28 = bf16[32,2304]{1,0:T(8,128)(2,1)S(1)} all-gather(bf16[8,2304]{1,0:T(8,128)(2,1)S(1)} %add_convert_fusion.9), channel_id=1, replica_groups=mesh['fsdp'=4,'blk'=8] {'fsdp'}, dimensions={0}, use_global_device_ids=true | all-gather | bytes 184320 | tf_op jit(solution)/shard_map/all_gather | solution.py:1101
  418.1 39.8 %collective-permute-done.36 = bf16[72,1152]{1,0:T(8,128)(2,1)S(1)} collective-permute-done((bf16[72,1152]{1,0:T(8,128)(2,1)S(1)}, bf16[72,1152]{1,0:T(8,128)(2,1)S(1)}, u32[]{:S(2)}, u32[]{:S(2)}) %collective-permute-start.36) | collective-permute-done | bytes 165920 | tf_op jit(solution)/shard_map/ppermute | solution.py:51
  468.2 9.8 %collective-permute-start.38 = (bf16[144,1152]{1,0:T(8,128)(2,1)}, bf16[144,1152]{1,0:T(8,128)(2,1)}, u32[]{:S(2)}, u32[]{:S(2)}) collective-permute-start(bf16[144,1152]{1,0:T(8,128)(2,1)} %pad_maximum_fusion.4), channel_id=1, source_target_pairs={{0,1},{1,0},{2,3},{3,2},{4,5},{5,4},{6,7},{7,6},{8,9},{9,8},{10,11... | collective-permute-start | bytes 995336 | tf_op jit(solution)/shard_map/ppermute | solution.py:51
  479.2 5.8 first_back.1
  485.1 65.9 %collective-permute-done.40 = bf16[576,1152]{1,0:T(8,128)(2,1)} collective-permute-done((bf16[576,1152]{1,0:T(8,128)(2,1)}, bf16[576,1152]{1,0:T(8,128)(2,1)}, u32[]{:S(2)}, u32[]{:S(2)}) %collective-permute-start.40) | collective-permute-done | bytes 1327136 | tf_op jit(solution)/shard_map/ppermute | solution.py:51
  556.9 7.8 %reshape.72 = bf16[8,288,3,2,128]{4,3,2,1,0:T(2,128)(2,1)} reshape(bf16[2304,768]{1,0:T(8,128)(2,1)} %all-gather.8.cloned.1.call-done) | data formatting | bytes 7077888 | tf_op jit(solution)/shard_map/reshape | solution.py:1146
  564.7 8.6 %copy.32 = bf16[8,288,3,2,72]{1,4,3,0,2:T(8,128)(2,1)} copy(bf16[8,288,3,2,72]{4,3,2,1,0:T(2,128)(2,1)} %bitcast.65) | data formatting | bytes 3981312
  573.3 4.6 convert_element_type.279
  577.9 6.0 copy.30
  589.2 6.8 %all_gather.26 = bf16[32,2304]{1,0:T(8,128)(2,1)S(1)} all-gather(bf16[8,2304]{1,0:T(8,128)(2,1)S(1)} %add_convert_fusion.11), channel_id=1, replica_groups=mesh['fsdp'=4,'blk'=8] {'fsdp'}, dimensions={0}, use_global_device_ids=true | all-gather | bytes 184320 | tf_op jit(solution)/shard_map/all_gather | solution.py:1101
  597.3 6.8 %all-gather.2 = f32[4,288,32]{1,2,0:T(8,128)S(1)} all-gather(f32[1,288,32]{1,2,0:T(8,128)S(1)} %add_bitcast_fusion), channel_id=1, replica_groups=mesh['fsdp'=4,'blk'=8] {'fsdp'}, dimensions={0}, use_global_device_ids=true | all-gather | bytes 184320 | tf_op jit(solution)/shard_map/all_gather | solution.py:1110
  604.5 5.2 fusion.4
  609.7 6.7 %collective-permute-start.43 = (bf16[576,1152]{1,0:T(8,128)(2,1)S(1)}, bf16[576,1152]{1,0:T(8,128)(2,1)}, u32[]{:S(2)}, u32[]{:S(2)}) collective-permute-start(bf16[576,1152]{1,0:T(8,128)(2,1)S(1)} %get-tuple-element.134), channel_id=1, source_target_pairs={{0,1},{1,0},{2,3},{3,2},{4,5},{5,4},{6,7},{7,6},{8,9},{9,8},{10,11... | collective-permute-start | bytes 3981320 | tf_op jit(solution)/shard_map/ppermute | solution.py:51
  620.9 5.0 concatenate.36
  625.9 4.8 convert_element_type.272
  (242 shorter events, 115.5 us)
Async XLA Ops:
  7.2 179.6 %all-gather.6.cloned.1.call-start = ((), (), s32[]{:S(2)}) async-start(), calls=%async_computation.2 | async-start | bytes 13271040 | tf_op jit(solution)/shard_map/all_gather | solution.py:876
  12.7 389.0 %reduce-scatter.5.cloned.1.call-start = ((), (), s32[]{:S(2)}) async-start(), calls=%async_computation.4 | async-start | bytes 13271040 | tf_op jit(solution)/shard_map/reduce_scatter | solution.py:1000
  156.4 10.0 %collective-permute-start.2 = (bf16[144,384]{1,0:T(8,128)(2,1)S(1)}, bf16[144,384]{1,0:T(8,128)(2,1)S(1)}, u32[]{:S(2)}, u32[]{:S(2)}) collective-permute-start(bf16[144,384]{1,0:T(8,128)(2,1)S(1)} %get-tuple-element.70), channel_id=1, source_target_pairs={{0,3},{1,2},{2,1},{3,0},{4,7},{5,6},{6,5},{7,4},{8,11},{9,10},{10,... | collective-permute-start | bytes 331784 | tf_op jit(solution)/shard_map/ppermute | solution.py:51
  156.5 9.9 %collective-permute-start.3 = (bf16[144,384]{1,0:T(8,128)(2,1)S(1)}, bf16[144,384]{1,0:T(8,128)(2,1)S(1)}, u32[]{:S(2)}, u32[]{:S(2)}) collective-permute-start(bf16[144,384]{1,0:T(8,128)(2,1)S(1)} %get-tuple-element.71), channel_id=1, source_target_pairs={{0,4},{1,5},{2,6},{3,7},{4,0},{5,1},{6,2},{7,3},{8,12},{9,13},{10,... | collective-permute-start | bytes 331784 | tf_op jit(solution)/shard_map/ppermute | solution.py:51
  159.2 15.7 %collective-permute-start.4 = (bf16[144,384]{1,0:T(8,128)(2,1)S(1)}, bf16[144,384]{1,0:T(8,128)(2,1)S(1)}, u32[]{:S(2)}, u32[]{:S(2)}) collective-permute-start(bf16[144,384]{1,0:T(8,128)(2,1)S(1)} %get-tuple-element.72), channel_id=1, source_target_pairs={{0,5},{1,4},{2,7},{3,6},{4,1},{5,0},{6,3},{7,2},{8,13},{9,12},{10,... | collective-permute-start | bytes 331784 | tf_op jit(solution)/shard_map/ppermute | solution.py:51
  159.3 15.6 %collective-permute-start.5 = (bf16[144,384]{1,0:T(8,128)(2,1)S(1)}, bf16[144,384]{1,0:T(8,128)(2,1)S(1)}, u32[]{:S(2)}, u32[]{:S(2)}) collective-permute-start(bf16[144,384]{1,0:T(8,128)(2,1)S(1)} %get-tuple-element.73), channel_id=1, source_target_pairs={{0,6},{1,7},{2,4},{3,5},{4,2},{5,3},{6,0},{7,1},{8,14},{9,15},{10,... | collective-permute-start | bytes 331784 | tf_op jit(solution)/shard_map/ppermute | solution.py:51
  161.8 13.1 %collective-permute-start.6 = (bf16[144,384]{1,0:T(8,128)(2,1)S(1)}, bf16[144,384]{1,0:T(8,128)(2,1)S(1)}, u32[]{:S(2)}, u32[]{:S(2)}) collective-permute-start(bf16[144,384]{1,0:T(8,128)(2,1)S(1)} %get-tuple-element.74), channel_id=1, source_target_pairs={{0,7},{1,6},{2,5},{3,4},{4,3},{5,2},{6,1},{7,0},{8,15},{9,14},{10,... | collective-permute-start | bytes 331784 | tf_op jit(solution)/shard_map/ppermute | solution.py:51
  233.5 244.5 %reduce-scatter.3.cloned.1.call-start = ((), (), s32[]{:S(2)}) async-start(), calls=%async_computation.3 | async-start | bytes 7962624 | tf_op jit(solution)/shard_map/reduce_scatter | solution.py:1083
  251.8 10.0 %collective-permute-start.12 = (bf16[144,384]{1,0:T(8,128)(2,1)S(1)}, bf16[144,384]{1,0:T(8,128)(2,1)S(1)}, u32[]{:S(2)}, u32[]{:S(2)}) collective-permute-start(bf16[144,384]{1,0:T(8,128)(2,1)S(1)} %get-tuple-element.96), channel_id=1, source_target_pairs={{0,3},{1,2},{2,1},{3,0},{4,7},{5,6},{6,5},{7,4},{8,11},{9,10},{10,... | collective-permute-start | bytes 331784 | tf_op jit(solution)/shard_map/ppermute | solution.py:51
  251.9 9.9 %collective-permute-start.13 = (bf16[144,384]{1,0:T(8,128)(2,1)S(1)}, bf16[144,384]{1,0:T(8,128)(2,1)S(1)}, u32[]{:S(2)}, u32[]{:S(2)}) collective-permute-start(bf16[144,384]{1,0:T(8,128)(2,1)S(1)} %get-tuple-element.97), channel_id=1, source_target_pairs={{0,4},{1,5},{2,6},{3,7},{4,0},{5,1},{6,2},{7,3},{8,12},{9,13},{10,... | collective-permute-start | bytes 331784 | tf_op jit(solution)/shard_map/ppermute | solution.py:51
  254.1 15.7 %collective-permute-start.14 = (bf16[144,384]{1,0:T(8,128)(2,1)S(1)}, bf16[144,384]{1,0:T(8,128)(2,1)S(1)}, u32[]{:S(2)}, u32[]{:S(2)}) collective-permute-start(bf16[144,384]{1,0:T(8,128)(2,1)S(1)} %get-tuple-element.98), channel_id=1, source_target_pairs={{0,5},{1,4},{2,7},{3,6},{4,1},{5,0},{6,3},{7,2},{8,13},{9,12},{10,... | collective-permute-start | bytes 331784 | tf_op jit(solution)/shard_map/ppermute | solution.py:51
  254.8 15.1 %collective-permute-start.15 = (bf16[144,384]{1,0:T(8,128)(2,1)S(1)}, bf16[144,384]{1,0:T(8,128)(2,1)S(1)}, u32[]{:S(2)}, u32[]{:S(2)}) collective-permute-start(bf16[144,384]{1,0:T(8,128)(2,1)S(1)} %get-tuple-element.99), channel_id=1, source_target_pairs={{0,6},{1,7},{2,4},{3,5},{4,2},{5,3},{6,0},{7,1},{8,14},{9,15},{10,... | collective-permute-start | bytes 331784 | tf_op jit(solution)/shard_map/ppermute | solution.py:51
  256.5 13.3 %collective-permute-start.16 = (bf16[144,384]{1,0:T(8,128)(2,1)S(1)}, bf16[144,384]{1,0:T(8,128)(2,1)S(1)}, u32[]{:S(2)}, u32[]{:S(2)}) collective-permute-start(bf16[144,384]{1,0:T(8,128)(2,1)S(1)} %get-tuple-element.100), channel_id=1, source_target_pairs={{0,7},{1,6},{2,5},{3,4},{4,3},{5,2},{6,1},{7,0},{8,15},{9,14},{10,... | collective-permute-start | bytes 331784 | tf_op jit(solution)/shard_map/ppermute | solution.py:51
  326.0 230.9 %all-gather.8.cloned.1.call-start = ((), (), s32[]{:S(2)}) async-start(), calls=%async_computation.5 | async-start | bytes 3981312 | tf_op jit(solution)/shard_map/all_gather | solution.py:1145
  326.0 14.1 %collective-permute-start.8 = (bf16[384,1152]{1,0:T(8,128)(2,1)}, bf16[384,1152]{1,0:T(8,128)(2,1)}, u32[]{:S(2)}, u32[]{:S(2)}) collective-permute-start(bf16[384,1152]{1,0:T(8,128)(2,1)} %get-tuple-element.81), channel_id=1, source_target_pairs={{0,1},{1,0},{2,3},{3,2},{4,5},{5,4},{6,7},{7,6},{8,9},{9,8},{10,11... | collective-permute-start | bytes 2654216 | tf_op jit(solution)/shard_map/ppermute | solution.py:51
  338.3 12.0 %collective-permute-start.23 = (f32[8,2304]{1,0:T(8,128)S(1)}, f32[8,2304]{1,0:T(8,128)S(1)}, u32[]{:S(2)}, u32[]{:S(2)}) collective-permute-start(f32[8,2304]{1,0:T(8,128)S(1)} %convert_convert_fusion), channel_id=1, source_target_pairs={{0,1},{1,0},{2,3},{3,2},{4,5},{5,4},{6,7},{7,6},{8,9},{9,8},{10,11... | collective-permute-start | bytes 221192 | tf_op jit(solution)/shard_map/ppermute | solution.py:51
  350.3 10.1 %collective-permute-start.24 = (f32[8,2304]{1,0:T(8,128)S(1)}, f32[8,2304]{1,0:T(8,128)S(1)}, u32[]{:S(2)}, u32[]{:S(2)}) collective-permute-start(f32[8,2304]{1,0:T(8,128)S(1)} %fusion.16), channel_id=1, source_target_pairs={{0,2},{1,3},{2,0},{3,1},{4,6},{5,7},{6,4},{7,5},{8,10},{9,11},{10,... | collective-permute-start | bytes 221192 | tf_op jit(solution)/shard_map/ppermute | solution.py:51
  355.4 10.5 %collective-permute-start.21 = (f32[8,2304]{1,0:T(8,128)S(1)}, f32[8,2304]{1,0:T(8,128)S(1)}, u32[]{:S(2)}, u32[]{:S(2)}) collective-permute-start(f32[8,2304]{1,0:T(8,128)S(1)} %fusion.15), channel_id=1, source_target_pairs={{0,2},{1,3},{2,0},{3,1},{4,6},{5,7},{6,4},{7,5},{8,10},{9,11},{10,... | collective-permute-start | bytes 221192 | tf_op jit(solution)/shard_map/ppermute | solution.py:51
  362.6 25.5 %collective-permute-start.30 = (bf16[4,144,1152]{2,1,0:T(8,128)(2,1)}, bf16[4,144,1152]{2,1,0:T(8,128)(2,1)S(1)}, u32[]{:S(2)}, u32[]{:S(2)}) collective-permute-start(bf16[4,144,1152]{2,1,0:T(8,128)(2,1)} %get-tuple-element.114), channel_id=1, source_target_pairs={{0,1},{1,0},{2,3},{3,2},{4,5},{5,4},{6,7},{7,6},{8,9},{9,8},{10,11... | collective-permute-start | bytes 3981320 | tf_op jit(solution)/shard_map/ppermute | solution.py:51
  364.4 18.2 %collective-permute-start.26 = (bf16[2,144,768]{2,1,0:T(8,128)(2,1)}, bf16[2,144,768]{2,1,0:T(8,128)(2,1)S(1)}, u32[]{:S(2)}, u32[]{:S(2)}) collective-permute-start(bf16[2,144,768]{2,1,0:T(8,128)(2,1)} %copy-done.23), channel_id=1, source_target_pairs={{0,8},{8,0},{16,24},{24,16},{1,9},{9,1},{17,25},{25,17},{2,10},{10... | collective-permute-start | bytes 1327112 | tf_op jit(solution)/shard_map/ppermute | solution.py:51
  364.4 19.8 %collective-permute-start.28 = (bf16[2,144,768]{2,1,0:T(8,128)(2,1)}, bf16[2,144,768]{2,1,0:T(8,128)(2,1)S(1)}, u32[]{:S(2)}, u32[]{:S(2)}) collective-permute-start(bf16[2,144,768]{2,1,0:T(8,128)(2,1)} %copy-done.22), channel_id=1, source_target_pairs={{0,16},{8,24},{16,0},{24,8},{1,17},{9,25},{17,1},{25,9},{2,18},{10... | collective-permute-start | bytes 1327112 | tf_op jit(solution)/shard_map/ppermute | solution.py:51
  365.9 10.3 %collective-permute-start.22 = (f32[8,2304]{1,0:T(8,128)S(1)}, f32[8,2304]{1,0:T(8,128)S(1)}, u32[]{:S(2)}, u32[]{:S(2)}) collective-permute-start(f32[8,2304]{1,0:T(8,128)S(1)} %add.102), channel_id=1, source_target_pairs={{0,4},{1,5},{2,6},{3,7},{4,0},{5,1},{6,2},{7,3},{8,12},{9,13},{10,... | collective-permute-start | bytes 221192 | tf_op jit(solution)/shard_map/ppermute | solution.py:51
  384.3 12.5 %collective-permute-start.29 = (bf16[144,768]{1,0:T(8,128)(2,1)S(1)}, bf16[144,768]{1,0:T(8,128)(2,1)S(1)}, u32[]{:S(2)}, u32[]{:S(2)}) collective-permute-start(bf16[144,768]{1,0:T(8,128)(2,1)S(1)} %slice_bitcast_fusion), channel_id=1, source_target_pairs={{0,8},{8,0},{16,24},{24,16},{1,9},{9,1},{17,25},{25,17},{2,10},{10... | collective-permute-start | bytes 663560 | tf_op jit(solution)/shard_map/ppermute | solution.py:51
  403.7 58.2 %collective-permute-start.39 = (bf16[576,1152]{1,0:T(8,128)(2,1)S(1)}, bf16[576,1152]{1,0:T(8,128)(2,1)S(1)}, u32[]{:S(2)}, u32[]{:S(2)}) collective-permute-start(bf16[576,1152]{1,0:T(8,128)(2,1)S(1)} %broadcast_select_fusion.4), channel_id=1, source_target_pairs={{0,2},{1,3},{2,0},{3,1},{4,6},{5,7},{6,4},{7,5},{8,10},{9,11},{10,... | collective-permute-start | bytes 3981320 | tf_op jit(solution)/shard_map/ppermute | solution.py:51
  410.1 47.8 %collective-permute-start.36 = (bf16[72,1152]{1,0:T(8,128)(2,1)S(1)}, bf16[72,1152]{1,0:T(8,128)(2,1)S(1)}, u32[]{:S(2)}, u32[]{:S(2)}) collective-permute-start(bf16[72,1152]{1,0:T(8,128)(2,1)S(1)} %add_convert_fusion.8), channel_id=1, source_target_pairs={{0,4},{1,5},{2,6},{3,7},{4,0},{5,1},{6,2},{7,3},{8,12},{9,13},{10,... | collective-permute-start | bytes 497672 | tf_op jit(solution)/shard_map/ppermute | solution.py:51
  463.6 87.4 %collective-permute-start.40 = (bf16[576,1152]{1,0:T(8,128)(2,1)}, bf16[576,1152]{1,0:T(8,128)(2,1)}, u32[]{:S(2)}, u32[]{:S(2)}) collective-permute-start(bf16[576,1152]{1,0:T(8,128)(2,1)} %add_convert_fusion.1), channel_id=1, source_target_pairs={{0,4},{1,5},{2,6},{3,7},{4,0},{5,1},{6,2},{7,3},{8,12},{9,13},{10,... | collective-permute-start | bytes 3981320 | tf_op jit(solution)/shard_map/ppermute | solution.py:51
  468.2 84.9 %collective-permute-start.38 = (bf16[144,1152]{1,0:T(8,128)(2,1)}, bf16[144,1152]{1,0:T(8,128)(2,1)}, u32[]{:S(2)}, u32[]{:S(2)}) collective-permute-start(bf16[144,1152]{1,0:T(8,128)(2,1)} %pad_maximum_fusion.4), channel_id=1, source_target_pairs={{0,1},{1,0},{2,3},{3,2},{4,5},{5,4},{6,7},{7,6},{8,9},{9,8},{10,11... | collective-permute-start | bytes 995336 | tf_op jit(solution)/shard_map/ppermute | solution.py:51
  485.0 69.2 %collective-permute-start.17 = (f32[8,2304]{1,0:T(8,128)S(1)}, f32[8,2304]{1,0:T(8,128)S(1)}, u32[]{:S(2)}, u32[]{:S(2)}) collective-permute-start(f32[8,2304]{1,0:T(8,128)S(1)} %convert_convert_fusion.2), channel_id=1, source_target_pairs={{0,1},{1,0},{2,3},{3,2},{4,5},{5,4},{6,7},{7,6},{8,9},{9,8},{10,11... | collective-permute-start | bytes 221192 | tf_op jit(solution)/shard_map/ppermute | solution.py:51
  553.0 31.3 %collective-permute-start.41 = (bf16[576,1152]{1,0:T(8,128)(2,1)S(1)}, bf16[576,1152]{1,0:T(8,128)(2,1)}, u32[]{:S(2)}, u32[]{:S(2)}) collective-permute-start(bf16[576,1152]{1,0:T(8,128)(2,1)S(1)} %add_convert_fusion), channel_id=1, source_target_pairs={{0,2},{1,3},{2,0},{3,1},{4,6},{5,7},{6,4},{7,5},{8,10},{9,11},{10,... | collective-permute-start | bytes 3981320 | tf_op jit(solution)/shard_map/ppermute | solution.py:51
  554.2 29.9 %collective-permute-start.18 = (f32[8,2304]{1,0:T(8,128)S(1)}, f32[8,2304]{1,0:T(8,128)S(1)}, u32[]{:S(2)}, u32[]{:S(2)}) collective-permute-start(f32[8,2304]{1,0:T(8,128)S(1)} %fusion.14), channel_id=1, source_target_pairs={{0,2},{1,3},{2,0},{3,1},{4,6},{5,7},{6,4},{7,5},{8,10},{9,11},{10,... | collective-permute-start | bytes 221192 | tf_op jit(solution)/shard_map/ppermute | solution.py:51
  587.2 30.3 %collective-permute-start.42 = (bf16[288,2304]{1,0:T(8,128)(2,1)}, bf16[288,2304]{1,0:T(8,128)(2,1)}, u32[]{:S(2)}, u32[]{:S(2)}) collective-permute-start(bf16[288,2304]{1,0:T(8,128)(2,1)} %pad_maximum_fusion), channel_id=1, source_target_pairs={{0,1},{1,0},{2,3},{3,2},{4,5},{5,4},{6,7},{7,6},{8,9},{9,8},{10,11... | collective-permute-start | bytes 3981320 | tf_op jit(solution)/shard_map/ppermute | solution.py:51
  609.7 21.0 %collective-permute-start.43 = (bf16[576,1152]{1,0:T(8,128)(2,1)S(1)}, bf16[576,1152]{1,0:T(8,128)(2,1)}, u32[]{:S(2)}, u32[]{:S(2)}) collective-permute-start(bf16[576,1152]{1,0:T(8,128)(2,1)S(1)} %get-tuple-element.134), channel_id=1, source_target_pairs={{0,1},{1,0},{2,3},{3,2},{4,5},{5,4},{6,7},{7,6},{8,9},{9,8},{10,11... | collective-permute-start | bytes 3981320 | tf_op jit(solution)/shard_map/ppermute | solution.py:51
  (61 other events, 984.9 us)
Sparse Core Ops, SparseCore 0:
  12.8 139.6 all-gather.5
  233.7 109.2 reduce-scatter.4
  345.9 105.2 reduce-scatter.2
  453.2 84.7 all-gather.7

commit v3 on v2

--- a/solution.py
+++ b/solution.py
@@ -51,10 +51,6 @@
     return lax.ppermute(array, axis, [(i, i ^ by) for i in range(size)])
 
 
-def after(array, *others):
-    return lax.optimization_barrier((array,) + others)[0]
-
-
 def frequencies(steps, entries):
     half = entries // 2
     ladder = jnp.exp(-math.log(10000.0) * lax.iota(jnp.int32, half) / half)
@@ -122,20 +118,19 @@
     def slot(self, name):
         return self.known.setdefault(name, len(self.known))
 
-    def copy(self, name, source, target, to):
-        slot = self.slot(name)
+    def copy(self, name, source, target, to, landed=None):
         return pltpu.make_async_remote_copy(
             src_ref=source,
             dst_ref=target,
-            send_sem=self.sent.at[slot],
-            recv_sem=self.got.at[slot],
+            send_sem=self.sent.at[self.slot(name)],
+            recv_sem=self.got.at[self.slot(landed or name)],
             device_id=to,
             device_id_type=pl.DeviceIdType.MESH,
         )
 
-    def start(self, name, source, target, to, when=None):
+    def start(self, name, source, target, to, when=None, landed=None):
         def make():
-            return self.copy(name, source, target, to)
+            return self.copy(name, source, target, to, landed)
 
         self.started.append((make, when))
         if when is None:
@@ -204,7 +199,7 @@
 
 def front_body(
     shards, chips, heads, items_ref, keep_ref, x_ref, c_ref, spec_ref, temb_ref, ada_ref, qkvw_ref,
-    outw_ref, xs_ref, cs_ref, hot_ref, info_ref, perm_ref, mod_ref, cond_ref, low_ref, dm_ref, h_ref,
+    outw_ref, xs_ref, cs_ref, hot_ref, info_ref, mark_ref, perm_ref, mod_ref, cond_ref, low_ref, wave_ref, dm_ref, h_ref,
     qkv_ref, wh_ref, wo_ref, x_all, spec_all, temb_all, part_own, part_got, hots, dms, wh_all, wo_all,
     h_all, ada_s, qkvw_s, local, sent, got,
 ):
@@ -268,6 +263,7 @@
     hots[0] = kept * ((at >= start) & (at < end)).astype(F32)
     first = (lax.broadcasted_iota(I32, (slots, LANES), 1) * width).astype(F32)
     mine = ((first >= start) & (first < end)).astype(F32)
+    mark_ref[...] = mine
     which = lax.broadcasted_iota(I32, (slots, LANES), 0).astype(F32)
     info_ref[0:1, :] = jnp.sum(mine * which, axis=0, keepdims=True).astype(I32)
     info_ref[1:2, :] = (jnp.sum(mine * start, axis=0, keepdims=True) / width).astype(I32)
@@ -286,6 +282,8 @@
         @pl.when(f == shard)
         def _():
             cond_ref[...] = condition[:, shard * rows : (shard + 1) * rows]
+            freqs = temb_ref.shape[0]
+            wave_ref[...] = spectra[:, shard * freqs : (shard + 1) * freqs].astype(F32)
 
     values = cond_ref[...]
     lifted = (values / (1.0 + jnp.exp(-values))).astype(BF16)
@@ -732,108 +730,370 @@
         other_ref[k] = grad[base + 1 - c]
 
 
-def qkv_back_body(rows, outs, blocks, ids_ref, h_ref, d_ref, w_ref, *refs):
-    n = len(outs)
-    dh_ref, g_refs, (acc, low, sems) = refs[0], refs[1 : 1 + n], refs[1 + n :]
-    f = ids_ref[0]
-    step = pl.program_id(0)
-    per, _, size = h_ref.shape
-    width = BLOCK // blocks
-    for i in range(per):
-        piece = nt(d_ref[i], w_ref[...]).astype(BF16)
-        dh_ref[:, i] = piece.reshape(blocks, width, size)
-    part = tn(h_ref[...].reshape(per * BLOCK, size), d_ref[...].reshape(per * BLOCK, -1))
-
-    @pl.when(step == 0)
-    def _():
-        acc[...] = part
-
-    @pl.when(step > 0)
-    def _():
-        acc[...] += part
-
-    @pl.when(step == pl.num_programs(0) - 1)
-    def _():
-        low[...] = acc[...].astype(BF16)
-        todo = []
-        for ref, (ks, start, height) in zip(g_refs, outs):
-            for i, k in enumerate(ks):
-                at = pl.multiple_of(lax.bitwise_xor(f, k) * rows + start, 16)
-                todo.append((low.at[pl.ds(at, height)], ref.at[i]))
-        for copy in fetch(todo, sems):
-            copy.wait()
-
-
-def last_body(width, info_ref, mod_ref, x_ref, dx_ref, dh_ref, perm_ref, o_ref, sum_ref, held):
+def stream_back_body(
+    shards, chips, heads, per, h_ref, gs_ref, d_ref, wh_ref, mod_ref, mine_ref, x_ref, dx_ref, perm_ref,
+    gm_ref, o_ref, sum_ref, g_ref, go_ref, give, take, keep, came, h_s, acc, low, others, out_in, out_low,
+    out_got, total, held, by_unit, local, sent, got,
+):
+    f, b = lax.axis_index("fsdp"), lax.axis_index("blk")
+    z, c = b // 2, b % 2
+    pair = b + 1 - 2 * c
+    width = BLOCK // (2 * chips)
+    units = d_ref.shape[0]
     count, size = x_ref.shape
-    sum_ref[...] = jnp.zeros_like(sum_ref)
+    wide = wh_ref.shape[1]
+    own = heads // (2 * chips)
+    head_size = size // heads
+    rows = low.shape[1]
+    steps = units // per
+    routes = Routes(sent, got)
+
+    def load(i):
+        return pltpu.make_async_copy(
+            h_ref.at[pl.ds(i * per, per)], h_s.at[i % 2], local.at[i % 2]
+        )
+
+    load(0).start()
+    greet(shards, chips)
+    routes.start("out", gs_ref, out_in, {"blk": pair})
+
+    def partial(device, target):
+        at = pl.ds(pl.multiple_of(device * width, width), width)
+        grads = d_ref[:, at, :].reshape(count, wide)
+        for col in range(0, size, 3 * LANES):
+            target[:, col : col + 3 * LANES] = nt(
+                grads, wh_ref[col : col + 3 * LANES, :]
+            ).astype(BF16)
+
+    def route(side, t):
+        if side == 0:
+            chip = chips - 1 - t
+            return chip, z < chip, z > 0
+        return t, z > t, z < chips - 1
+
+    def onward(side, t, chip, when):
+        if side == 0:
+            slot, to = chip, b + 2
+        else:
+            slot, to = chip + (chips - chip) * (z - 1 == chip).astype(I32), b - 2
+        routes.start(("sum", side, t), keep.at[chip], came.at[slot], {"blk": to}, when)
+
+    def join(chip, slot=None):
+        value = keep[chip].astype(F32) + take[chip].astype(F32)
+        if slot is not None:
+            value = value + came[slot].astype(F32)
+        keep[chip] = value.astype(BF16)
+
+    for t in range(chips - 1):
+        for side in range(2):
+            chip, passes, inside = route(side, t)
+
+            @pl.when(passes)
+            def _():
+                partial(chip * 2 + 1 - c, give.at[chip])
+
+            routes.start(("pair", side, t), give.at[chip], take.at[chip], {"blk": pair}, passes)
+
+            @pl.when(passes)
+            def _():
+                partial(chip * 2 + c, keep.at[chip])
+
+            first = passes & jnp.logical_not(inside)
+            routes.arrive(("pair", side, t), take.at[chip], first)
+
+            pl.when(first)(lambda: join(chip))
+            onward(side, t, chip, first)
+
+    partial(z * 2 + 1 - c, give.at[z])
+    routes.start(("pair", "own"), give.at[z], take.at[z], {"blk": pair})
+    partial(z * 2 + c, keep.at[z])
+
+    def gather(i):
+        if i + 1 < steps:
+            load(i + 1).start()
+        load(i).wait()
+        part = tn(
+            h_s[i % 2].reshape(per * BLOCK, size),
+            d_ref[i * per : (i + 1) * per].reshape(per * BLOCK, wide),
+        )
+        if i:
+            acc[...] += part
+        else:
+            acc[...] = part
+
+    for t in range(max(chips - 1, steps)):
+        if t < steps:
+            gather(t)
+        if t == steps - 1:
+            packed = jnp.concatenate(
+                [acc[:, i * LANES : i * LANES + head_size] for i in range(3 * own)], axis=1
+            )
+            low[...] = packed.astype(BF16).reshape(low.shape)
+            for k in range(1, shards):
+                other = flip(f, k)
+                routes.start(("grad", k), low.at[other], others.at[k], {"fsdp": other})
+        if t == 0:
+            routes.arrive("out", out_in)
+            out_low[...] = (gm_ref[...].astype(F32) + out_in[...].astype(F32)).astype(BF16)
+            for k in range(1, shards):
+                routes.start(("out", k), out_low.at[k], out_got.at[k], {"fsdp": flip(f, k)})
+        if t >= chips - 1:
+            continue
+        for near, side in ((True, 0), (True, 1), (False, 1), (False, 0)):
+            chip, passes, inside = route(side, t)
+            when = passes & inside & ((z < chips // 2) == near)
+            routes.arrive(("pair", side, t), take.at[chip], when)
+            routes.arrive(("sum", side, t), came.at[chip], when)
+            pl.when(when)(lambda: join(chip, chip))
+            onward(side, t, chip, when)
+
+    grad, grad_out = low[f].astype(F32), out_low[0].astype(F32)
+    for k in range(1, shards):
+        routes.arrive(("grad", k), others.at[k])
+        grad = grad + others[k].astype(F32)
+        routes.arrive(("out", k), out_got.at[k])
+        grad_out = grad_out + out_got[k].astype(F32)
+    g_ref[...] = grad.astype(BF16)
+    go_ref[...] = grad_out.astype(BF16)
+
+    routes.arrive(("pair", "own"), take.at[z])
+    total[...] = keep[z].astype(F32) + take[z].astype(F32)
+    for t in range(chips - 1):
+        for side in range(2):
+            chip, _, inside = route(side, t)
+            slot = chip if side == 0 else chips
+            here = (z == chip) & inside
+            routes.arrive(("sum", side, t), came.at[slot], here)
+
+            @pl.when(here)
+            def _():
+                total[...] += came[slot].astype(F32)
+
+    by_unit[...] = jnp.zeros_like(by_unit)
 
     def one(u):
         rows = pl.ds(pl.multiple_of(u * width, width), width)
-        slot = info_ref[0, u]
         scale = mod_ref[pl.ds(u, 1), size : 2 * size]
         normed, spread = normal(x_ref[rows, :].astype(F32))
-        grad = dh_ref[rows, :].astype(F32)
-        sum_ref[pl.ds(slot, 1), 0:size] += jnp.sum(grad, axis=0, keepdims=True)
-        sum_ref[pl.ds(slot, 1), size : 2 * size] += jnp.sum(grad * normed, axis=0, keepdims=True)
+        grad = total[rows, :]
+        by_unit[pl.ds(u, 1), 0:size] = jnp.sum(grad, axis=0, keepdims=True)
+        by_unit[pl.ds(u, 1), size : 2 * size] = jnp.sum(grad * normed, axis=0, keepdims=True)
         dx = dx_ref[rows, :] + normal_back(grad * (1.0 + scale), normed, spread)
         held[rows, :] = dx.astype(BF16)
 
-    each(count // width, one)
+    each(units, one, 3)
     o_ref[...] = tn(perm_ref[...], held[...]).astype(BF16)
-
-
-def reduce_plan(shards, rows):
-    if shards == 4:
-        half = rows // 2
-        return [
-            ((0, 2), 0, half),
-            ((1, 3), 0, half),
-            ((0, 1), half, half),
-            ((2, 3), half, half),
-        ]
-    return [(tuple(range(shards)), 0, rows)]
-
-
-def add(left, right):
-    return (left.astype(F32) + right.astype(F32)).astype(BF16)
-
-
-def reduce_rows(pieces, shards):
-    if shards == 4:
-        keep_a, send_a, keep_b, send_b = pieces
-        sum_a = add(keep_a, swap(send_a, "fsdp", 1))
-        sum_b = add(keep_b, swap(send_b, "fsdp", 2))
-        return (
-            add(sum_a[0], swap(sum_a[1], "fsdp", 2)),
-            add(sum_b[0], swap(sum_b[1], "fsdp", 1)),
+    sum_ref[...] = lax.dot_general(
+        mine_ref[:, : by_unit.shape[0]], by_unit[...], (((1,), (0,)), ((), ())), precision=HIGH,
+        preferred_element_type=F32,
+    )
+    routes.finish()
+
+
+def finish_body(
+    shards, chips, fc_ref, ada_ref, go_ref, gq_ref, one_ref, two_ref, gate_ref, cond_ref, tot_ref, gqa_ref,
+    dm_ref, dc_ref, mine, up, inner_in, result, other, gq_all, sum_own, sum_pair, sums, mods, conds, ada_s,
+    local, sent, got,
+):
+    f, b = lax.axis_index("fsdp"), lax.axis_index("blk")
+    z, c = b // 2, b % 2
+    pair = b + 1 - 2 * c
+    count = mine.shape[0]
+    slots, wider = sum_own.shape
+    size = wider // 6
+    routes = Routes(sent, got)
+    loads = fetch([(fc_ref, mine.at[0 : count - 1]), (ada_ref, ada_s)], local)
+    greet(shards, chips)
+
+    sum_own[:, 0 : 2 * size] = one_ref[...]
+    sum_own[:, 2 * size : 3 * size] = gate_ref[:, 0:size]
+    sum_own[:, 3 * size : 5 * size] = two_ref[...]
+    sum_own[:, 5 * size : 6 * size] = gate_ref[:, size : 2 * size]
+    routes.start("sum", sum_own, sum_pair, {"blk": pair})
+    gq_all[b] = gq_ref[...]
+
+    def line(side, s, send):
+        away = s - 1 if send else s
+        chip = z - away if side == 0 else z + away
+        ahead = z + 1 < chips if side == 0 else z > 0
+        known = z >= away if side == 0 else z + away < chips
+        return chip, {"blk": b + 2 if side == 0 else b - 2}, known & ahead if send else known
+
+    def send(name, s, place):
+        for side in range(2):
+            chip, to, when = line(side, s, True)
+            routes.start((name, side, s), place(chip), place(chip), to, when)
+
+    def take(name, s, place):
+        for side in range(2):
+            chip, _, when = line(side, s, False)
+            routes.arrive((name, side, s), place(chip), when)
+        if s + 1 < chips:
+            send(name, s + 1, place)
+
+    def head(chip):
+        return gq_all.at[chip * 2 + c]
+
+    send("head", 1, head)
+    routes.start("head pair", gq_all.at[b], gq_all.at[b], {"blk": pair})
+
+    half = chips // 2
+    right = z // half
+    inner, outer = {"blk": b + 2 - 4 * right}, {"blk": b - 2 + 4 * right}
+    ends = (z > 0) & (z < chips - 1)
+    middle = (z == half - 1) | (z == half)
+    edge = jnp.logical_not(middle)
+
+    def inward(i, when):
+        routes.start(("up", i), mine.at[i], up.at[i], inner, when & edge)
+        routes.start(("across", i), mine.at[i], inner_in.at[i], inner, when & middle, ("in", i))
+
+    routes.arrive("sum", sum_pair)
+    sums[z] = (sum_own[...] + sum_pair[...]).astype(BF16).astype(F32)
+    send("small", 1, lambda chip: sums.at[chip])
+    mine[count - 1] = go_ref[...]
+    loads[0].wait()
+    ahead = min(3, count)
+    for i in range(ahead):
+        inward(i, jnp.logical_not(ends))
+
+    def combine():
+        total = sums[0]
+        for chip in range(1, chips):
+            total = total + sums[chip]
+        mods[f] = total.astype(BF16).astype(F32)
+        for k in range(1, shards):
+            routes.start(("mod", k), mods.at[f], mods.at[f], {"fsdp": flip(f, k)})
+
+    def condition():
+        for k in range(1, shards):
+            routes.arrive(("mod", k), mods.at[flip(f, k)])
+        dm_ref[...] = mods[...]
+        loads[1].wait()
+        grad = nt(mods[...].reshape(shards * slots, wider).astype(BF16), ada_s[...])
+        values = cond_ref[...]
+        gate = 1.0 / (1.0 + jnp.exp(-values))
+        conds[f] = grad * (gate + values * gate * (1.0 - gate))
+        for k in range(1, shards):
+            routes.start(("cond", k), conds.at[f], conds.at[f], {"fsdp": flip(f, k)})
+
+    def conditions():
+        for k in range(1, shards):
+            routes.arrive(("cond", k), conds.at[flip(f, k)])
+        dc_ref[...] = conds[...]
+
+    jobs = []
+    for s in range(1, chips):
+        jobs.append(lambda s=s: take("small", s, lambda chip: sums.at[chip]))
+    jobs += [combine, condition, conditions]
+    heads = [lambda s=s: take("head", s, head) for s in range(1, chips)]
+
+    def forward(i):
+        routes.arrive(("up", i), up.at[i], ends)
+
+        @pl.when(ends)
+        def _():
+            mine[i] = (mine[i].astype(F32) + up[i].astype(F32)).astype(BF16)
+
+        inward(i, ends)
+        if i + ahead < count:
+            inward(i + ahead, jnp.logical_not(ends))
+
+    def back(i):
+        routes.arrive(("in", i), inner_in.at[i])
+
+        @pl.when(middle)
+        def _():
+            result[i] = (mine[i].astype(F32) + inner_in[i].astype(F32)).astype(BF16)
+
+        @pl.when(edge)
+        def _():
+            result[i] = inner_in[i]
+
+        routes.start(("down", i), result.at[i], inner_in.at[i], outer, ends, ("in", i))
+        routes.start(("pair", i), result.at[i], other.at[i], {"blk": pair})
+
+    for i in range(count + 1):
+        if i < count:
+            forward(i)
+        if i:
+            back(i - 1)
+            if jobs and i > 1:
+                jobs.pop(0)()
+            if heads and i % 2 == 1 and i > 2:
+                heads.pop(0)()
+    for job in jobs + heads:
+        job()
+    for s in range(1, chips):
+        for side in range(2):
+            chip, _, when = line(side, s, False)
+            routes.start(("head pair", side, s), head(chip), head(chip), {"blk": pair}, when)
+    copies = fetch([(result, tot_ref.at[c])], local)
+    for i in range(count):
+        routes.arrive(("pair", i), other.at[i])
+    copies += fetch([(other, tot_ref.at[1 - c])], local, 1)
+    routes.arrive("head pair", gq_all.at[pair])
+    for s in range(1, chips):
+        for side in range(2):
+            chip, _, when = line(side, s, False)
+            routes.arrive(("head pair", side, s), gq_all.at[chip * 2 + 1 - c], when)
+    copies += fetch([(gq_all, gqa_ref)], local, 2)
+    routes.finish()
+    for copy in copies:
+        copy.wait()
+
+
+def unfold_body(
+    shards, low_ref, wave_ref, dm_ref, dc_ref, tot_ref, gq_ref, temb_ref, ada_ref, qkv_ref, out_ref,
+    fc1_ref, fc2_ref, ada_s, qkv_s, out_s, fc1_s, fc2_s, sems,
+):
+    _, count, rows, size = tot_ref.shape
+    slots = dm_ref.shape[1]
+    copies = []
+
+    def leave(source, target):
+        copy = pltpu.make_async_copy(source, target, sems.at[len(copies)])
+        copy.start()
+        copies.append(copy)
+
+    hidden = fc1_s.shape[1]
+    part = hidden // shards // 2
+    height = fc1_s.shape[0]
+    blocks = hidden // 2 // size
+    per = height // rows
+    for core in range(2):
+        for i in range(blocks * per):
+            piece = tot_ref[core, i].astype(F32)
+            block, at = i // per, (i % per) * rows
+            for j in range(size // part):
+                column = (block * (size // part) + j) * 2 * part + core * part
+                fc1_s[at : at + rows, column : column + part] = piece[:, j * part : (j + 1) * part]
+        rest = count - 1 - blocks * per
+        for i in range(rest):
+            at = (core * rest + i) * rows
+            fc2_s[at : at + rows, :] = tot_ref[core, blocks * per + i].astype(F32)
+        out_s[core * rows : (core + 1) * rows, :] = tot_ref[core, count - 1].astype(F32)
+    leave(fc1_s, fc1_ref)
+    leave(fc2_s, fc2_ref)
+    leave(out_s, out_ref)
+    devices, _, packed = gq_ref.shape
+    narrow = packed // 3
+    for p in range(3):
+        for i in range(devices):
+            at = p * size + i * narrow
+            qkv_s[:, at : at + narrow] = gq_ref[i, :, p * narrow : (p + 1) * narrow].astype(F32)
+    leave(qkv_s, qkv_ref)
+    grads = dm_ref[...].reshape(shards * slots, -1).astype(BF16)
+    ada_s[...] = tn(low_ref[...], grads)
+    leave(ada_s, ada_ref)
+    step = dc_ref.shape[2]
+    for i in range(shards):
+        temb_ref[:, i * step : (i + 1) * step] = lax.dot_general(
+            wave_ref[...], dc_ref[i], (((0,), (0,)), ((), ())), precision=HIGH,
+            preferred_element_type=F32,
         )
-    (pieces,) = pieces
-    total = pieces[0]
-    for k in range(1, shards):
-        total = add(total, swap(pieces[k], "fsdp", k))
-    half = total.shape[0] // 2
-    return total[:half], total[half:]
-
-
-def sum_chips(pair, chips):
-    one, two = pair
-    if chips == 4:
-        even = (lax.axis_index("blk") // 2) % 2 == 0
-        send, keep = jnp.where(even, two, one), jnp.where(even, one, two)
-        part = add(keep, swap(send, "blk", 2))
-        part = add(part, swap(part, "blk", 4))
-        other = swap(part, "blk", 2)
-        return jnp.where(even, part, other), jnp.where(even, other, part)
-    groups = [[2 * i + core for i in range(chips)] for core in range(2)]
-    both = lax.psum(jnp.concatenate([one, two]), "blk", axis_index_groups=groups)
-    return both[: one.shape[0]], both[one.shape[0] :]
-
-
-def both_cores(array):
-    other = swap(array, "blk", 1)
-    first = lax.axis_index("blk") % 2 == 0
-    return jnp.where(first, array, other), jnp.where(first, other, array)
+    for copy in copies:
+        copy.wait()
 
 
 def on_device(
@@ -896,10 +1156,12 @@
             (VMEM, shape((count, size))),
             (ANY, shape((2, slots, count), F32)),
             (VMEM, shape((8, LANES), I32)),
+            (VMEM, shape((slots, LANES), F32)),
             (VMEM, shape((count, count))),
             (VMEM, shape((padded, wider), F32)),
             (VMEM, shape((shards * slots, ada_rows), F32)),
             (VMEM, shape((shards * slots, ada_rows))),
+            (VMEM, shape((shards * slots, rows), F32)),
             (ANY, shape((2, count, size))),
             (ANY, shape((units, BLOCK, size))),
             (VMEM, shape((units, BLOCK, wide))),
@@ -927,7 +1189,7 @@
         vmem=60,
         collective=0,
     )
-    x_s, c_s, hots, info, perm, mod, condition, lifted, dms, normed, qkv, w_heads, w_out_all = outs
+    x_s, c_s, hots, info, mark, perm, mod, condition, lifted, waves, dms, normed, qkv, w_heads, w_out_all = outs
     w_out_all = w_out_all.reshape(size, size)
 
     mask = head_mask[0]
@@ -1033,7 +1295,6 @@
         [pltpu.VMEM((count, size), BF16), pltpu.VMEM((2 * shards, out_rows, size), BF16)],
         flops=2 * count * size * size,
     )
-    g_out = add(g_out, swap(g_out_send, "blk", 1))
 
     (d_qkv,) = run(
         "attend_back",
@@ -1052,99 +1313,91 @@
         ],
         flops=5 * units * units * BLOCK * BLOCK * wide // 3,
     )
-    per = 4
+    per = 4 if units % 4 == 0 else 1
     rows_qkv = w_qkv.shape[0]
-    outs_qkv = reduce_plan(shards, rows_qkv)
-    outs = run(
-        "qkv_back",
-        functools.partial(qkv_back_body, rows_qkv, outs_qkv, blocks),
-        [
-            (SMEM, ids),
-            (pl.BlockSpec((per, BLOCK, size), lambda i: (i, 0, 0)), normed),
-            (pl.BlockSpec((per, BLOCK, wide), lambda i: (i, 0, 0)), d_qkv),
-            (VMEM, w_heads),
+    n_copies = 4 * chips + 2 * shards + 4
+    grad_tokens, sums_one, g_qkv, g_out = run(
+        "stream_back",
+        functools.partial(stream_back_body, shards, chips, heads, per),
+        [(ANY, normed), (ANY, g_out_send)]
+        + [(VMEM, a) for a in (d_qkv, w_heads, mod, mark, x_s, dx1, perm, g_out)],
+        [
+            (VMEM, shape((count, size))),
+            (VMEM, shape((slots, 2 * size), F32)),
+            (VMEM, shape((rows_qkv, 3 * narrow))),
+            (VMEM, shape((out_rows, size))),
         ],
         [
-            (
-                pl.BlockSpec((blocks, per, width, size), lambda i: (0, i, 0, 0)),
-                shape((blocks, units, width, size)),
-            )
-        ]
-        + [(ANY, shape((len(ks), height, wide))) for ks, _, height in outs_qkv],
-        [
+            pltpu.VMEM((chips, count, size), BF16),
+            pltpu.VMEM((chips, count, size), BF16),
+            pltpu.VMEM((chips, count, size), BF16),
+            pltpu.VMEM((chips + 1, count, size), BF16),
+            pltpu.VMEM((2, per, BLOCK, size), BF16),
             pltpu.VMEM((size, wide), F32),
-            pltpu.VMEM((size, wide), BF16),
-            pltpu.SemaphoreType.DMA((2 * shards,)),
+            pltpu.VMEM((shards, rows_qkv, 3 * narrow), BF16),
+            pltpu.VMEM((shards, rows_qkv, 3 * narrow), BF16),
+            pltpu.VMEM((shards, out_rows, size), BF16),
+            pltpu.VMEM((shards, out_rows, size), BF16),
+            pltpu.VMEM((shards, out_rows, size), BF16),
+            pltpu.VMEM((count, size), F32),
+            pltpu.VMEM((count, size), BF16),
+            pltpu.VMEM((padded, 2 * size), F32),
+            pltpu.SemaphoreType.DMA((2,)),
+            pltpu.SemaphoreType.DMA((n_copies,)),
+            pltpu.SemaphoreType.DMA((n_copies,)),
         ],
         flops=4 * units * BLOCK * size * wide,
-        grid=(units // per,),
-    )
-    d_normed, gq_parts = outs[0], outs[1:]
-    d_normed = lax.psum_scatter(
-        d_normed.reshape(blocks * count, size), "blk", scatter_dimension=0, tiled=True
-    )
-    grad_tokens, sums_one = run(
-        "first_back",
-        functools.partial(last_body, width),
-        [(SMEM, info)] + [(VMEM, a) for a in (mod, x_s, dx1, d_normed, perm)],
-        [(VMEM, shape((count, size))), (VMEM, shape((slots, 2 * size), F32))],
-        [pltpu.VMEM((count, size), BF16)],
-    )
-
-    def over_stream(sums):
-        low = sums.astype(BF16)
-        total = low.astype(F32)
-        for k in (1, 2, 4, 8, 16):
-            if k < blocks:
-                total = total + swap(total, "blk", k)
-        low = total.astype(BF16)
-        return lax.all_gather(low, "fsdp", axis=0, tiled=True)
-
-    gate_all, two_all, one_all = over_stream(sums_gate), over_stream(sums_two), over_stream(sums_one)
-    d_mod = jnp.concatenate(
-        [one_all, gate_all[:, :size], two_all, gate_all[:, size:]], axis=1
-    )
-    grad_ada = tn(lifted, d_mod)
-    _, silu_pull = jax.vjp(lambda v: v / (1.0 + jnp.exp(-v)), condition)
-    (d_condition,) = silu_pull(nt(d_mod, w_ada))
-    d_all = lax.all_gather(d_condition, "fsdp", axis=1, tiled=True)
-    steps = lax.all_gather(timesteps, "fsdp", axis=0, tiled=True)
-    spectra = frequencies(steps.reshape(-1), entries).astype(BF16).astype(F32)
-    grad_temb = lax.dot_general(
-        lax.dynamic_slice_in_dim(spectra, f * rows, rows, axis=1),
-        d_all,
-        (((0,), (0,)), ((), ())),
-        precision=HIGH,
-    )
-
-    cut = fc_rows - w_fc2.shape[0] // 2
-    g1, g2 = sum_chips((g_fc[:cut], g_fc[cut:]), chips)
-    if shards == 4:
-        cut = out_rows // 2
-        pieces = [
-            jnp.stack([g_out[0, :cut], g_out[2, :cut]]),
-            jnp.stack([g_out[1, :cut], g_out[3, :cut]]),
-            g_out[0:2, cut:],
-            g_out[2:4, cut:],
+        vmem=60,
+        collective=1,
+    )
+
+    pieces = fc_rows // out_rows
+    n_copies = 5 * pieces + 10 + 6 * chips + 2 * shards
+    totals, g_qkv, d_mod, d_cond = run(
+        "finish",
+        functools.partial(finish_body, shards, chips),
+        [(ANY, g_fc.reshape(pieces, out_rows, size)), (ANY, w_ada)]
+        + [(VMEM, a) for a in (g_out, g_qkv, sums_one, sums_two, sums_gate, condition)],
+        [
+            (ANY, shape((2, pieces + 1, out_rows, size))),
+            (ANY, shape((blocks, rows_qkv, 3 * narrow))),
+            (VMEM, shape((shards, slots, wider), F32)),
+            (VMEM, shape((shards, shards * slots, ada_rows), F32)),
+        ],
+        [pltpu.VMEM((pieces + 1, out_rows, size), BF16)] * 5
+        + [
+            pltpu.VMEM((blocks, rows_qkv, 3 * narrow), BF16),
+            pltpu.VMEM((slots, wider), F32),
+            pltpu.VMEM((slots, wider), F32),
+            pltpu.VMEM((chips, slots, wider), F32),
+            pltpu.VMEM((shards, slots, wider), F32),
+            pltpu.VMEM((shards, shards * slots, ada_rows), F32),
+            pltpu.VMEM(w_ada.shape, BF16),
+            pltpu.SemaphoreType.DMA((3,)),
+            pltpu.SemaphoreType.DMA((n_copies,)),
+            pltpu.SemaphoreType.DMA((n_copies,)),
+        ],
+        vmem=60,
+        collective=2,
+    )
+    grad_temb, grad_ada, grad_qkv, grad_out, grad_fc1, grad_fc2 = run(
+        "unfold",
+        functools.partial(unfold_body, shards),
+        [(VMEM, a) for a in (lifted, waves, d_mod, d_cond, totals, g_qkv)],
+        [
+            (VMEM, shape(w_temb.shape, F32)),
+            (ANY, shape(w_ada.shape, F32)),
+            (ANY, shape(w_qkv.shape, F32)),
+            (ANY, shape(w_out.shape, F32)),
+            (ANY, shape(w_fc1.shape, F32)),
+            (ANY, shape(w_fc2.shape, F32)),
+        ],
+        [
+            pltpu.VMEM(a.shape, F32) for a in (w_ada, w_qkv, w_out, w_fc1, w_fc2)
         ]
-    else:
-        pieces = [g_out]
-    o_one, o_two = sum_chips(reduce_rows(pieces, shards), chips)
-    first, second = both_cores(jnp.concatenate([o_one, o_two]))
-    grad_out = jnp.concatenate([first, second]).astype(F32)
-    first, second = both_cores(g2)
-    grad_fc2 = jnp.concatenate([first, second]).astype(F32)
-    first, second = both_cores(
-        jnp.concatenate(jnp.split(g1, half // size, axis=0), axis=1)
-    )
-    part = half // shards
-    grad_fc1 = jnp.concatenate(
-        [side[:, i * part : (i + 1) * part] for i in range(shards) for side in (first, second)],
-        axis=1,
-    ).astype(F32)
-    gq = lax.all_gather(jnp.concatenate(reduce_rows(gq_parts, shards)), "blk", axis=0)
-    gq = gq.reshape(blocks, -1, 3, own, LANES)[..., :head_size]
-    grad_qkv = jnp.transpose(gq, (1, 2, 0, 3, 4)).reshape(w_qkv.shape).astype(F32)
+        + [pltpu.SemaphoreType.DMA((5,))],
+        vmem=60,
+    )
     return (
         result,
         grad_tokens,

time: 654 us -> 546 us (0.83)
  Pallas kernels: 269 us -> 471 us
  waiting for transfers between devices: 164 us -> 15.4 us
  starting transfers between devices: 70.5 us -> 26.4 us
  blocking collectives: 39 us -> 0 us
  local copies, waits for them, and re-layouts: 46.5 us -> 11.8 us
  other arithmetic: 30.5 us -> 0.81 us
  matrix products: 7.62 us -> 0 us
    pallas_call x10 -> x11, Pallas kernels: 269 us -> 471 us  [run(): pl.pallas_call(body, out_shape=[o for _, o in outs], in_specs=[s for s, _...]
    ppermute x44 -> x17, waiting for transfers between devices: 164 us -> 15.3 us  [swap(): return lax.ppermute(array, axis, [(i, i ^ by) for i in range(size)])]
    ppermute x44 -> x17, starting transfers between devices: 69.9 us -> 26.4 us  [swap(): return lax.ppermute(array, axis, [(i, i ^ by) for i in range(size)])]
    all_gather x5 -> x0, blocking collectives: 39 us -> none  [the longest x3 20.2 us: over_stream(): return lax.all_gather(low, 'fsdp', axis=0, tiled=True)]
    unnamed x93 -> x47, local copies, waits for them, and re-layouts: 28.7 us -> 9.51 us
    convert_element_type x21 -> x0, other arithmetic: 17.9 us -> none  [the longest x1 4.77 us: on_device(): grad_fc1 = jnp.concatenate([side[:, i * part:(i + 1) * part] for i in ran...]
    select_n x7 -> x0, other arithmetic: 8.24 us -> none  [the longest x3 4.52 us: both_cores(): return (jnp.where(first, array, other), jnp.where(first, other, array))]
    reshape x1 -> x0, local copies, waits for them, and re-layouts: 7.82 us -> none  [on_device(): gq = gq.reshape(blocks, -1, 3, own, LANES)[..., :head_size]]
  transfers between devices with their start and end apart: 48 -> 19, of which waited for: 18 -> 5; matrix products, arithmetic and copies ran while one was open for 10% -> 1% of each run, Pallas kernels for 34% -> 52%
where the time goes in v3:
time: 546 us; the launch traced here: 540 us
  Pallas kernels  471 us (86%)
  starting transfers between devices  26.4 us (5%)
  waiting for transfers between devices  15.4 us (3%)
  between operations  14.7 us (3%)
  local copies, waits for them, and re-layouts  11.8 us (2%)
    pallas_call x11, Pallas kernels, run(): pl.pallas_call(body, out_shape=[o for _, o in outs], in_specs=[s for s, _...  471 us
    ppermute x17, starting transfers between devices, swap(): return lax.ppermute(array, axis, [(i, i ^ by) for i in range(size)])  26.4 us
    ppermute x17, waiting for transfers between devices, swap(): return lax.ppermute(array, axis, [(i, i ^ by) for i in range(size)])  15.3 us
  transfers between devices with their start and end apart: 19, of which 5 were waited for; matrix products, arithmetic and copies ran while one was open for 1% of the time, Pallas kernels for 52%

profile of v3, /device:TPU:1, one launch (start us, length us, event | category | flops | bytes accessed | tf_op | source)
XLA Modules:
  0.0 539.7 jit_solution(13515914669409627540)
XLA Ops:
  7.3 1.7 copy-done.4
  9.1 3.6 pick_half.1
  15.2 102.0 %front.1 = (bf16[384,1152]{1,0:T(8,128)(2,1)}, bf16[384,1152]{1,0:T(8,128)(2,1)}, f32[2,8,384]{2,1,0:T(8,128)}, s32[8,128]{1,0:T(8,128)}, f32[8,128]{1,0:T(8,128...) custom-call(s32[1,384]{1,0:T(1,128)} %constant_dynamic-slice_fusion., ...), custom_call_target="tpu_custom_call" | custom-call | flops 5435817984 | bytes 29156352 | tf_op jit(solution)/shard_map/front/pallas_call | solution.py:32
  118.0 36.4 %attend.1 = (bf16[12,144,256]{2,1,0:T(8,128)(2,1)S(1)}, f32[12,8,256]{2,1,0:T(8,128)S(1)}, bf16[144,384]{1,0:T(8,128)(2,1)S(1)}, bf16[144,384]{1,0:T(8,128)(2,1)...) custom-call(s32[3]{0:T(128)S(1)} %pad_add_fusion.ids_ref, ...), custom_call_target="tpu_custom_call" | custom-call | flops 4831838208 | bytes 6590988 | tf_op jit(solution)/shard_map/attend/pallas_call | solution.py:32
  154.4 0.9 copy-done.16
  155.3 2.1 collective-permute-start
  157.4 1.5 collective-permute-start.1
  159.1 2.7 collective-permute-start.3
  161.9 2.4 collective-permute-start.5
  164.3 4.1 collective-permute-start.6
  168.9 8.6 %collective-permute-done.4.refs_5_ = bf16[144,384]{1,0:T(8,128)(2,1)S(1)} collective-permute-done((bf16[144,384]{1,0:T(8,128)(2,1)S(1)}, bf16[144,384]{1,0:T(8,128)(2,1)S(1)}, u32[]{:S(2)}, u32[]{:S(2)}) %collective-permute-start.4) | collective-permute-done | bytes 110624 | tf_op jit(solution)/shard_map/ppermute | solution.py:51
  177.5 8.0 %project.1 = (f32[384,1152]{1,0:T(8,128)S(1)}, f32[384,1152]{1,0:T(8,128)}, bf16[384,1152]{1,0:T(8,128)(2,1)S(1)}, bf16[1152,384]{1,0:T(8,128)(2,1)S(1)}) custom-call(s32[3]{0:T(128)S(1)} %pad_add_fusion.ids_ref, f32[16,6912]{1,0:T(8,128)S(1)} %copy-done.2, bf16[384,1152]{1,0:T(8,128)(2,1)S(1)} %copy-done.7, bf16[1152,1152]{1,0:T(8,128)(2,1)} %bitcast.15, ...), custom_call_target="tpu_custom_call" | custom-call | flops 1019215872 | bytes 10174476 | tf_op jit(solution)/shard_map/project/pallas_call | solution.py:32
  185.6 1.2 copy-done.5
  188.3 1.1 collective-permute-done.7.h_o
  189.3 46.5 %feed_forward.1 = (f32[384,1152]{1,0:T(8,128)}, bf16[384,1152]{1,0:T(8,128)(2,1)}, f32[384,1152]{1,0:T(8,128)}, bf16[384,1152]{1,0:T(8,128)(2,1)}, bf16[4,1152,1152]{2,1,0:T(8,128)(2,1)}) custom-call(f32[2,8,384]{2,1,0:T(8,128)} %get-tuple-element.86.hot_ref, s32[8,2304]{1,0:T(8,128)} %reshape.48.chan_ref, bf16[384,1152]{1,0:T(8,128)(2,1)} %copy-done.14, ...), custom_call_target="tpu_custom_call" | custom-call | flops 24461180928 | bytes 30179328 | tf_op jit(solution)/shard_map/feed_forward/pallas_call | solution.py:32
  235.9 1.1 copy-done.21
  237.6 1.9 collective-permute-done.9.got_ref
  239.5 8.8 %middle_back.1 = (bf16[144,384]{1,0:T(8,128)(2,1)S(1)}, bf16[144,384]{1,0:T(8,128)(2,1)S(1)}, bf16[144,384]{1,0:T(8,128)(2,1)S(1)}, bf16[144,384]{1,0:T(8,128)(2...) custom-call(s32[3]{0:T(128)S(1)} %pad_add_fusion.ids_ref, ...), custom_call_target="tpu_custom_call" | custom-call | flops 1019215872 | bytes 12021772 | tf_op jit(solution)/shard_map/middle_back/pallas_call | solution.py:32
  248.3 1.2 copy-done.6
  249.8 5.9 %collective-permute-start.11 = (bf16[144,384]{1,0:T(8,128)(2,1)S(1)}, bf16[144,384]{1,0:T(8,128)(2,1)S(1)}, u32[]{:S(2)}, u32[]{:S(2)}) collective-permute-start(bf16[144,384]{1,0:T(8,128)(2,1)S(1)} %get-tuple-element.105), channel_id=1, source_target_pairs={{0,2},{1,3},{2,0},{3,1},{4,6},{5,7},{6,4},{7,5},{8,10},{9,11},{10,... | collective-permute-start | bytes 331784 | tf_op jit(solution)/shard_map/ppermute | solution.py:51
  255.8 1.9 collective-permute-start.13
  257.7 1.0 collective-permute-start.14
  258.7 1.3 collective-permute-start.15
  260.0 2.0 collective-permute-start.16
  262.0 7.8 %result.1 = (bf16[384,1152]{1,0:T(8,128)(2,1)}, f32[8,2304]{1,0:T(8,128)S(1)}, bf16[4,144,1152]{2,1,0:T(8,128)(2,1)S(1)}, bf16[4,144,1152]{2,1,0:T(8,128)(2,1)}) custom-call(s32[3]{0:T(128)S(1)} %pad_add_fusion.ids_ref, s32[8,128]{1,0:T(8,128)S(1)} %copy-done.12, f32[16,6912]{1,0:T(8,128)S(1)} %copy-done.2, f32[384,1152]{1,0:T(8,128)} %get-tuple-element.84.x1_ref, ...), custom_call_target="tpu_custom_call" | custom-call | flops 1019215872 | bytes 14970892 | tf_op jit(solution)/shard_map/result/pallas_call | solution.py:32
  269.8 1.1 copy-done.13
  270.8 3.2 collective-permute-done.14.refs_5_
  274.1 35.7 %attend_back.1.d_ref = bf16[12,256,768]{2,1,0:T(8,128)(2,1)} custom-call(s32[3]{0:T(128)S(1)} %pad_add_fusion.ids_ref, s32[8,128]{1,0:T(8,128)S(1)} %copy-done.12, s32[8,16]{1,0:T(8,128)S(1)} %bitcast.13, bf16[12,256,768]{2,1,0:T(8,128)(2,1)} %get-tuple-element.75.qkv_ref, bf16[12,144,256]{2,1,0:T(8,128)(2,1)S(1)} %copy-done.17, ...), custom_call_target="tpu_custom_call" | custom-call | flops 12079595520 | bytes 11309580 | tf_op jit(solution)/shard_map/attend_back/pallas_call | solution.py:32
  309.8 79.2 %stream_back.1 = (bf16[384,1152]{1,0:T(8,128)(2,1)}, f32[8,2304]{1,0:T(8,128)}, bf16[288,432]{1,0:T(8,128)(2,1)}, bf16[144,1152]{1,0:T(8,128)(2,1)}) custom-call(bf16[12,256,1152]{2,1,0:T(8,128)(2,1)} %get-tuple-element.99.h_ref, bf16[4,144,1152]{2,1,0:T(8,128)(2,1)} %get-tuple-element.100.gs_ref, bf16[12,256,768]{2,1,0:T(8,128)(2,1)} %attend_back.1.d_ref, ...), custom_call_target="tpu_custom_call" | custom-call | flops 10871635968 | bytes 21154816 | tf_op jit(solution)/shard_map/stream_back/pallas_call | solution.py:32
  389.0 127.8 %finish.1 = (bf16[2,9,144,1152]{3,2,1,0:T(8,128)(2,1)}, bf16[8,288,432]{2,1,0:T(8,128)(2,1)}, f32[4,8,6912]{2,1,0:T(8,128)}, f32[4,32,288]{2,1,0:T(8,128)}) custom-call(bf16[8,144,1152]{2,1,0:T(8,128)(2,1)} %bitcast.17, bf16[288,6912]{1,0:T(8,128)(2,1)} %ada_ref.3, bf16[144,1152]{1,0:T(8,128)(2,1)} %get-tuple-element.118.go_ref, ...), custom_call_target="tpu_custom_call" | custom-call | bytes 16468992 | tf_op jit(solution)/shard_map/finish/pallas_call | solution.py:32
  516.8 14.6 %unfold.1 = (f32[64,1152]{1,0:T(8,128)}, f32[288,6912]{1,0:T(8,128)}, f32[288,3456]{1,0:T(8,128)}, f32[288,1152]{1,0:T(8,128)}, f32[288,4608]{1,0:T(8,128)}, /*index=5*/f32[1152,1152]{1,0:T(8,128)}) custom-call(bf16[32,288]{1,0:T(8,128)(2,1)} %get-tuple-element.115.low_ref, f32[32,64]{1,0:T(8,128)} %get-tuple-element.116.wave_ref, ...), custom_call_target="tpu_custom_call" | custom-call | bytes 33204224 | tf_op jit(solution)/shard_map/unfold/pallas_call | solution.py:32
  531.5 0.9 copy.24
  (76 shorter events, 6.6 us)
Async XLA Ops:
  7.2 6.8 %copy-start = (s32[1,3072]{1,0:T(1,128)S(1)}, s32[1,3072]{1,0:T(1,128)}, u32[]{:S(2)}) copy-start(s32[1,3072]{1,0:T(1,128)} %param.15) | copy-start | bytes 36868
  7.2 182.1 %all-gather.2.cloned.1.call-start = ((), (), s32[]{:S(2)}) async-start(), calls=%async_computation.1 | async-start | bytes 13271040 | tf_op jit(solution)/shard_map/all_gather | solution.py:1136
  12.7 376.3 %reduce-scatter.2.cloned.1.call-start = ((), (), s32[]{:S(2)}) async-start(), calls=%async_computation.2 | async-start | bytes 13271040 | tf_op jit(solution)/shard_map/reduce_scatter | solution.py:1262
  15.2 102.0 %copy-start.15 = (s32[1,8,16]{2,1,0:T(8,128)S(1)}, s32[1,8,16]{2,1,0:T(8,128)}, u32[]{:S(2)}) copy-start(s32[1,8,16]{2,1,0:T(8,128)} %param.16) | copy-start | bytes 1540
  117.9 59.5 %copy-start.2 = (f32[16,6912]{1,0:T(8,128)S(1)}, f32[16,6912]{1,0:T(8,128)}, u32[]{:S(2)}) copy-start(f32[16,6912]{1,0:T(8,128)} %get-tuple-element.72.mod_ref) | copy-start | bytes 1327108
  118.0 59.5 %copy-start.7 = (bf16[384,1152]{1,0:T(8,128)(2,1)S(1)}, bf16[384,1152]{1,0:T(8,128)(2,1)}, u32[]{:S(2)}) copy-start(bf16[384,1152]{1,0:T(8,128)(2,1)} %get-tuple-element.73.x_ref) | copy-start | bytes 2654212
  155.3 31.7 %copy-start.19 = (s32[1,8,4608]{2,1,0:T(8,128)S(1)}, s32[1,8,4608]{2,1,0:T(8,128)}, u32[]{:S(2)}) copy-start(s32[1,8,4608]{2,1,0:T(8,128)} %param.17) | copy-start | bytes 442372
  155.3 6.6 %collective-permute-start = (bf16[144,384]{1,0:T(8,128)(2,1)S(1)}, bf16[144,384]{1,0:T(8,128)(2,1)S(1)}, u32[]{:S(2)}, u32[]{:S(2)}) collective-permute-start(bf16[144,384]{1,0:T(8,128)(2,1)S(1)} %get-tuple-element.77), channel_id=1, source_target_pairs={{0,1},{1,0},{2,3},{3,2},{4,5},{5,4},{6,7},{7,6},{8,9},{9,8},{10,11... | collective-permute-start | bytes 331784 | tf_op jit(solution)/shard_map/ppermute | solution.py:51
  157.4 6.9 %collective-permute-start.1 = (bf16[144,384]{1,0:T(8,128)(2,1)S(1)}, bf16[144,384]{1,0:T(8,128)(2,1)S(1)}, u32[]{:S(2)}, u32[]{:S(2)}) collective-permute-start(bf16[144,384]{1,0:T(8,128)(2,1)S(1)} %get-tuple-element.78), channel_id=1, source_target_pairs={{0,2},{1,3},{2,0},{3,1},{4,6},{5,7},{6,4},{7,5},{8,10},{9,11},{10,... | collective-permute-start | bytes 331784 | tf_op jit(solution)/shard_map/ppermute | solution.py:51
  158.9 10.0 %collective-permute-start.2 = (bf16[144,384]{1,0:T(8,128)(2,1)S(1)}, bf16[144,384]{1,0:T(8,128)(2,1)S(1)}, u32[]{:S(2)}, u32[]{:S(2)}) collective-permute-start(bf16[144,384]{1,0:T(8,128)(2,1)S(1)} %get-tuple-element.79), channel_id=1, source_target_pairs={{0,3},{1,2},{2,1},{3,0},{4,7},{5,6},{6,5},{7,4},{8,11},{9,10},{10,... | collective-permute-start | bytes 331784 | tf_op jit(solution)/shard_map/ppermute | solution.py:51
  159.1 9.9 %collective-permute-start.3 = (bf16[144,384]{1,0:T(8,128)(2,1)S(1)}, bf16[144,384]{1,0:T(8,128)(2,1)S(1)}, u32[]{:S(2)}, u32[]{:S(2)}) collective-permute-start(bf16[144,384]{1,0:T(8,128)(2,1)S(1)} %get-tuple-element.80), channel_id=1, source_target_pairs={{0,4},{1,5},{2,6},{3,7},{4,0},{5,1},{6,2},{7,3},{8,12},{9,13},{10,... | collective-permute-start | bytes 331784 | tf_op jit(solution)/shard_map/ppermute | solution.py:51
  161.7 15.7 %collective-permute-start.4 = (bf16[144,384]{1,0:T(8,128)(2,1)S(1)}, bf16[144,384]{1,0:T(8,128)(2,1)S(1)}, u32[]{:S(2)}, u32[]{:S(2)}) collective-permute-start(bf16[144,384]{1,0:T(8,128)(2,1)S(1)} %get-tuple-element.81), channel_id=1, source_target_pairs={{0,5},{1,4},{2,7},{3,6},{4,1},{5,0},{6,3},{7,2},{8,13},{9,12},{10,... | collective-permute-start | bytes 331784 | tf_op jit(solution)/shard_map/ppermute | solution.py:51
  161.9 15.6 %collective-permute-start.5 = (bf16[144,384]{1,0:T(8,128)(2,1)S(1)}, bf16[144,384]{1,0:T(8,128)(2,1)S(1)}, u32[]{:S(2)}, u32[]{:S(2)}) collective-permute-start(bf16[144,384]{1,0:T(8,128)(2,1)S(1)} %get-tuple-element.82), channel_id=1, source_target_pairs={{0,6},{1,7},{2,4},{3,5},{4,2},{5,3},{6,0},{7,1},{8,14},{9,15},{10,... | collective-permute-start | bytes 331784 | tf_op jit(solution)/shard_map/ppermute | solution.py:51
  164.3 13.2 %collective-permute-start.6 = (bf16[144,384]{1,0:T(8,128)(2,1)S(1)}, bf16[144,384]{1,0:T(8,128)(2,1)S(1)}, u32[]{:S(2)}, u32[]{:S(2)}) collective-permute-start(bf16[144,384]{1,0:T(8,128)(2,1)S(1)} %get-tuple-element.83), channel_id=1, source_target_pairs={{0,7},{1,6},{2,5},{3,4},{4,3},{5,2},{6,1},{7,0},{8,15},{9,14},{10,... | collective-permute-start | bytes 331784 | tf_op jit(solution)/shard_map/ppermute | solution.py:51
  186.8 2.6 collective-permute-start.7
  235.9 3.6 copy-start.3
  235.9 3.6 copy-start.12
  237.0 2.4 collective-permute-start.9
  237.4 20.3 %collective-permute-start.8 = (bf16[384,1152]{1,0:T(8,128)(2,1)}, bf16[384,1152]{1,0:T(8,128)(2,1)S(1)}, u32[]{:S(2)}, u32[]{:S(2)}) collective-permute-start(bf16[384,1152]{1,0:T(8,128)(2,1)} %get-tuple-element.90), channel_id=1, source_target_pairs={{0,1},{1,0},{2,3},{3,2},{4,5},{5,4},{6,7},{7,6},{8,9},{9,8},{10,11... | collective-permute-start | bytes 2654216 | tf_op jit(solution)/shard_map/ppermute | solution.py:51
  239.5 22.5 %copy-start.8 = (bf16[384,384]{1,0:T(8,128)(2,1)S(1)}, bf16[384,384]{1,0:T(8,128)(2,1)}, u32[]{:S(2)}) copy-start(bf16[384,384]{1,0:T(8,128)(2,1)} %get-tuple-element.97.perm_ref) | copy-start | bytes 884740
  249.5 20.3 %copy-start.9 = (f32[8,2304]{1,0:T(8,128)}, f32[8,2304]{1,0:T(8,128)S(1)}, u32[]{:S(2)}) copy-start(f32[8,2304]{1,0:T(8,128)S(1)} %get-tuple-element.121.two_ref) | copy-start | bytes 221188
  249.5 9.2 %collective-permute-start.10 = (bf16[144,384]{1,0:T(8,128)(2,1)S(1)}, bf16[144,384]{1,0:T(8,128)(2,1)S(1)}, u32[]{:S(2)}, u32[]{:S(2)}) collective-permute-start(bf16[144,384]{1,0:T(8,128)(2,1)S(1)} %get-tuple-element.104), channel_id=1, source_target_pairs={{0,1},{1,0},{2,3},{3,2},{4,5},{5,4},{6,7},{7,6},{8,9},{9,8},{10,11... | collective-permute-start | bytes 331784 | tf_op jit(solution)/shard_map/ppermute | solution.py:51
  249.8 10.2 %collective-permute-start.11 = (bf16[144,384]{1,0:T(8,128)(2,1)S(1)}, bf16[144,384]{1,0:T(8,128)(2,1)S(1)}, u32[]{:S(2)}, u32[]{:S(2)}) collective-permute-start(bf16[144,384]{1,0:T(8,128)(2,1)S(1)} %get-tuple-element.105), channel_id=1, source_target_pairs={{0,2},{1,3},{2,0},{3,1},{4,6},{5,7},{6,4},{7,5},{8,10},{9,11},{10,... | collective-permute-start | bytes 331784 | tf_op jit(solution)/shard_map/ppermute | solution.py:51
  255.7 15.1 %collective-permute-start.12 = (bf16[144,384]{1,0:T(8,128)(2,1)S(1)}, bf16[144,384]{1,0:T(8,128)(2,1)S(1)}, u32[]{:S(2)}, u32[]{:S(2)}) collective-permute-start(bf16[144,384]{1,0:T(8,128)(2,1)S(1)} %get-tuple-element.106), channel_id=1, source_target_pairs={{0,3},{1,2},{2,1},{3,0},{4,7},{5,6},{6,5},{7,4},{8,11},{9,10},{10,... | collective-permute-start | bytes 331784 | tf_op jit(solution)/shard_map/ppermute | solution.py:51
  255.8 15.1 %collective-permute-start.13 = (bf16[144,384]{1,0:T(8,128)(2,1)S(1)}, bf16[144,384]{1,0:T(8,128)(2,1)S(1)}, u32[]{:S(2)}, u32[]{:S(2)}) collective-permute-start(bf16[144,384]{1,0:T(8,128)(2,1)S(1)} %get-tuple-element.107), channel_id=1, source_target_pairs={{0,4},{1,5},{2,6},{3,7},{4,0},{5,1},{6,2},{7,3},{8,12},{9,13},{10,... | collective-permute-start | bytes 331784 | tf_op jit(solution)/shard_map/ppermute | solution.py:51
  257.7 16.4 %collective-permute-start.14 = (bf16[144,384]{1,0:T(8,128)(2,1)S(1)}, bf16[144,384]{1,0:T(8,128)(2,1)S(1)}, u32[]{:S(2)}, u32[]{:S(2)}) collective-permute-start(bf16[144,384]{1,0:T(8,128)(2,1)S(1)} %get-tuple-element.108), channel_id=1, source_target_pairs={{0,5},{1,4},{2,7},{3,6},{4,1},{5,0},{6,3},{7,2},{8,13},{9,12},{10,... | collective-permute-start | bytes 331784 | tf_op jit(solution)/shard_map/ppermute | solution.py:51
  258.7 15.4 %collective-permute-start.15 = (bf16[144,384]{1,0:T(8,128)(2,1)S(1)}, bf16[144,384]{1,0:T(8,128)(2,1)S(1)}, u32[]{:S(2)}, u32[]{:S(2)}) collective-permute-start(bf16[144,384]{1,0:T(8,128)(2,1)S(1)} %get-tuple-element.109), channel_id=1, source_target_pairs={{0,6},{1,7},{2,4},{3,5},{4,2},{5,3},{6,0},{7,1},{8,14},{9,15},{10,... | collective-permute-start | bytes 331784 | tf_op jit(solution)/shard_map/ppermute | solution.py:51
  260.0 14.0 %collective-permute-start.16 = (bf16[144,384]{1,0:T(8,128)(2,1)S(1)}, bf16[144,384]{1,0:T(8,128)(2,1)S(1)}, u32[]{:S(2)}, u32[]{:S(2)}) collective-permute-start(bf16[144,384]{1,0:T(8,128)(2,1)S(1)} %get-tuple-element.110), channel_id=1, source_target_pairs={{0,7},{1,6},{2,5},{3,4},{4,3},{5,2},{6,1},{7,0},{8,15},{9,14},{10,... | collective-permute-start | bytes 331784 | tf_op jit(solution)/shard_map/ppermute | solution.py:51
  262.0 12.1 %copy-start.17 = (bf16[12,144,256]{2,1,0:T(8,128)(2,1)S(1)}, bf16[12,144,256]{2,1,0:T(8,128)(2,1)}, u32[]{:S(2)}) copy-start(bf16[12,144,256]{2,1,0:T(8,128)(2,1)} %copy-done.16) | copy-start | bytes 2654212
  270.8 38.9 %copy-start.10 = (f32[8,2304]{1,0:T(8,128)}, f32[8,2304]{1,0:T(8,128)S(1)}, u32[]{:S(2)}) copy-start(f32[8,2304]{1,0:T(8,128)S(1)} %get-tuple-element.122.gate_ref) | copy-start | bytes 221188
  516.8 14.7 %copy-start.18 = (bf16[384,1152]{1,0:T(8,128)(2,1)S(1)}, bf16[384,1152]{1,0:T(8,128)(2,1)}, u32[]{:S(2)}) copy-start(bf16[384,1152]{1,0:T(8,128)(2,1)} %get-tuple-element.145) | copy-start | bytes 2654212
  516.8 15.6 %copy-start.1 = (s32[1,3072]{1,0:T(1,128)S(1)}, s32[1,3072]{1,0:T(1,128)}, u32[]{:S(2)}) copy-start(s32[1,3072]{1,0:T(1,128)} %param.15) | copy-start | bytes 36868
  (10 other events, 13.1 us)
Sparse Core Ops, SparseCore 0:
  12.8 139.6 all-gather.1
  236.1 113.0 reduce-scatter.1

commit v4 on v3

--- a/solution.py
+++ b/solution.py
@@ -449,30 +449,51 @@
     return tiles
 
 
+def in_groups(first, last, sizes, step, carry):
+    for size in sizes:
+        count = (last - first) // size
+
+        def one(index, carry, first=first, size=size):
+            return step(first + index * size, size, carry)
+
+        carry = lax.fori_loop(0, count, one, carry)
+        first = first + count * size
+    return carry
+
+
 def attend_body(own, size, blocks, ids_ref, info_ref, mask_ref, qkv_ref, o_ref, lse_ref, *refs):
-    outs, (held,) = refs[:blocks], refs[blocks:]
+    outs, (held, turned, placed) = refs[:blocks], refs[blocks:]
     units = qkv_ref.shape[0]
     width = BLOCK // blocks
     b = ids_ref[1]
     scale = LOG2E / math.sqrt(size)
-    pad = -size % 16
+    tall = turned.shape[2]
+
+    def turn(j):
+        for h in range(own):
+            at = (2 * own + h) * LANES
+            values = qkv_ref[j, :, at : at + LANES].astype(F32).T
+            turned[j, h] = values[0:tall].astype(BF16)
+
+    each(units, turn, 2)
 
     def one_unit(u):
         queries = [qkv_ref[u, :, h * LANES : (h + 1) * LANES] for h in range(own)]
 
-        def one_block(j, carry):
+        def some_blocks(j, count, carry):
             fresh = []
             for h in range(own):
                 top, total, acc = carry[h]
-                keys = qkv_ref[j, :, (own + h) * LANES : (own + h + 1) * LANES]
-                at = (2 * own + h) * LANES
-                values = qkv_ref[j, :, at : at + LANES]
-                scores = nt(keys, queries[h]) * scale
+                keys = qkv_ref[pl.ds(j, count), :, (own + h) * LANES : (own + h + 1) * LANES]
+                scores = nt(keys.reshape(count * BLOCK, LANES), queries[h]) * scale
                 new_top = jnp.maximum(top, jnp.max(scores, axis=0, keepdims=True))
                 probs = jnp.exp2(scores - new_top)
                 decay = jnp.exp2(top - new_top)
                 total = total * decay + jnp.sum(probs, axis=0, keepdims=True)
-                acc = acc * decay + tn(values, probs.astype(BF16))
+                acc = acc * decay
+                low = probs.astype(BF16)
+                for i in range(count):
+                    acc = acc + nn(turned[j + i, h], low[i * BLOCK : (i + 1) * BLOCK])
                 fresh.append((new_top, total, acc))
             return tuple(fresh)
 
@@ -480,11 +501,11 @@
             (
                 jnp.full((1, BLOCK), NEG, F32),
                 jnp.zeros((1, BLOCK), F32),
-                jnp.zeros((LANES, BLOCK), F32),
+                jnp.zeros((tall, BLOCK), F32),
             )
             for _ in range(own)
         )
-        done = lax.fori_loop(info_ref[1, u], info_ref[2, u], one_block, start)
+        done = in_groups(info_ref[1, u], info_ref[2, u], (4, 2, 1), some_blocks, start)
         slot = info_ref[0, u]
         rows = []
         for h in range(own):
@@ -503,12 +524,9 @@
                 held[groups * g + i, :, e * LANES : (e + 1) * LANES] for i in range(groups)
             ]
             for j, tile in enumerate(exchange_lanes(tiles, width)):
-                device = groups * e + j
-                for k in range(blocks):
-
-                    @pl.when(lax.bitwise_xor(b, k) == device)
-                    def _():
-                        outs[k][:, g * LANES : (g + 1) * LANES] = tile.astype(BF16)
+                placed[groups * e + j, :, g * LANES : (g + 1) * LANES] = tile.astype(BF16)
+    for k in range(blocks):
+        outs[k][...] = placed[lax.bitwise_xor(b, k)]
 
 
 def attend_back_body(own, size, blocks, ids_ref, info_ref, mask_ref, qkv_ref, o_ref, lse_ref, *refs):
@@ -547,21 +565,25 @@
         keys = [qkv_ref[j, :, (own + h) * LANES : (own + h + 1) * LANES] for h in range(own)]
         turned = [keys[h].astype(F32).T.astype(BF16) for h in range(own)]
 
-        def one_block(i, carry):
+        def some_blocks(i, count, carry):
             for h in range(own):
-                queries = qkv_ref[i, :, h * LANES : (h + 1) * LANES]
                 at = (2 * own + h) * LANES
                 values = qkv_ref[j, :, at : at + LANES]
-                scores = nt(keys[h], queries) * scale
-                probs = jnp.exp2(scores - lse_ref[i, h : h + 1, :])
-                d_probs = nn(values, up[i, h])
-                d_scores = (probs * (d_probs - delta[i, h : h + 1, :])).astype(BF16)
-                d_k[h] += nn(d_scores, queries)
-                d_v[h] += nt(probs.astype(BF16), up[i, h])
-                d_q[i, h] += nn(turned[h], d_scores)
+                sum_k = sum_v = 0.0
+                for n in range(count):
+                    queries = qkv_ref[i + n, :, h * LANES : (h + 1) * LANES]
+                    scores = nt(keys[h], queries) * scale
+                    probs = jnp.exp2(scores - lse_ref[i + n, h : h + 1, :])
+                    d_probs = nn(values, up[i + n, h])
+                    d_scores = (probs * (d_probs - delta[i + n, h : h + 1, :])).astype(BF16)
+                    sum_k = sum_k + nn(d_scores, queries)
+                    sum_v = sum_v + nt(probs.astype(BF16), up[i + n, h])
+                    d_q[i + n, h] += nn(turned[h], d_scores)
+                d_k[h] += sum_k
+                d_v[h] += sum_v
             return carry
 
-        lax.fori_loop(info_ref[1, j], info_ref[2, j], one_block, 0)
+        in_groups(info_ref[1, j], info_ref[2, j], (4, 2, 1), some_blocks, 0)
         for h in range(own):
             at = (own + h) * LANES
             d_ref[j, :, at : at + LANES] = (d_k[h] * factor).astype(BF16)
@@ -603,7 +625,7 @@
     each(x_ref.shape[0] // width, one)
 
 
-def ff_body(shards, step, hot_ref, chan_ref, h_m, h_o, dm_ref, w_ref, *refs):
+def ff_body(shards, step, sides, hot_ref, chan_ref, h_m, h_o, dm_ref, w_ref, *refs):
     mlp_m, mlp_o, dh_m, dh_o, g_ref, w1, w2, h, dm, turned, hid_s, du_s, mlp, dh, g1, g2, sems = refs
     total = h.shape[0]
     count = total // 2
@@ -611,41 +633,73 @@
     blocks = f_size // size
     row1, row2 = size // shards, f_size // shards
 
-    def placed(rows, one, two):
-        for shard in range(shards):
-            for block in range(blocks):
-                yield (
-                    rows.at[shard, block * row1 : (block + 1) * row1],
-                    one.at[shard * row1 : (shard + 1) * row1, block * size : (block + 1) * size],
-                )
-            yield rows.at[shard, blocks * row1 :], two.at[shard * row2 : (shard + 1) * row2]
-
-    copies = fetch(
-        [
-            (h_m, h.at[0:count]),
-            (h_o, h.at[count:total]),
-            (dm_ref.at[0], dm.at[0:count]),
-            (dm_ref.at[1], dm.at[count:total]),
+    def up_part(ref, shard, low, high):
+        block = low // size
+        return ref.at[
+            shard, block * row1 : (block + 1) * row1, low - block * size : high - block * size
         ]
-        + list(placed(w_ref, w1, w2)),
-        sems,
-    )
-    for copy in copies:
+
+    def down_part(ref, shard, low, high):
+        at = blocks * row1 - shard * row2
+        return ref.at[shard, at + low : at + high]
+
+    def chunk(index):
+        low, high = index * step, (index + 1) * step
+        cols = [
+            (max(low, i * size), min(high, (i + 1) * size))
+            for i in range(blocks)
+            if max(low, i * size) < min(high, (i + 1) * size)
+        ]
+        rows = [
+            (i, max(low, i * row2), min(high, (i + 1) * row2))
+            for i in range(shards)
+            if max(low, i * row2) < min(high, (i + 1) * row2)
+        ]
+        return cols, rows
+
+    used = [0]
+
+    def begin(pairs):
+        copies = fetch(pairs, sems, used[0])
+        used[0] += len(copies)
+        return copies
+
+    waits = [
+        begin(
+            [
+                (h_m, h.at[0:count]),
+                (h_o, h.at[count:total]),
+                (dm_ref.at[0], dm.at[0:count]),
+                (dm_ref.at[1], dm.at[count:total]),
+            ]
+        )
+    ]
+    chunks = f_size // step
+    for index in range(chunks):
+        cols, rows = chunk(index)
+        pairs = [
+            (up_part(w_ref, shard, lo, hi), w1.at[shard * row1 : (shard + 1) * row1, lo:hi])
+            for shard in range(shards)
+            for lo, hi in cols
+        ]
+        pairs += [(down_part(w_ref, shard, lo, hi), w2.at[lo:hi]) for shard, lo, hi in rows]
+        waits.append(begin(pairs))
+    for copy in waits[0]:
         copy.wait()
     for at in range(0, total, LANES):
         turned[:, at : at + LANES] = h[at : at + LANES, :].astype(F32).T.astype(BF16)
-    mlp[...] = jnp.zeros_like(mlp)
-    dh[...] = jnp.zeros_like(dh)
-    hots = [hot_ref[side].astype(BF16) for side in range(2)]
-
-    def one(index):
-        cols = pl.ds(pl.multiple_of(index * step, step), step)
+    hots = jnp.concatenate([hot_ref[side] for side in range(2)], axis=1).astype(BF16)
+    left = []
+    for index in range(chunks):
+        for copy in waits[index + 1]:
+            copy.wait()
+        cols = slice(index * step, (index + 1) * step)
         up = w1[:, cols]
         down = w2[cols, :]
         chan = chan_ref[:, cols].astype(F32).astype(BF16)
-        for side in range(2):
-            rows = slice(side * count, (side + 1) * count)
-            keep = tn(hots[side], chan)
+        for side in range(sides):
+            rows = slice(side * total // sides, (side + 1) * total // sides)
+            keep = tn(hots[:, rows], chan)
             pre = nn(h[rows, :], up)
             inner = pre * pre
             bent = jnp.tanh(0.7978845608028654 * (pre + 0.044715 * inner * pre))
@@ -658,18 +712,27 @@
             du = (slope * back * keep).astype(BF16)
             hid_s[rows, :] = hid
             du_s[rows, :] = du
-            mlp[rows, :] += nn(hid, down)
-            dh[rows, :] += nt(du, up)
+            if index:
+                mlp[rows, :] += nn(hid, down)
+                dh[rows, :] += nt(du, up)
+            else:
+                mlp[rows, :] = nn(hid, down)
+                dh[rows, :] = nt(du, up)
         g1[:, cols] = nn(turned[...], du_s[...]).astype(BF16)
         g2[cols, :] = tn(hid_s[...], dm[...]).astype(BF16)
-
-    each(f_size // step, one)
+        parts, rows = chunk(index)
+        pairs = [
+            (g1.at[shard * row1 : (shard + 1) * row1, lo:hi], up_part(g_ref, shard, lo, hi))
+            for shard in range(shards)
+            for lo, hi in parts
+        ]
+        pairs += [(g2.at[lo:hi], down_part(g_ref, shard, lo, hi)) for shard, lo, hi in rows]
+        left += begin(pairs)
     mlp_m[...] = mlp[0:count, :]
     mlp_o[...] = mlp[count:total, :].astype(BF16)
     dh_m[...] = dh[0:count, :]
     dh_o[...] = dh[count:total, :].astype(BF16)
-
-    for copy in fetch([(found, rows) for rows, found in placed(g_ref, g1, g2)], sems):
+    for copy in left:
         copy.wait()
 
 
@@ -892,7 +955,7 @@
 
 def finish_body(
     shards, chips, fc_ref, ada_ref, go_ref, gq_ref, one_ref, two_ref, gate_ref, cond_ref, tot_ref, gqa_ref,
-    dm_ref, dc_ref, mine, up, inner_in, result, other, gq_all, sum_own, sum_pair, sums, mods, conds, ada_s,
+    dm_ref, dc_ref, mine, up, inner_in, result, other, gq_all, sum_own, sum_pair, small, mods, conds, ada_s,
     local, sent, got,
 ):
     f, b = lax.axis_index("fsdp"), lax.axis_index("blk")
@@ -944,24 +1007,30 @@
     middle = (z == half - 1) | (z == half)
     edge = jnp.logical_not(middle)
 
+    parts = [[small.at[i] for i in range(4)]]
+    parts += [[ref.at[i] for ref in (mine, up, inner_in, result)] for i in range(count)]
+    count += 1
+
     def inward(i, when):
-        routes.start(("up", i), mine.at[i], up.at[i], inner, when & edge)
-        routes.start(("across", i), mine.at[i], inner_in.at[i], inner, when & middle, ("in", i))
-
+        own, above, within, _ = parts[i]
+        routes.start(("up", i), own, above, inner, when & edge)
+        routes.start(("across", i), own, within, inner, when & middle, ("in", i))
+
+    mine[count - 2] = go_ref[...]
     routes.arrive("sum", sum_pair)
-    sums[z] = (sum_own[...] + sum_pair[...]).astype(BF16).astype(F32)
-    send("small", 1, lambda chip: sums.at[chip])
-    mine[count - 1] = go_ref[...]
+    total = sum_own[...] + sum_pair[...]
+    small[0] = jnp.concatenate(
+        [total[:, : 3 * size], total[:, 3 * size :]], axis=0
+    ).astype(BF16)
+    ahead = min(4, count)
+    inward(0, jnp.logical_not(ends))
     loads[0].wait()
-    ahead = min(3, count)
-    for i in range(ahead):
+    for i in range(1, ahead):
         inward(i, jnp.logical_not(ends))
 
     def combine():
-        total = sums[0]
-        for chip in range(1, chips):
-            total = total + sums[chip]
-        mods[f] = total.astype(BF16).astype(F32)
+        mods[f, :, : 3 * size] = small[3, 0:slots].astype(F32)
+        mods[f, :, 3 * size :] = small[3, slots : 2 * slots].astype(F32)
         for k in range(1, shards):
             routes.start(("mod", k), mods.at[f], mods.at[f], {"fsdp": flip(f, k)})
 
@@ -982,45 +1051,45 @@
             routes.arrive(("cond", k), conds.at[flip(f, k)])
         dc_ref[...] = conds[...]
 
-    jobs = []
-    for s in range(1, chips):
-        jobs.append(lambda s=s: take("small", s, lambda chip: sums.at[chip]))
-    jobs += [combine, condition, conditions]
+    jobs = [combine, condition, conditions]
     heads = [lambda s=s: take("head", s, head) for s in range(1, chips)]
 
     def forward(i):
-        routes.arrive(("up", i), up.at[i], ends)
+        own, above, _, _ = parts[i]
+        routes.arrive(("up", i), above, ends)
 
         @pl.when(ends)
         def _():
-            mine[i] = (mine[i].astype(F32) + up[i].astype(F32)).astype(BF16)
+            own[...] = (own[...].astype(F32) + above[...].astype(F32)).astype(BF16)
 
         inward(i, ends)
         if i + ahead < count:
             inward(i + ahead, jnp.logical_not(ends))
 
     def back(i):
-        routes.arrive(("in", i), inner_in.at[i])
+        own, _, within, full = parts[i]
+        routes.arrive(("in", i), within)
 
         @pl.when(middle)
         def _():
-            result[i] = (mine[i].astype(F32) + inner_in[i].astype(F32)).astype(BF16)
+            full[...] = (own[...].astype(F32) + within[...].astype(F32)).astype(BF16)
 
         @pl.when(edge)
         def _():
-            result[i] = inner_in[i]
-
-        routes.start(("down", i), result.at[i], inner_in.at[i], outer, ends, ("in", i))
-        routes.start(("pair", i), result.at[i], other.at[i], {"blk": pair})
+            full[...] = within[...]
+
+        routes.start(("down", i), full, within, outer, ends, ("in", i))
+        if i:
+            routes.start(("pair", i - 1), full, other.at[i - 1], {"blk": pair})
 
     for i in range(count + 1):
         if i < count:
             forward(i)
         if i:
             back(i - 1)
-            if jobs and i > 1:
+            if jobs and i % 2 == 1:
                 jobs.pop(0)()
-            if heads and i % 2 == 1 and i > 2:
+            if heads and i % 2 == 0 and i > 2:
                 heads.pop(0)()
     for job in jobs + heads:
         job()
@@ -1029,7 +1098,7 @@
             chip, _, when = line(side, s, False)
             routes.start(("head pair", side, s), head(chip), head(chip), {"blk": pair}, when)
     copies = fetch([(result, tot_ref.at[c])], local)
-    for i in range(count):
+    for i in range(count - 1):
         routes.arrive(("pair", i), other.at[i])
     copies += fetch([(other, tot_ref.at[1 - c])], local, 1)
     routes.arrive("head pair", gq_all.at[pair])
@@ -1203,7 +1272,11 @@
             (VMEM, shape((units, 8, BLOCK), F32)),
         ]
         + [(VMEM, shape((narrow, count)))] * blocks,
-        [pltpu.VMEM((units, narrow, BLOCK), F32)],
+        [
+            pltpu.VMEM((units, narrow, BLOCK), F32),
+            pltpu.VMEM((units, own, -(-head_size // 16) * 16, BLOCK), BF16),
+            pltpu.VMEM((blocks, narrow, count), BF16),
+        ],
         flops=2 * units * units * BLOCK * BLOCK * wide // 3,
     )
     held, lse, pieces = outs[0], outs[1], outs[2:]
@@ -1230,10 +1303,11 @@
 
     chan = chan_mask[0].reshape(slots, shards, 2, half // shards)
     chan = lax.dynamic_slice_in_dim(chan, c, 1, axis=2).reshape(slots, half)
-    n_sems = 4 + shards * (half // size + 1)
+    ff_step = 768
+    n_sems = 4 + 4 * shards * (half // ff_step + 1)
     mlp, mlp_send, dh2, dh2_send, g_fc = run(
         "feed_forward",
-        functools.partial(ff_body, shards, 256),
+        functools.partial(ff_body, shards, ff_step, 2),
         [(VMEM, hots), (VMEM, chan)] + [(ANY, a) for a in (h2, h2_other, dms, fc_all)],
         [
             (VMEM, shape((count, size), F32)),
@@ -1248,8 +1322,8 @@
             pltpu.VMEM((2 * count, size), BF16),
             pltpu.VMEM((2 * count, size), BF16),
             pltpu.VMEM((size, 2 * count), BF16),
-            pltpu.VMEM((2 * count, 256), BF16),
-            pltpu.VMEM((2 * count, 256), BF16),
+            pltpu.VMEM((2 * count, ff_step), BF16),
+            pltpu.VMEM((2 * count, ff_step), BF16),
             pltpu.VMEM((2 * count, size), F32),
             pltpu.VMEM((2 * count, size), F32),
             pltpu.VMEM((size, half), BF16),
@@ -1352,7 +1426,7 @@
     )
 
     pieces = fc_rows // out_rows
-    n_copies = 5 * pieces + 10 + 6 * chips + 2 * shards
+    n_copies = 5 * pieces + 16 + 4 * chips + 2 * shards
     totals, g_qkv, d_mod, d_cond = run(
         "finish",
         functools.partial(finish_body, shards, chips),
@@ -1369,7 +1443,7 @@
             pltpu.VMEM((blocks, rows_qkv, 3 * narrow), BF16),
             pltpu.VMEM((slots, wider), F32),
             pltpu.VMEM((slots, wider), F32),
-            pltpu.VMEM((chips, slots, wider), F32),
+            pltpu.VMEM((4, 2 * slots, wider // 2), BF16),
             pltpu.VMEM((shards, slots, wider), F32),
             pltpu.VMEM((shards, shards * slots, ada_rows), F32),
             pltpu.VMEM(w_ada.shape, BF16),

time: 546 us -> 506 us (0.927)
  Pallas kernels: 471 us -> 431 us
    pallas_call x11, Pallas kernels: 471 us -> 431 us  [run(): pl.pallas_call(body, out_shape=[o for _, o in outs], in_specs=[s for s, _...]
  transfers between devices with their start and end apart: 19 -> 19, of which waited for: 5 -> 5; matrix products, arithmetic and copies ran while one was open for 1% -> 1% of each run, Pallas kernels for 52% -> 50%
where the time goes in v4:
time: 506 us; the launch traced here: 499 us
  Pallas kernels  431 us (85%)
  starting transfers between devices  25.5 us (5%)
  waiting for transfers between devices  15.2 us (3%)
  between operations  14.7 us (3%)
  local copies, waits for them, and re-layouts  11.8 us (2%)
    pallas_call x11, Pallas kernels, run(): pl.pallas_call(body, out_shape=[o for _, o in outs], in_specs=[s for s, _...  431 us
    ppermute x17, starting transfers between devices, swap(): return lax.ppermute(array, axis, [(i, i ^ by) for i in range(size)])  25.5 us
    ppermute x17, waiting for transfers between devices, swap(): return lax.ppermute(array, axis, [(i, i ^ by) for i in range(size)])  15.2 us
  transfers between devices with their start and end apart: 19, of which 5 were waited for; matrix products, arithmetic and copies ran while one was open for 1% of the time, Pallas kernels for 50%

profile of v4, /device:TPU:1, one launch (start us, length us, event | category | flops | bytes accessed | tf_op | source)
XLA Modules:
  0.0 498.9 jit_solution(4881736693269947813)
XLA Ops:
  7.3 1.7 copy-done.4
  9.1 3.6 pick_half.1
  15.2 102.4 %front.1 = (bf16[384,1152]{1,0:T(8,128)(2,1)}, bf16[384,1152]{1,0:T(8,128)(2,1)}, f32[2,8,384]{2,1,0:T(8,128)}, s32[8,128]{1,0:T(8,128)}, f32[8,128]{1,0:T(8,128...) custom-call(s32[1,384]{1,0:T(1,128)} %constant_dynamic-slice_fusion., ...), custom_call_target="tpu_custom_call" | custom-call | flops 5435817984 | bytes 29156352 | tf_op jit(solution)/shard_map/front/pallas_call | solution.py:32
  118.3 20.4 %attend.1 = (bf16[12,144,256]{2,1,0:T(8,128)(2,1)S(1)}, f32[12,8,256]{2,1,0:T(8,128)S(1)}, bf16[144,384]{1,0:T(8,128)(2,1)S(1)}, bf16[144,384]{1,0:T(8,128)(2,1)...) custom-call(s32[3]{0:T(128)S(1)} %pad_add_fusion.ids_ref, ...), custom_call_target="tpu_custom_call" | custom-call | flops 4831838208 | bytes 6590988 | tf_op jit(solution)/shard_map/attend/pallas_call | solution.py:32
  138.8 0.9 copy-done.16
  139.7 2.1 collective-permute-start
  141.8 1.5 collective-permute-start.1
  143.4 2.7 collective-permute-start.3
  146.2 2.4 collective-permute-start.5
  148.7 4.1 collective-permute-start.6
  153.2 8.6 %collective-permute-done.4.refs_5_ = bf16[144,384]{1,0:T(8,128)(2,1)S(1)} collective-permute-done((bf16[144,384]{1,0:T(8,128)(2,1)S(1)}, bf16[144,384]{1,0:T(8,128)(2,1)S(1)}, u32[]{:S(2)}, u32[]{:S(2)}) %collective-permute-start.4) | collective-permute-done | bytes 110624 | tf_op jit(solution)/shard_map/ppermute | solution.py:51
  161.8 8.0 %project.1 = (f32[384,1152]{1,0:T(8,128)S(1)}, f32[384,1152]{1,0:T(8,128)}, bf16[384,1152]{1,0:T(8,128)(2,1)S(1)}, bf16[1152,384]{1,0:T(8,128)(2,1)S(1)}) custom-call(s32[3]{0:T(128)S(1)} %pad_add_fusion.ids_ref, f32[16,6912]{1,0:T(8,128)S(1)} %copy-done.2, bf16[384,1152]{1,0:T(8,128)(2,1)S(1)} %copy-done.7, bf16[1152,1152]{1,0:T(8,128)(2,1)} %bitcast.15, ...), custom_call_target="tpu_custom_call" | custom-call | flops 1019215872 | bytes 10174476 | tf_op jit(solution)/shard_map/project/pallas_call | solution.py:32
  169.9 1.2 copy-done.5
  171.9 0.7 reshape.48.chan_ref
  172.6 1.1 collective-permute-done.7.h_o
  173.7 38.3 %feed_forward.1 = (f32[384,1152]{1,0:T(8,128)}, bf16[384,1152]{1,0:T(8,128)(2,1)}, f32[384,1152]{1,0:T(8,128)}, bf16[384,1152]{1,0:T(8,128)(2,1)}, bf16[4,1152,1152]{2,1,0:T(8,128)(2,1)}) custom-call(f32[2,8,384]{2,1,0:T(8,128)} %get-tuple-element.86.hot_ref, s32[8,2304]{1,0:T(8,128)} %reshape.48.chan_ref, bf16[384,1152]{1,0:T(8,128)(2,1)} %copy-done.14, ...), custom_call_target="tpu_custom_call" | custom-call | flops 24461180928 | bytes 30179328 | tf_op jit(solution)/shard_map/feed_forward/pallas_call | solution.py:32
  212.0 1.1 copy-done.21
  213.6 1.9 collective-permute-done.9.got_ref
  215.6 8.8 %middle_back.1 = (bf16[144,384]{1,0:T(8,128)(2,1)S(1)}, bf16[144,384]{1,0:T(8,128)(2,1)S(1)}, bf16[144,384]{1,0:T(8,128)(2,1)S(1)}, bf16[144,384]{1,0:T(8,128)(2...) custom-call(s32[3]{0:T(128)S(1)} %pad_add_fusion.ids_ref, ...), custom_call_target="tpu_custom_call" | custom-call | flops 1019215872 | bytes 12021772 | tf_op jit(solution)/shard_map/middle_back/pallas_call | solution.py:32
  224.4 1.2 copy-done.6
  225.9 5.0 %collective-permute-start.11 = (bf16[144,384]{1,0:T(8,128)(2,1)S(1)}, bf16[144,384]{1,0:T(8,128)(2,1)S(1)}, u32[]{:S(2)}, u32[]{:S(2)}) collective-permute-start(bf16[144,384]{1,0:T(8,128)(2,1)S(1)} %get-tuple-element.105), channel_id=1, source_target_pairs={{0,2},{1,3},{2,0},{3,1},{4,6},{5,7},{6,4},{7,5},{8,10},{9,11},{10,... | collective-permute-start | bytes 331784 | tf_op jit(solution)/shard_map/ppermute | solution.py:51
  231.0 2.2 collective-permute-start.13
  233.9 1.7 collective-permute-start.15
  235.6 1.6 collective-permute-start.16
  237.2 7.5 %result.1 = (bf16[384,1152]{1,0:T(8,128)(2,1)}, f32[8,2304]{1,0:T(8,128)S(1)}, bf16[4,144,1152]{2,1,0:T(8,128)(2,1)S(1)}, bf16[4,144,1152]{2,1,0:T(8,128)(2,1)}) custom-call(s32[3]{0:T(128)S(1)} %pad_add_fusion.ids_ref, s32[8,128]{1,0:T(8,128)S(1)} %copy-done.12, f32[16,6912]{1,0:T(8,128)S(1)} %copy-done.2, f32[384,1152]{1,0:T(8,128)} %get-tuple-element.84.x1_ref, ...), custom_call_target="tpu_custom_call" | custom-call | flops 1019215872 | bytes 14970892 | tf_op jit(solution)/shard_map/result/pallas_call | solution.py:32
  244.8 1.1 copy-done.13
  245.8 3.1 collective-permute-done.14.refs_5_
  248.9 29.9 %attend_back.1.d_ref = bf16[12,256,768]{2,1,0:T(8,128)(2,1)} custom-call(s32[3]{0:T(128)S(1)} %pad_add_fusion.ids_ref, s32[8,128]{1,0:T(8,128)S(1)} %copy-done.12, s32[8,16]{1,0:T(8,128)S(1)} %bitcast.13, bf16[12,256,768]{2,1,0:T(8,128)(2,1)} %get-tuple-element.75.qkv_ref, bf16[12,144,256]{2,1,0:T(8,128)(2,1)S(1)} %copy-done.17, ...), custom_call_target="tpu_custom_call" | custom-call | flops 12079595520 | bytes 11309580 | tf_op jit(solution)/shard_map/attend_back/pallas_call | solution.py:32
  278.9 74.4 %stream_back.1 = (bf16[384,1152]{1,0:T(8,128)(2,1)}, f32[8,2304]{1,0:T(8,128)}, bf16[288,432]{1,0:T(8,128)(2,1)}, bf16[144,1152]{1,0:T(8,128)(2,1)}) custom-call(bf16[12,256,1152]{2,1,0:T(8,128)(2,1)} %get-tuple-element.99.h_ref, bf16[4,144,1152]{2,1,0:T(8,128)(2,1)} %get-tuple-element.100.gs_ref, bf16[12,256,768]{2,1,0:T(8,128)(2,1)} %attend_back.1.d_ref, ...), custom_call_target="tpu_custom_call" | custom-call | flops 10871635968 | bytes 21154816 | tf_op jit(solution)/shard_map/stream_back/pallas_call | solution.py:32
  353.3 122.7 %finish.1 = (bf16[2,9,144,1152]{3,2,1,0:T(8,128)(2,1)}, bf16[8,288,432]{2,1,0:T(8,128)(2,1)}, f32[4,8,6912]{2,1,0:T(8,128)}, f32[4,32,288]{2,1,0:T(8,128)}) custom-call(bf16[8,144,1152]{2,1,0:T(8,128)(2,1)} %bitcast.17, bf16[288,6912]{1,0:T(8,128)(2,1)} %ada_ref.3, bf16[144,1152]{1,0:T(8,128)(2,1)} %get-tuple-element.118.go_ref, ...), custom_call_target="tpu_custom_call" | custom-call | bytes 16468992 | tf_op jit(solution)/shard_map/finish/pallas_call | solution.py:32
  476.0 14.7 %unfold.1 = (f32[64,1152]{1,0:T(8,128)}, f32[288,6912]{1,0:T(8,128)}, f32[288,3456]{1,0:T(8,128)}, f32[288,1152]{1,0:T(8,128)}, f32[288,4608]{1,0:T(8,128)}, /*index=5*/f32[1152,1152]{1,0:T(8,128)}) custom-call(bf16[32,288]{1,0:T(8,128)(2,1)} %get-tuple-element.115.low_ref, f32[32,64]{1,0:T(8,128)} %get-tuple-element.116.wave_ref, ...), custom_call_target="tpu_custom_call" | custom-call | bytes 33204224 | tf_op jit(solution)/shard_map/unfold/pallas_call | solution.py:32
  490.7 0.9 copy.24
  (76 shorter events, 6.6 us)
Async XLA Ops:
  7.2 6.8 %copy-start = (s32[1,3072]{1,0:T(1,128)S(1)}, s32[1,3072]{1,0:T(1,128)}, u32[]{:S(2)}) copy-start(s32[1,3072]{1,0:T(1,128)} %param.15) | copy-start | bytes 36868
  7.2 166.5 %all-gather.2.cloned.1.call-start = ((), (), s32[]{:S(2)}) async-start(), calls=%async_computation.1 | async-start | bytes 13271040 | tf_op jit(solution)/shard_map/all_gather | solution.py:1205
  12.7 340.6 %reduce-scatter.2.cloned.1.call-start = ((), (), s32[]{:S(2)}) async-start(), calls=%async_computation.2 | async-start | bytes 13271040 | tf_op jit(solution)/shard_map/reduce_scatter | solution.py:1336
  15.2 102.4 %copy-start.15 = (s32[1,8,16]{2,1,0:T(8,128)S(1)}, s32[1,8,16]{2,1,0:T(8,128)}, u32[]{:S(2)}) copy-start(s32[1,8,16]{2,1,0:T(8,128)} %param.16) | copy-start | bytes 1540
  118.3 43.5 %copy-start.2 = (f32[16,6912]{1,0:T(8,128)S(1)}, f32[16,6912]{1,0:T(8,128)}, u32[]{:S(2)}) copy-start(f32[16,6912]{1,0:T(8,128)} %get-tuple-element.72.mod_ref) | copy-start | bytes 1327108
  118.3 43.5 %copy-start.7 = (bf16[384,1152]{1,0:T(8,128)(2,1)S(1)}, bf16[384,1152]{1,0:T(8,128)(2,1)}, u32[]{:S(2)}) copy-start(bf16[384,1152]{1,0:T(8,128)(2,1)} %get-tuple-element.73.x_ref) | copy-start | bytes 2654212
  139.7 31.7 %copy-start.19 = (s32[1,8,4608]{2,1,0:T(8,128)S(1)}, s32[1,8,4608]{2,1,0:T(8,128)}, u32[]{:S(2)}) copy-start(s32[1,8,4608]{2,1,0:T(8,128)} %param.17) | copy-start | bytes 442372
  139.7 6.5 %collective-permute-start = (bf16[144,384]{1,0:T(8,128)(2,1)S(1)}, bf16[144,384]{1,0:T(8,128)(2,1)S(1)}, u32[]{:S(2)}, u32[]{:S(2)}) collective-permute-start(bf16[144,384]{1,0:T(8,128)(2,1)S(1)} %get-tuple-element.77), channel_id=1, source_target_pairs={{0,1},{1,0},{2,3},{3,2},{4,5},{5,4},{6,7},{7,6},{8,9},{9,8},{10,11... | collective-permute-start | bytes 331784 | tf_op jit(solution)/shard_map/ppermute | solution.py:51
  141.8 6.9 %collective-permute-start.1 = (bf16[144,384]{1,0:T(8,128)(2,1)S(1)}, bf16[144,384]{1,0:T(8,128)(2,1)S(1)}, u32[]{:S(2)}, u32[]{:S(2)}) collective-permute-start(bf16[144,384]{1,0:T(8,128)(2,1)S(1)} %get-tuple-element.78), channel_id=1, source_target_pairs={{0,2},{1,3},{2,0},{3,1},{4,6},{5,7},{6,4},{7,5},{8,10},{9,11},{10,... | collective-permute-start | bytes 331784 | tf_op jit(solution)/shard_map/ppermute | solution.py:51
  143.3 10.0 %collective-permute-start.2 = (bf16[144,384]{1,0:T(8,128)(2,1)S(1)}, bf16[144,384]{1,0:T(8,128)(2,1)S(1)}, u32[]{:S(2)}, u32[]{:S(2)}) collective-permute-start(bf16[144,384]{1,0:T(8,128)(2,1)S(1)} %get-tuple-element.79), channel_id=1, source_target_pairs={{0,3},{1,2},{2,1},{3,0},{4,7},{5,6},{6,5},{7,4},{8,11},{9,10},{10,... | collective-permute-start | bytes 331784 | tf_op jit(solution)/shard_map/ppermute | solution.py:51
  143.4 9.8 %collective-permute-start.3 = (bf16[144,384]{1,0:T(8,128)(2,1)S(1)}, bf16[144,384]{1,0:T(8,128)(2,1)S(1)}, u32[]{:S(2)}, u32[]{:S(2)}) collective-permute-start(bf16[144,384]{1,0:T(8,128)(2,1)S(1)} %get-tuple-element.80), channel_id=1, source_target_pairs={{0,4},{1,5},{2,6},{3,7},{4,0},{5,1},{6,2},{7,3},{8,12},{9,13},{10,... | collective-permute-start | bytes 331784 | tf_op jit(solution)/shard_map/ppermute | solution.py:51
  146.1 15.7 %collective-permute-start.4 = (bf16[144,384]{1,0:T(8,128)(2,1)S(1)}, bf16[144,384]{1,0:T(8,128)(2,1)S(1)}, u32[]{:S(2)}, u32[]{:S(2)}) collective-permute-start(bf16[144,384]{1,0:T(8,128)(2,1)S(1)} %get-tuple-element.81), channel_id=1, source_target_pairs={{0,5},{1,4},{2,7},{3,6},{4,1},{5,0},{6,3},{7,2},{8,13},{9,12},{10,... | collective-permute-start | bytes 331784 | tf_op jit(solution)/shard_map/ppermute | solution.py:51
  146.2 15.6 %collective-permute-start.5 = (bf16[144,384]{1,0:T(8,128)(2,1)S(1)}, bf16[144,384]{1,0:T(8,128)(2,1)S(1)}, u32[]{:S(2)}, u32[]{:S(2)}) collective-permute-start(bf16[144,384]{1,0:T(8,128)(2,1)S(1)} %get-tuple-element.82), channel_id=1, source_target_pairs={{0,6},{1,7},{2,4},{3,5},{4,2},{5,3},{6,0},{7,1},{8,14},{9,15},{10,... | collective-permute-start | bytes 331784 | tf_op jit(solution)/shard_map/ppermute | solution.py:51
  148.7 13.2 %collective-permute-start.6 = (bf16[144,384]{1,0:T(8,128)(2,1)S(1)}, bf16[144,384]{1,0:T(8,128)(2,1)S(1)}, u32[]{:S(2)}, u32[]{:S(2)}) collective-permute-start(bf16[144,384]{1,0:T(8,128)(2,1)S(1)} %get-tuple-element.83), channel_id=1, source_target_pairs={{0,7},{1,6},{2,5},{3,4},{4,3},{5,2},{6,1},{7,0},{8,15},{9,14},{10,... | collective-permute-start | bytes 331784 | tf_op jit(solution)/shard_map/ppermute | solution.py:51
  171.1 2.6 collective-permute-start.7
  212.0 3.6 copy-start.3
  212.0 3.6 copy-start.12
  213.1 2.4 collective-permute-start.9
  213.5 19.8 %collective-permute-start.8 = (bf16[384,1152]{1,0:T(8,128)(2,1)}, bf16[384,1152]{1,0:T(8,128)(2,1)S(1)}, u32[]{:S(2)}, u32[]{:S(2)}) collective-permute-start(bf16[384,1152]{1,0:T(8,128)(2,1)} %get-tuple-element.90), channel_id=1, source_target_pairs={{0,1},{1,0},{2,3},{3,2},{4,5},{5,4},{6,7},{7,6},{8,9},{9,8},{10,11... | collective-permute-start | bytes 2654216 | tf_op jit(solution)/shard_map/ppermute | solution.py:51
  215.6 21.7 %copy-start.8 = (bf16[384,384]{1,0:T(8,128)(2,1)S(1)}, bf16[384,384]{1,0:T(8,128)(2,1)}, u32[]{:S(2)}) copy-start(bf16[384,384]{1,0:T(8,128)(2,1)} %get-tuple-element.97.perm_ref) | copy-start | bytes 884740
  225.6 19.2 %copy-start.9 = (f32[8,2304]{1,0:T(8,128)}, f32[8,2304]{1,0:T(8,128)S(1)}, u32[]{:S(2)}) copy-start(f32[8,2304]{1,0:T(8,128)S(1)} %get-tuple-element.121.two_ref) | copy-start | bytes 221188
  225.6 8.3 %collective-permute-start.10 = (bf16[144,384]{1,0:T(8,128)(2,1)S(1)}, bf16[144,384]{1,0:T(8,128)(2,1)S(1)}, u32[]{:S(2)}, u32[]{:S(2)}) collective-permute-start(bf16[144,384]{1,0:T(8,128)(2,1)S(1)} %get-tuple-element.104), channel_id=1, source_target_pairs={{0,1},{1,0},{2,3},{3,2},{4,5},{5,4},{6,7},{7,6},{8,9},{9,8},{10,11... | collective-permute-start | bytes 331784 | tf_op jit(solution)/shard_map/ppermute | solution.py:51
  225.9 9.7 %collective-permute-start.11 = (bf16[144,384]{1,0:T(8,128)(2,1)S(1)}, bf16[144,384]{1,0:T(8,128)(2,1)S(1)}, u32[]{:S(2)}, u32[]{:S(2)}) collective-permute-start(bf16[144,384]{1,0:T(8,128)(2,1)S(1)} %get-tuple-element.105), channel_id=1, source_target_pairs={{0,2},{1,3},{2,0},{3,1},{4,6},{5,7},{6,4},{7,5},{8,10},{9,11},{10,... | collective-permute-start | bytes 331784 | tf_op jit(solution)/shard_map/ppermute | solution.py:51
  230.9 14.9 %collective-permute-start.12 = (bf16[144,384]{1,0:T(8,128)(2,1)S(1)}, bf16[144,384]{1,0:T(8,128)(2,1)S(1)}, u32[]{:S(2)}, u32[]{:S(2)}) collective-permute-start(bf16[144,384]{1,0:T(8,128)(2,1)S(1)} %get-tuple-element.106), channel_id=1, source_target_pairs={{0,3},{1,2},{2,1},{3,0},{4,7},{5,6},{6,5},{7,4},{8,11},{9,10},{10,... | collective-permute-start | bytes 331784 | tf_op jit(solution)/shard_map/ppermute | solution.py:51
  231.0 14.8 %collective-permute-start.13 = (bf16[144,384]{1,0:T(8,128)(2,1)S(1)}, bf16[144,384]{1,0:T(8,128)(2,1)S(1)}, u32[]{:S(2)}, u32[]{:S(2)}) collective-permute-start(bf16[144,384]{1,0:T(8,128)(2,1)S(1)} %get-tuple-element.107), channel_id=1, source_target_pairs={{0,4},{1,5},{2,6},{3,7},{4,0},{5,1},{6,2},{7,3},{8,12},{9,13},{10,... | collective-permute-start | bytes 331784 | tf_op jit(solution)/shard_map/ppermute | solution.py:51
  233.2 15.7 %collective-permute-start.14 = (bf16[144,384]{1,0:T(8,128)(2,1)S(1)}, bf16[144,384]{1,0:T(8,128)(2,1)S(1)}, u32[]{:S(2)}, u32[]{:S(2)}) collective-permute-start(bf16[144,384]{1,0:T(8,128)(2,1)S(1)} %get-tuple-element.108), channel_id=1, source_target_pairs={{0,5},{1,4},{2,7},{3,6},{4,1},{5,0},{6,3},{7,2},{8,13},{9,12},{10,... | collective-permute-start | bytes 331784 | tf_op jit(solution)/shard_map/ppermute | solution.py:51
  233.9 15.0 %collective-permute-start.15 = (bf16[144,384]{1,0:T(8,128)(2,1)S(1)}, bf16[144,384]{1,0:T(8,128)(2,1)S(1)}, u32[]{:S(2)}, u32[]{:S(2)}) collective-permute-start(bf16[144,384]{1,0:T(8,128)(2,1)S(1)} %get-tuple-element.109), channel_id=1, source_target_pairs={{0,6},{1,7},{2,4},{3,5},{4,2},{5,3},{6,0},{7,1},{8,14},{9,15},{10,... | collective-permute-start | bytes 331784 | tf_op jit(solution)/shard_map/ppermute | solution.py:51
  235.6 13.3 %collective-permute-start.16 = (bf16[144,384]{1,0:T(8,128)(2,1)S(1)}, bf16[144,384]{1,0:T(8,128)(2,1)S(1)}, u32[]{:S(2)}, u32[]{:S(2)}) collective-permute-start(bf16[144,384]{1,0:T(8,128)(2,1)S(1)} %get-tuple-element.110), channel_id=1, source_target_pairs={{0,7},{1,6},{2,5},{3,4},{4,3},{5,2},{6,1},{7,0},{8,15},{9,14},{10,... | collective-permute-start | bytes 331784 | tf_op jit(solution)/shard_map/ppermute | solution.py:51
  237.2 11.7 %copy-start.17 = (bf16[12,144,256]{2,1,0:T(8,128)(2,1)S(1)}, bf16[12,144,256]{2,1,0:T(8,128)(2,1)}, u32[]{:S(2)}) copy-start(bf16[12,144,256]{2,1,0:T(8,128)(2,1)} %copy-done.16) | copy-start | bytes 2654212
  245.8 33.0 %copy-start.10 = (f32[8,2304]{1,0:T(8,128)}, f32[8,2304]{1,0:T(8,128)S(1)}, u32[]{:S(2)}) copy-start(f32[8,2304]{1,0:T(8,128)S(1)} %get-tuple-element.122.gate_ref) | copy-start | bytes 221188
  476.0 14.7 %copy-start.18 = (bf16[384,1152]{1,0:T(8,128)(2,1)S(1)}, bf16[384,1152]{1,0:T(8,128)(2,1)}, u32[]{:S(2)}) copy-start(bf16[384,1152]{1,0:T(8,128)(2,1)} %get-tuple-element.145) | copy-start | bytes 2654212
  476.0 15.6 %copy-start.1 = (s32[1,3072]{1,0:T(1,128)S(1)}, s32[1,3072]{1,0:T(1,128)}, u32[]{:S(2)}) copy-start(s32[1,3072]{1,0:T(1,128)} %param.15) | copy-start | bytes 36868
  (10 other events, 13.1 us)
Sparse Core Ops, SparseCore 0:
  12.8 139.5 all-gather.1
  212.1 123.3 reduce-scatter.1
